TPU v7x, 512 devices: a whole 4x4x16 slice. The times are simulated.
512 devices in a mesh: ctx: 32 (over z, core), exp: 16 (over x, y).
Axes of the slice: x: 4, y: 4, z: 16, core: 2. Of those that a mesh axis runs over, the one named last changes fastest.
Arguments:
- seq_x: bfloat16 [4096, 5120], P('ctx', 'exp'), may hold values from -6 to 6
- z_gate: bfloat16 [4096, 5120], P('ctx', 'exp'), may hold values from -6 to 6
- bc_in: bfloat16 [4096, 256], P('ctx'), may hold values from -6 to 6
- conv_x: float32 [4, 5120], P(None, 'exp'), may hold values from -3 to 3
- conv_bc: float32 [4, 256], replicated, may hold values from -3 to 3
- log_decay: float32 [4096, 80], P('ctx', 'exp'), may hold values from -1 to 0
- skip_d: float32 [80], P('exp'), may hold values from 0.5 to 2
- norm_gain: float32 [5120], P('exp'), may hold values from 0.25 to 1.75
- routes: int32 [4096, 2], P('ctx'), may hold values from 0 to 31, all different within a row; in each aligned block of 128 rows (0 to 127, 128 to 255, ...) at most 12 rows name the same one
- route_gates: float32 [4096, 2], P('ctx'), may hold values from 0.2 to 1
- placement: int32 [32], replicated, may hold values from 0 to 31, each once
- gate_w: bfloat16 [32, 5120, 2048], P('ctx', None, 'exp'), may hold values from -0.078125 to 0.078125
- up_w: bfloat16 [32, 5120, 2048], P('ctx', None, 'exp'), may hold values from -0.078125 to 0.078125
- down_w: bfloat16 [32, 2048, 5120], P('ctx', 'exp'), may hold values from -0.125 to 0.125
Outputs:
- normed: bfloat16 [4096, 5120], P('ctx', 'exp')
- mixed: bfloat16 [4096, 5120], P('ctx', 'exp')
Inputs may be any that keep to these rules, and one draw needn't show every extreme that they name: `routes`: in every aligned block of 128 tokens no expert is named by more than 12 choices, a bound that some block reaches; a token's two experts differ. `placement`: each slot holds exactly one expert.
All inputs are finite; a program needn't handle non-finite values.
Results may differ from a plain program's by a relative error of at most 0.023.
Values may be sent and summed in bfloat16 or wider, within the bound.
No kernel may reach another device: no remote copies, remote signals or barrier semaphores. Data moves between devices by JAX's collectives and lax.ppermute only.
A program may use at most 128 MiB of HBM per device.

v0:
```python
import jax
import jax.numpy as jnp
from jax import lax
from jax.sharding import PartitionSpec as P

HEAD_DIM = 64
STATE = 128
CONV = 4
SPAN = 128


def shifted(value, axis, steps):
    count = lax.axis_size(axis)
    initial, last = (max(0, -steps), min(count, count - steps))
    return lax.ppermute(value, axis, [(source, source + steps) for source in range(initial, last)])


def carried_in(array, axis, join, neutral):
    place = lax.axis_index(axis)
    gathered = jax.tree.map(
        lambda a, kind: lax.all_gather(a.astype(kind), axis), array, (jnp.bfloat16, jnp.bfloat16)
    )
    state = jax.tree.map(lambda a, e: jnp.zeros_like(a) + jnp.asarray(e, a.dtype), array, neutral)

    def one(step, state):
        return join(
            state,
            jax.tree.map(
                lambda a, own: lax.dynamic_index_in_dim(a, step, 0, False).astype(own.dtype),
                gathered,
                array,
            ),
        )

    return lax.fori_loop(0, place, one, state)


def chain_combine(earlier, later):
    return (earlier[0] + later[0], jnp.exp(later[0])[:, None, None] * earlier[1] + later[1])


def expert_part(gates, ups, down_rows):
    hidden = (jax.nn.silu(gates) * ups).astype(jnp.bfloat16)
    return jnp.einsum("eif,fd->eid", hidden, down_rows, preferred_element_type=jnp.float32).astype(
        jnp.bfloat16
    )


def body(
    seq_x,
    z_gate,
    bc_in,
    conv_x,
    conv_bc,
    log_decay,
    skip_d,
    norm_gain,
    routes,
    route_gates,
    placement,
    gate_w,
    up_w,
    down_w,
):
    highest = lax.Precision.HIGHEST
    tokens = seq_x.shape[0]
    local_width = seq_x.shape[1]
    local_heads = local_width // HEAD_DIM
    rim_x, rim_bc = shifted((seq_x[tokens - CONV + 1 :], bc_in[tokens - CONV + 1 :]), "ctx", 1)
    long_x = jnp.concatenate([rim_x, seq_x], axis=0).astype(jnp.float32)
    long_bc = jnp.concatenate([rim_bc, bc_in], axis=0).astype(jnp.float32)
    conv_xs = jnp.zeros((tokens, local_width), jnp.float32)
    conv_bcs = jnp.zeros((tokens, bc_in.shape[1]), jnp.float32)
    for offset in range(CONV):
        conv_xs = conv_xs + conv_x[offset][None, :] * long_x[offset : offset + tokens]
        conv_bcs = conv_bcs + conv_bc[offset][None, :] * long_bc[offset : offset + tokens]
    conv_xs = jax.nn.silu(conv_xs)
    conv_bcs = jax.nn.silu(conv_bcs)
    blocks = tokens // SPAN
    head_x = conv_xs.reshape(blocks, SPAN, local_heads, HEAD_DIM)
    in_keys = conv_bcs[:, :STATE].reshape(blocks, SPAN, STATE)
    out_keys = conv_bcs[:, STATE:].reshape(blocks, SPAN, STATE)
    running = jnp.cumsum(log_decay.reshape(blocks, SPAN, local_heads), axis=1)
    places = jnp.arange(SPAN)
    lower = (places[:, None] >= places[None, :])[None, :, :, None]
    log_gaps = running[:, :, None, :] - running[:, None, :, :]
    weights = jnp.where(lower, jnp.exp(jnp.where(lower, log_gaps, 0.0)), 0.0)
    scores = jnp.einsum("cin,cjn->cij", out_keys, in_keys, precision=highest)
    inner = jnp.einsum("cij,cijh,cjhp->cihp", scores, weights, head_x, precision=highest)
    tails = jnp.exp(running[:, -1:, :] - running)
    block_states = jnp.einsum("cjh,cjhp,cjn->chpn", tails, head_x, in_keys, precision=highest)
    block_logs = running[:, -1, :]

    def walk(carry, item):
        state, log_total = carry
        new_state = jnp.exp(item[1])[:, None, None] * state + item[0]
        return ((new_state, log_total + item[1]), (state, log_total))

    start = (
        jnp.zeros((local_heads, HEAD_DIM, STATE), jnp.float32),
        jnp.zeros((local_heads,), jnp.float32),
    )
    (own_state, own_log), (enter_states, enter_logs) = lax.scan(
        walk, start, (block_states, block_logs)
    )
    identity = (
        jnp.zeros((local_heads,), jnp.float32),
        jnp.zeros((local_heads, HEAD_DIM, STATE), jnp.float32),
    )
    _, carried = carried_in((own_log, own_state), "ctx", chain_combine, identity)
    entering = enter_states + jnp.exp(enter_logs)[:, :, None, None] * carried[None]
    outer = (
        jnp.einsum("cin,chpn->cihp", out_keys, entering, precision=highest)
        * jnp.exp(running)[..., None]
    )
    outputs = inner + outer + skip_d[None, None, :, None] * head_x
    outputs = outputs.reshape(tokens, local_heads, HEAD_DIM)
    gated = outputs * jax.nn.silu(z_gate.astype(jnp.float32).reshape(tokens, local_heads, HEAD_DIM))
    expert_scales = lax.rsqrt(jnp.mean(gated * gated, axis=-1, keepdims=True) + 1e-05)
    normed = (
        (gated * expert_scales * norm_gain.reshape(local_heads, HEAD_DIM))
        .reshape(tokens, local_width)
        .astype(jnp.bfloat16)
    )
    experts = placement.shape[0]
    capacity = max(2, 3 * tokens // experts)
    flat_routes = routes.reshape(tokens * 2)
    onehot = (flat_routes[:, None] == jnp.arange(experts, dtype=jnp.int32)[None, :]).astype(
        jnp.int32
    )
    ranks = jnp.sum(jnp.cumsum(onehot, axis=0) * onehot, axis=1) - 1
    owners = jnp.sum(onehot * placement[None, :], axis=1)
    positions = owners * capacity + ranks
    holders = jnp.arange(tokens * 2, dtype=jnp.int32) // 2
    slot_token = jnp.full((experts * capacity,), tokens, jnp.int32).at[positions].set(holders)
    gate_rows = gate_w[0]
    up_rows = up_w[0]
    down_rows = down_w[0]
    full = lax.all_gather(normed, "exp", axis=1, tiled=True)
    padded = jnp.concatenate([full, jnp.zeros((1, full.shape[1]), jnp.bfloat16)], axis=0)
    outgoing = padded[slot_token].reshape(experts, capacity, full.shape[1])
    arrived = lax.all_to_all(outgoing, "ctx", split_axis=0, concat_axis=0, tiled=True)
    gates = jnp.einsum("eid,df->eif", arrived, gate_rows, preferred_element_type=jnp.float32)
    ups = jnp.einsum("eid,df->eif", arrived, up_rows, preferred_element_type=jnp.float32)
    parts = expert_part(gates, ups, down_rows)
    gate_weights = route_gates.reshape(tokens, 2, 1)
    returned = lax.all_to_all(parts, "ctx", split_axis=0, concat_axis=0, tiled=True)
    picked = returned.reshape(experts * capacity, parts.shape[2])[positions]
    weighted = jnp.sum(
        picked.reshape(tokens, 2, parts.shape[2]).astype(jnp.float32) * gate_weights, axis=1
    )
    mixed = lax.psum_scatter(weighted.astype(jnp.bfloat16), "exp", scatter_dimension=1, tiled=True)
    return (normed, mixed)


def solution(mesh):
    placed = (
        P("ctx", "exp"),
        P("ctx", "exp"),
        P("ctx", None),
        P(None, "exp"),
        P(),
        P("ctx", "exp"),
        P("exp"),
        P("exp"),
        P("ctx", None),
        P("ctx", None),
        P(),
        P("ctx", None, "exp"),
        P("ctx", None, "exp"),
        P("ctx", "exp", None),
    )
    return jax.shard_map(
        body,
        mesh=mesh,
        in_specs=placed,
        out_specs=(P("ctx", "exp"), P("ctx", "exp")),
        check_vma=False,
    )
```

profile of v0, /device:TPU:1, one launch (start us, length us, event | category | flops | bytes accessed | tf_op | source)
XLA Modules:
  0.0 826.5 jit_solution(370255345154275503)
XLA Ops:
  7.3 1.1 slice.82
  8.3 4.9 collective-permute-start.1
  14.0 1.9 collective-permute-start
  16.9 0.8 fusion.67
  17.9 0.9 slice_reduce_fusion.4
  19.1 0.9 maximum_convert_fusion.1
  20.1 1.0 maximum_convert_fusion
  21.5 0.9 fusion.24
  22.5 34.1 %all-gather = bf16[32,1,5]{2,1,0:T(2,128)(2,1)S(1)} all-gather(bf16[1,1,5]{2,1,0:T(2,128)(2,1)S(1)} %slice.178), channel_id=2, replica_groups=mesh['ctx'=32,'exp'=16] {'ctx'}, dimensions={0}, use_global_device_ids=true | all-gather | bytes 330 | tf_op jit(solution)/shard_map/all_gather | solution.py:21
  56.9 42.0 %all-gather.7.cloned.1.call-done = bf16[160,64,128]{2,1,0:T(8,128)(2,1)} async-done(((bf16[5,64,128]{2,1,0:T(8,128)(2,1)}), bf16[160,64,128]{2,1,0:T(8,128)(2,1)}) %all-gather.7.cloned.1.call-update) | async-done | bytes 2621456 | tf_op jit(solution)/shard_map/all_gather | solution.py:21
  98.9 1.0 while.3
  98.9 1.0 convert_add_fusion.2
  100.3 0.8 fusion.41
  103.3 1.4 scatter_custom_fusion
  104.7 78.4 %all-gather.5.cloned.1.call-done = bf16[128,5120]{0,1:T(8,128)(2,1)} async-done(((bf16[128,320]{0,1:T(8,128)(2,1)}), bf16[128,5120]{0,1:T(8,128)(2,1)}) %all-gather.5.cloned.1.call-update) | async-done | bytes 1310736 | tf_op jit(solution)/shard_map/all_gather | solution.py:139
  183.1 2.5 copy.89
  185.6 1.4 concatenate.11
  187.0 4.8 gather_fusion
  191.8 7.0 reshape.232
  198.8 249.5 %all_to_all.10 = bf16[32,12,5120]{2,1,0:T(8,128)(2,1)S(1)} all-to-all(bf16[32,12,5120]{2,1,0:T(8,128)(2,1)} %reshape.232), channel_id=1, replica_groups=mesh['ctx'=32,'exp'=16] {'ctx'}, dimensions={0} | all-to-all | bytes 7864320 | tf_op jit(solution)/shard_map/all_to_all | solution.py:142
  448.2 2.3 copy-done.1
  450.6 2.6 fusion.2
  453.2 8.7 %convolution_convert_fusion = bf16[32,12,5120]{2,0,1:T(8,128)(2,1)} fusion(bf16[1,128,5120]{2,1,0:T(8,128)(2,1)S(1)} %copy-done, bf16[1,5120,128]{2,1,0:T(8,128)(2,1)S(1)} %copy-done.2, bf16[32,12,5120]{2,1,0:T(8,128)(2,1)} %copy-done.1, f32[32,12,128]{2,0,1:T(8,128)S(1)} %fusion.2), kind=kOutput, calls=%fused_computation.5 | convolution fusion | flops 1008893952 | bytes 10682368 | tf_op jit(solution)/shard_map/eif,fd->eid/dot_general | solution.py:44
  461.9 6.7 copy.95
  468.6 5.1 all-to-all-start.1
  474.1 231.2 %all-to-all-done.1 = bf16[32,12,5120]{2,1,0:T(8,128)(2,1)} async-done(((bf16[32,12,5120]{2,1,0:T(8,128)(2,1)}), bf16[32,12,5120]{2,1,0:T(8,128)(2,1)}, u32[]{:S(2)}, u32[]{:S(2)}) %all-to-all-start.1) | async-done | bytes 3932192 | tf_op jit(solution)/shard_map/all_to_all | solution.py:147
  705.3 7.1 reshape.233
  712.4 8.8 %gather_fusion.1 = bf16[256,5120]{1,0:T(8,128)(2,1)} fusion(bf16[384,5120]{1,0:T(8,128)(2,1)} %reshape.233, s32[1024]{0:T(1024)S(1)} %pad_clamp_fusion), kind=kCustom, calls=%fused_computation.1 | custom fusion | bytes 5243904 | tf_op jit(solution)/shard_map/gather | solution.py:148
  721.2 6.6 reshape.235
  727.9 10.0 %multiply_reduce_fusion = bf16[128,5120]{1,0:T(8,128)(2,1)S(1)} fusion(f32[128,2,5120]{2,1,0:T(2,128)} %reshape.235, f32[128,2]{1,0:T(8,128)S(1)} %copy.96), kind=kLoop, calls=%fused_computation.6 | loop fusion | flops 1966080 | bytes 6554624 | tf_op jit(solution)/shard_map/reduce_sum | solution.py:149
  737.8 1.5 copy.99
  739.3 80.6 %reduce-scatter.4.cloned.1.call-done = bf16[320,128]{1,0:T(8,128)(2,1)} async-done(((bf16[5120,128]{1,0:T(8,128)(2,1)}), bf16[320,128]{1,0:T(8,128)(2,1)}) %reduce-scatter.4.cloned.1.call-update) | async-done | bytes 81936
  (61 shorter events, 5.9 us)
Async XLA Ops:
  7.2 446.1 %copy-start = (bf16[1,128,5120]{2,1,0:T(8,128)(2,1)S(1)}, bf16[1,128,5120]{2,1,0:T(8,128)(2,1)}, u32[]{:S(2)}) copy-start(bf16[1,128,5120]{2,1,0:T(8,128)(2,1)} %param.29) | copy-start | bytes 3932164
  7.2 93.1 %copy-start.3 = (bf16[128,320]{0,1:T(8,128)(2,1)S(1)}, bf16[128,320]{0,1:T(8,128)(2,1)}, u32[]{:S(2)}) copy-start(bf16[128,320]{0,1:T(8,128)(2,1)} %param.17) | copy-start | bytes 245764
  7.2 93.1 %copy-start.9 = (f32[5]{0:T(128)S(1)}, f32[5]{0:T(128)}, u32[]{:S(2)}) copy-start(f32[5]{0:T(128)} %param.22) | copy-start | bytes 64
  7.2 93.9 %copy-start.4 = (f32[320]{0:T(512)S(1)}, f32[320]{0:T(512)}, u32[]{:S(2)}) copy-start(f32[320]{0:T(512)} %param.23) | copy-start | bytes 3844
  7.2 91.7 %all-gather.7.cloned.1.call-start = ((), (), s32[]{:S(2)}) async-start(), calls=%async_computation.4 | async-start | bytes 2703360 | tf_op jit(solution)/shard_map/all_gather | solution.py:21
  8.3 11.8 %collective-permute-start.1 = (bf16[3,320]{0,1:T(8,128)(2,1)S(1)}, bf16[3,320]{0,1:T(8,128)(2,1)S(1)}, u32[]{:S(2)}, u32[]{:S(2)}) collective-permute-start(bf16[3,320]{0,1:T(8,128)(2,1)S(1)} %slice.82), channel_id=1, source_target_pairs={{0,16},{16,32},{32,48},{48,64},{64,80},{80,96},{96,112},{112,128},... | collective-permute-start | bytes 5768 | tf_op jit(solution)/shard_map/ppermute | solution.py:15
  14.0 5.2 collective-permute-start
  16.9 85.1 %copy-start.5 = (s32[128,2]{0,1:T(2,128)S(1)}, s32[128,2]{0,1:T(2,128)}, u32[]{:S(2)}) copy-start(s32[128,2]{0,1:T(2,128)} %param.24) | copy-start | bytes 3076
  20.0 83.2 %copy-start.7 = (s32[32]{0:T(128)S(1)}, s32[32]{0:T(128)}, u32[]{:S(2)}) copy-start(s32[32]{0:T(128)} %param.26) | copy-start | bytes 388
  22.4 160.7 %all-gather.5.cloned.1.call-start = ((), (), s32[]{:S(2)}) async-start(), calls=%async_computation.3 | async-start | bytes 1392640 | tf_op jit(solution)/shard_map/all_gather | solution.py:139
  198.8 251.8 %copy-start.8 = (bf16[1,5120,128]{2,1,0:T(8,128)(2,1)S(1)}, bf16[1,5120,128]{2,1,0:T(8,128)(2,1)}, u32[]{:S(2)}) copy-start(bf16[1,5120,128]{2,1,0:T(8,128)(2,1)} %param.27) | copy-start | bytes 3932164
  448.2 2.3 copy-start.1
  450.6 2.6 copy-start.2
  468.6 5.4 copy-start.6
  468.6 236.7 %all-to-all-start.1 = ((bf16[32,12,5120]{2,1,0:T(8,128)(2,1)}), bf16[32,12,5120]{2,1,0:T(8,128)(2,1)}, u32[]{:S(2)}, u32[]{:S(2)}) async-start(bf16[32,12,5120]{2,1,0:T(8,128)(2,1)} %copy.95), calls=%async_computation.1 | async-start | bytes 10485760 | tf_op jit(solution)/shard_map/all_to_all | solution.py:147
  473.7 346.2 %reduce-scatter.4.cloned.1.call-start = ((), (), s32[]{:S(2)}) async-start(), calls=%async_computation.5 | async-start | bytes 1392640
Sparse Core Ops, SparseCore 0:
  22.6 76.2 all-gather.6
  102.5 80.5 all-gather.4
  739.4 80.4 reduce-scatter.3
where the time goes:
time: 829 us; the launch traced here: 826 us
  waiting for transfers between devices  433 us (52%)
  blocking collectives  284 us (34%)
  local copies, waits for them, and re-layouts  55.1 us (7%)
  other arithmetic  15.1 us (2%)
  between operations  14.1 us (2%)
  matrix products  13.6 us (2%)
  starting transfers between devices  12.3 us (1%)
    all_to_all x1, blocking collectives, body(): lax.all_to_all(outgoing, 'ctx', split_axis=0, concat_axis=0, tiled=True)  249 us
    all_to_all x1, waiting for transfers between devices, body(): lax.all_to_all(parts, 'ctx', split_axis=0, concat_axis=0, tiled=True)  231 us
    unnamed x4, waiting for transfers between devices  80.7 us
    all_gather x1, waiting for transfers between devices, body(): full = lax.all_gather(normed, 'exp', axis=1, tiled=True)  78.4 us
    all_gather x1, waiting for transfers between devices, carried_in(): lax.all_gather(a.astype(kind), axis)  42 us
    all_gather x1, blocking collectives, carried_in(): lax.all_gather(a.astype(kind), axis)  34.1 us
  transfers between devices with their start and end apart: 6, of which 5 were waited for; matrix products, arithmetic and copies ran while one was open for 1% of the time, Pallas kernels for 0%

commit v1 on v0

v1 whole, which is shorter than its diff:
```python
import jax
import jax.numpy as jnp
from jax import lax
from jax.experimental import pallas as pl
from jax.experimental.pallas import tpu as pltpu
from jax.sharding import Mesh
from jax.sharding import PartitionSpec as P

HEAD_DIM = 64
STATE = 128
CONV = 4
CTX = ("zh", "zl", "c")
EXP = ("x", "y")
NEAR = ("zl", "c")
LANES = 128
HALF = 6
GROUPS = 5
PIECE = 32

BF = jnp.bfloat16
F32 = jnp.float32


def dot(a, b):
    return jnp.dot(a, b, preferred_element_type=F32)


def kernel_call(kernel, out_shape, count, scalars=1):
    specs = [pl.BlockSpec(memory_space=pltpu.SMEM)] * scalars
    specs += [pl.BlockSpec(memory_space=pltpu.VMEM)] * (count - scalars)
    return pl.pallas_call(
        kernel,
        out_shape=out_shape,
        in_specs=specs,
        out_specs=pl.BlockSpec(memory_space=pltpu.VMEM),
        compiler_params=pltpu.CompilerParams(vmem_limit_bytes=48 << 20),
    )


def gate_up_kernel(ix_ref, g_ref, w0_ref, w1_ref, w2_ref, w3_ref, out_ref):
    rows = 2 * 192
    wide = [jnp.concatenate([g_ref[y, :rows], g_ref[y, rows : 2 * rows]], axis=1) for y in range(4)]
    slim = []
    for y in range(4):
        packed = g_ref[y, 2 * rows :]
        slim.append(jnp.concatenate([packed[:, :64], packed[:, 64:]], axis=0))
    pairs = [jnp.concatenate([slim[0], slim[1]], axis=1), jnp.concatenate([slim[2], slim[3]], axis=1)]
    for s, w_ref in enumerate((w0_ref, w1_ref, w2_ref, w3_ref)):
        target = lax.rem(ix_ref[0] - s + 4, 4)

        def weight(start, size):
            return jnp.concatenate(
                [w_ref[start : start + size], w_ref[1280 + start : 1280 + start + size]], axis=1
            )

        total = dot(wide[0], weight(0, 256))
        for y in range(1, 4):
            total += dot(wide[y], weight(y * 320, 256))
        for p in range(2):
            low, high = weight(p * 640 + 256, 64), weight(p * 640 + 576, 64)
            total += dot(pairs[p], jnp.concatenate([low, high], axis=0))
        out_ref[target, :rows] = total[:, :LANES].astype(BF)
        out_ref[target, rows:] = total[:, LANES:].astype(BF)


def hidden_kernel(p_ref, out_ref):
    rows = p_ref.shape[1] // 2
    total = p_ref[0].astype(F32)
    for i in range(1, 4):
        total += p_ref[i].astype(F32)
    gate, up = total[:rows], total[rows:]
    out_ref[...] = (gate * jax.nn.sigmoid(gate) * up).astype(BF)


def down_kernel(ix_ref, h_ref, w0_ref, w1_ref, w2_ref, w3_ref, out_ref):
    rows = h_ref.shape[1]
    half = rows // 2
    hid = jnp.concatenate([h_ref[lax.rem(ix_ref[0] - s + 4, 4)] for s in range(4)], axis=1)
    blocks = []
    for b in range(5):
        weight = []
        for w_ref in (w0_ref, w1_ref, w2_ref, w3_ref):
            start = 2560 + b * 256
            weight.append(
                jnp.concatenate([w_ref[start : start + 128], w_ref[start + 128 : start + 256]], axis=1)
            )
        blocks.append(dot(hid, jnp.concatenate(weight, axis=0)))
    full = jnp.concatenate(blocks, axis=1)
    for y in range(4):
        own = full[:, y * 320 : (y + 1) * 320]
        out_ref[y, :rows] = own[:, :128].astype(BF)
        out_ref[y, rows : 2 * rows] = own[:, 128:256].astype(BF)
        last = own[:, 256:]
        out_ref[y, 2 * rows :] = jnp.concatenate([last[:half], last[half:]], axis=1).astype(BF)


def split_log(value):
    high = value.astype(BF)
    low = (value - high.astype(F32)).astype(BF)
    return high, low


def pack_state(state, logs):
    heads = logs.shape[0]
    tail = jnp.zeros((16, STATE), BF)
    high, low = split_log(logs)
    tail = tail.at[0, :heads].set(high).at[1, :heads].set(low)
    return jnp.concatenate([state.reshape(heads * HEAD_DIM, STATE).astype(BF), tail], axis=0)


def unpack_state(message, heads):
    rows = heads * HEAD_DIM
    states = message[:, :rows].astype(F32).reshape(-1, heads, HEAD_DIM, STATE)
    logs = message[:, rows, :heads].astype(F32) + message[:, rows + 1, :heads].astype(F32)
    return states, logs


def prefix(states, logs, end):
    count = logs.shape[0]
    places = jnp.arange(count)
    inside = (places[None, :] > places[:, None]) & (places[None, :] < end)
    gaps = jnp.sum(jnp.where(inside[:, :, None], logs[None], 0.0), axis=1)
    weights = jnp.where((places < end)[:, None], jnp.exp(gaps), 0.0)
    total = jnp.sum(weights[:, :, None, None] * states, axis=0)
    return total, jnp.sum(jnp.where((places < end)[:, None], logs, 0.0), axis=0)


def body(
    seq_x,
    z_gate,
    bc_in,
    conv_x,
    conv_bc,
    log_decay,
    skip_d,
    norm_gain,
    routes,
    route_gates,
    placement,
    gate_w,
    up_w,
    down_w,
):
    highest = lax.Precision.HIGHEST
    tokens, width = seq_x.shape
    heads = width // HEAD_DIM
    ix = lax.axis_index("x")

    edge = jnp.concatenate([seq_x[tokens - CONV + 1 :], bc_in[tokens - CONV + 1 :]], axis=1)
    rim = lax.ppermute(edge, CTX, [(i, i + 1) for i in range(31)])

    span = gate_w.shape[1] // 4
    gate_own, up_own = gate_w[0], up_w[0]
    down_own = down_w[0].reshape(LANES, 4 * span // LANES, LANES).transpose(1, 0, 2).reshape(4 * span, LANES)
    weights = []
    for s in range(4):
        start = lax.rem(ix + s, 4) * span
        piece = jnp.concatenate(
            [lax.dynamic_slice_in_dim(a, start, span, 0) for a in (gate_own, up_own, down_own)], axis=0
        )
        if s:
            piece = lax.ppermute(piece, "x", [(i, (i + s) % 4) for i in range(4)])
        weights.append(piece)

    experts = placement.shape[0]
    flat = routes.reshape(tokens * 2)
    onehot = (flat[:, None] == jnp.arange(experts, dtype=jnp.int32)[None, :]).astype(BF)
    places = jnp.arange(tokens * 2)
    tri = (places[:, None] > places[None, :]).astype(BF)
    before = dot(tri, onehot)
    hot = onehot.astype(F32)
    ranks = jnp.sum(before * hot, axis=1).astype(jnp.int32)
    owners = jnp.sum(hot * placement[None, :].astype(F32), axis=1).astype(jnp.int32)
    half = (ranks >= HALF).astype(jnp.int32)
    base = owners * PIECE + ranks - HALF * half
    half, base = half.reshape(tokens, 2), base.reshape(tokens, 2)
    columns = jnp.arange(experts * PIECE, dtype=jnp.int32)

    def table(values):
        planes = []
        for plane in range(4):
            if plane < 2:
                where, value = base + 2 * HALF * plane + HALF * half, values
            else:
                where, value = base + 4 * HALF, jnp.where(half == plane - 2, values, 0.0)
            hit = where[:, :, None] == columns[None, None, :]
            planes.append(jnp.sum(jnp.where(hit, value[:, :, None], 0.0), axis=1))
        return jnp.stack(planes)

    select = table(jnp.ones((tokens, 2), F32)).astype(BF)
    mixing = table(route_gates)

    long_x = jnp.concatenate([rim[:, :width], seq_x], axis=0).astype(F32)
    long_bc = jnp.concatenate([rim[:, width:], bc_in], axis=0).astype(F32)
    xs = jnp.zeros((tokens, width), F32)
    bcs = jnp.zeros((tokens, bc_in.shape[1]), F32)
    for offset in range(CONV):
        xs = xs + conv_x[offset][None, :] * long_x[offset : offset + tokens]
        bcs = bcs + conv_bc[offset][None, :] * long_bc[offset : offset + tokens]
    xs = jax.nn.silu(xs)
    bcs = jax.nn.silu(bcs)
    head_x = xs.reshape(tokens, heads, HEAD_DIM)
    in_keys, out_keys = bcs[:, :STATE], bcs[:, STATE:]
    steps = jnp.arange(tokens)
    lower = steps[:, None] >= steps[None, :]
    running = jnp.dot(lower.astype(F32), log_decay, precision=highest)
    tails = jnp.exp(running[-1:] - running)
    own_state = jnp.einsum("jh,jhp,jn->hpn", tails, head_x, in_keys, precision=highest)
    own_log = running[-1]

    near = lax.all_gather(pack_state(own_state, own_log), NEAR)
    near_states, near_logs = unpack_state(near, heads)
    count = near_logs.shape[0]
    near_carried, near_log = prefix(near_states, near_logs, lax.axis_index(NEAR))
    group_state, group_log = prefix(near_states, near_logs, count)
    far = lax.all_gather(pack_state(group_state, group_log), "zh")
    far_states, far_logs = unpack_state(far, heads)
    far_carried, _ = prefix(far_states, far_logs, lax.axis_index("zh"))
    carried = near_carried + jnp.exp(near_log)[:, None, None] * far_carried

    gaps = running[:, None, :] - running[None, :, :]
    weights_in = jnp.where(lower[:, :, None], jnp.exp(jnp.where(lower[:, :, None], gaps, 0.0)), 0.0)
    scores = jnp.einsum("in,jn->ij", out_keys, in_keys, precision=highest)
    inner = jnp.einsum("ij,ijh,jhp->ihp", scores, weights_in, head_x, precision=highest)
    outer = jnp.einsum("in,hpn->ihp", out_keys, carried, precision=highest) * jnp.exp(running)[..., None]
    outputs = inner + outer + skip_d[None, :, None] * head_x
    gated = outputs * jax.nn.silu(z_gate.astype(F32).reshape(tokens, heads, HEAD_DIM))
    scales = lax.rsqrt(jnp.mean(gated * gated, axis=-1, keepdims=True) + 1e-05)
    normed = (gated * scales * norm_gain.reshape(heads, HEAD_DIM)).reshape(tokens, width).astype(BF)

    blank = jnp.zeros((tokens, 64), BF)
    planes = jnp.stack(
        [
            normed[:, :128],
            normed[:, 128:256],
            jnp.concatenate([normed[:, 256:], blank], axis=1),
            jnp.concatenate([blank, normed[:, 256:]], axis=1),
        ]
    )
    outgoing = jnp.einsum("btj,btl->jl", select, planes, preferred_element_type=F32).astype(BF)
    arrived = lax.all_to_all(outgoing.reshape(experts, PIECE, LANES), CTX, 0, 0, tiled=True)
    rows = (
        arrived[:, : GROUPS * HALF]
        .reshape(experts, GROUPS, HALF, LANES)
        .transpose(1, 0, 2, 3)
        .reshape(GROUPS * experts * HALF, LANES)
    )
    wide = lax.all_gather(rows, "y")
    ixs = ix.reshape(1).astype(jnp.int32)
    count = 2 * experts * HALF
    parts = kernel_call(gate_up_kernel, jax.ShapeDtypeStruct((4, 2 * count, LANES), BF), 6)(
        ixs, wide, *weights
    )
    parts = lax.all_to_all(parts, "x", 0, 0, tiled=True)
    hidden = kernel_call(hidden_kernel, jax.ShapeDtypeStruct((count, LANES), BF), 1, 0)(parts)
    hiddens = lax.all_gather(hidden, "x")
    downs = kernel_call(down_kernel, jax.ShapeDtypeStruct((4, count * 5 // 2, LANES), BF), 6)(
        ixs, hiddens, *weights
    )
    downs = lax.all_to_all(downs, "y", 0, 0, tiled=True)
    result = jnp.sum(downs.astype(F32), axis=0).astype(BF)
    result = result.reshape(GROUPS, experts, HALF, LANES).transpose(1, 0, 2, 3)
    result = jnp.pad(result.reshape(experts, GROUPS * HALF, LANES), ((0, 0), (0, 2), (0, 0)))
    returned = lax.all_to_all(result, CTX, 0, 0, tiled=True).reshape(experts * PIECE, LANES)
    high, low = split_log(mixing)
    summed = jnp.einsum("btj,jl->btl", high, returned, preferred_element_type=F32) + jnp.einsum(
        "btj,jl->btl", low, returned, preferred_element_type=F32
    )
    mixed = jnp.concatenate([summed[0], summed[1], summed[2][:, :64] + summed[3][:, 64:]], axis=1)
    return (normed, mixed.astype(BF))


def solution(mesh):
    split = Mesh(mesh.devices.reshape(4, 4, 2, 4, 4), ("zh", "zl", "c", "x", "y"))
    placed = (
        P(CTX, EXP),
        P(CTX, EXP),
        P(CTX, None),
        P(None, EXP),
        P(),
        P(CTX, EXP),
        P(EXP),
        P(EXP),
        P(CTX, None),
        P(CTX, None),
        P(),
        P(CTX, None, EXP),
        P(CTX, None, EXP),
        P(CTX, EXP, None),
    )
    return jax.shard_map(
        body,
        mesh=split,
        in_specs=placed,
        out_specs=(P(CTX, EXP), P(CTX, EXP)),
        check_vma=False,
    )
```

time: 829 us -> 216 us (0.26)
  waiting for transfers between devices: 433 us -> 15.6 us
  blocking collectives: 284 us -> 128 us
  local copies, waits for them, and re-layouts: 55.1 us -> 18.9 us
  between operations: 14.1 us -> 1.35 us
  starting transfers between devices: 12.3 us -> 23.7 us
    all_to_all x1, waiting for transfers between devices: 231 us -> 15.6 us  [body(): lax.all_to_all(outgoing.reshape(experts, PIECE, LANES), CTX, 0, 0, tiled=...]
    all_to_all x1 -> x3, blocking collectives: 249 us -> 59.6 us  [the longest x1 34.5 us: body(): lax.all_to_all(result, CTX, 0, 0, tiled=True)]
    all_gather x2 -> x0, waiting for transfers between devices: 120 us -> none  [the longest x1 78.4 us: body(): full = lax.all_gather(normed, 'exp', axis=1, tiled=True)]
    unnamed x4 -> x0, waiting for transfers between devices: 80.7 us -> none
    all_gather x1 -> x4, blocking collectives: 34.1 us -> 68.7 us  [the longest x1 27.9 us: body(): far = lax.all_gather(pack_state(group_state, group_log), 'zh')]
    reshape x3 -> x1, local copies, waits for them, and re-layouts: 14.8 us -> 0.08 us  [body(): result = result.reshape(GROUPS, experts, HALF, LANES).transpose(1, 0, 2, 3)]
    gather x2 -> x0, local copies, waits for them, and re-layouts: 13.6 us -> none  [the longest x1 8.81 us: body(): picked = returned.reshape(experts * capacity, parts.shape[2])[positions]]
    convert_element_type x2 -> x0, local copies, waits for them, and re-layouts: 13.3 us -> none  [the longest x1 6.72 us: expert_part(): jnp.einsum('eif,fd->eid', hidden, down_rows, preferred_element_type=jnp.f...]
  transfers between devices with their start and end apart: 6 -> 5, of which waited for: 5 -> 1; matrix products, arithmetic and copies ran while one was open for 1% -> 16% of each run, Pallas kernels for 0% -> 0%
where the time goes in v1:
time: 216 us
  blocking collectives  128 us (59%)
  starting transfers between devices  23.7 us (11%)
  local copies, waits for them, and re-layouts  18.9 us (9%)
  waiting for transfers between devices  15.6 us (7%)
  other arithmetic  15.1 us (7%)
  matrix products  7.91 us (4%)
  Pallas kernels  4.7 us (2%)
    all_to_all x1, blocking collectives, body(): lax.all_to_all(result, CTX, 0, 0, tiled=True)  34.5 us
    all_gather x1, blocking collectives, body(): far = lax.all_gather(pack_state(group_state, group_log), 'zh')  27.9 us
    all_gather x1, blocking collectives, body(): near = lax.all_gather(pack_state(own_state, own_log), NEAR)  17.6 us
    all_to_all x1, waiting for transfers between devices, body(): lax.all_to_all(outgoing.reshape(experts, PIECE, LANES), CTX, 0, 0, tiled=...  15.6 us
    all_gather x1, blocking collectives, body(): wide = lax.all_gather(rows, 'y')  13.6 us
    all_to_all x1, blocking collectives, body(): parts = lax.all_to_all(parts, 'x', 0, 0, tiled=True)  13.1 us
    all_to_all x1, blocking collectives, body(): downs = lax.all_to_all(downs, 'y', 0, 0, tiled=True)  11.9 us
    ppermute x3, starting transfers between devices, body(): piece = lax.ppermute(piece, 'x', [(i, (i + s) % 4) for i in range(4)])  11.3 us
  transfers between devices with their start and end apart: 5, of which 1 were waited for; matrix products, arithmetic and copies ran while one was open for 16% of the time, Pallas kernels for 0%

profile of v1, /device:TPU:1, one launch (start us, length us, event | category | flops | bytes accessed | tf_op | source)
XLA Modules:
  0.0 215.5 jit_solution(10441248905658448847)
XLA Ops:
  1.3 1.0 slice.190
  3.1 4.9 %collective-permute-start = (bf16[3,576]{1,0:T(4,128)(2,1)}, bf16[3,576]{1,0:T(4,128)(2,1)S(1)}, u32[]{:S(2)}, u32[]{:S(2)}) collective-permute-start(bf16[3,576]{1,0:T(4,128)(2,1)} %pad_maximum_fusion.8), channel_id=1, source_target_pairs={{0,16},{16,32},{32,48},{48,64},{64,80},{80,96},{96,112},{112,128},... | collective-permute-start | bytes 10376 | tf_op jit(solution)/shard_map/ppermute | solution.py:150
  8.1 1.6 copy.157
  10.0 0.9 constant_dynamic-slice_fusion.3
  11.9 1.0 dynamic-slice_bitcast_fusion
  12.9 1.0 pad_maximum_fusion.3
  14.0 4.8 %collective-permute-start.2 = (bf16[3840,128]{1,0:T(8,128)(2,1)}, bf16[3840,128]{1,0:T(8,128)(2,1)S(1)}, u32[]{:S(2)}, u32[]{:S(2)}) collective-permute-start(bf16[3840,128]{1,0:T(8,128)(2,1)} %pad_maximum_fusion.3), channel_id=1, source_target_pairs={{0,8},{4,12},{8,0},{12,4},{1,9},{5,13},{9,1},{13,5},{2,10},{6,14},... | collective-permute-start | bytes 2949128 | tf_op jit(solution)/shard_map/ppermute | solution.py:162
  18.8 1.0 pad_maximum_fusion.2
  19.8 2.2 %collective-permute-start.1 = (bf16[3840,128]{1,0:T(8,128)(2,1)}, bf16[3840,128]{1,0:T(8,128)(2,1)S(1)}, u32[]{:S(2)}, u32[]{:S(2)}) collective-permute-start(bf16[3840,128]{1,0:T(8,128)(2,1)} %pad_maximum_fusion.2), channel_id=1, source_target_pairs={{0,4},{4,8},{8,12},{12,0},{1,5},{5,9},{9,13},{13,1},{2,6},{6,10},{... | collective-permute-start | bytes 2949128 | tf_op jit(solution)/shard_map/ppermute | solution.py:162
  26.8 2.2 %select_reduce_fusion.5 = (f32[128,1024]{1,0:T(8,128)}, bf16[128,1024]{1,0:T(8,128)(2,1)}, bf16[128,1024]{1,0:T(8,128)(2,1)S(1)}, f32[128,1024]{1,0:T(8,128)}, b...) fusion(f32[128,2]{0,1:T(2,128)S(1)} %copy.127, ...), kind=kLoop, calls=%fused_computation.30 | loop fusion | flops 3932160 | bytes 3153920 | tf_op jit(solution)/shard_map/reduce_sum | solution.py:187
  29.7 1.8 copy.135
  32.3 0.9 copy.131
  35.1 0.9 maximum_convert_fusion.1
  36.7 0.9 fusion.52
  38.8 17.6 %all-gather = bf16[2688,128]{1,0:T(8,128)(2,1)S(1)} all-gather(bf16[336,128]{1,0:T(8,128)(2,1)S(1)} %pad_maximum_fusion.5), channel_id=2, replica_groups=mesh['zh'=4,'zl'=4,'c'=2,'x'=4,'y'=4] {'zl','c'}, dimensions={0}, use_global_device_ids=true | all-gather | bytes 774144 | tf_op jit(solution)/shard_map/all_gather | solution.py:211
  57.4 1.5 fusion.1
  58.9 27.9 %all-gather.1 = bf16[1344,128]{1,0:T(8,128)(2,1)S(1)} all-gather(bf16[336,128]{1,0:T(8,128)(2,1)S(1)} %pad_maximum_fusion.6), channel_id=3, replica_groups=mesh['zh'=4,'zl'=4,'c'=2,'x'=4,'y'=4] {'zh'}, dimensions={0}, use_global_device_ids=true | all-gather | bytes 430080 | tf_op jit(solution)/shard_map/all_gather | solution.py:216
  87.4 1.3 convolution_multiply_fusion
  88.7 1.8 multiply_reduce_fusion.1
  93.5 2.4 %fusion.3 = bf16[1024,128]{1,0:T(8,128)(2,1)} fusion(bf16[1,128,1024]{1,2,0:T(8,128)(2,1)S(1)} %bitcast.138, bf16[1,128,1024]{1,2,0:T(8,128)(2,1)} %bitcast.139, bf16[1,128,1024]{1,2,0:T(8,128)(2,1)} %bitcast.140, bf16[1,128,1024]{1,2,0:T(8,128)(2,1)} %bitcast.141, bf16[1,128,128]{2,1,0:T(8,128)(2,1)} %get-tuple-element.89, ...), kind=kOutput, calls=%fused_computation.8 | convolution fusion | flops 136118272 | bytes 1441792 | tf_op jit(solution)/shard_map/btj,btl->jl/dot_general | solution.py:240
  95.8 7.5 %all-to-all-start = ((bf16[32,32,128]{2,1,0:T(8,128)(2,1)}), bf16[32,32,128]{2,1,0:T(8,128)(2,1)S(1)}, u32[]{:S(2)}, u32[]{:S(2)}) async-start(bf16[32,32,128]{2,1,0:T(8,128)(2,1)} %bitcast.142), calls=%async_computation | async-start | bytes 524288 | tf_op jit(solution)/shard_map/all_to_all | solution.py:241
  103.4 1.0 pad_maximum_fusion.4
  104.4 4.3 %collective-permute-start.3 = (bf16[3840,128]{1,0:T(8,128)(2,1)}, bf16[3840,128]{1,0:T(8,128)(2,1)}, u32[]{:S(2)}, u32[]{:S(2)}) collective-permute-start(bf16[3840,128]{1,0:T(8,128)(2,1)} %pad_maximum_fusion.4), channel_id=1, source_target_pairs={{0,12},{4,0},{8,4},{12,8},{1,13},{5,1},{9,5},{13,9},{2,14},{6,2},{... | collective-permute-start | bytes 2949128 | tf_op jit(solution)/shard_map/ppermute | solution.py:162
  108.7 1.1 pad_maximum_fusion.1.w0_ref
  109.8 15.6 %all-to-all-done = bf16[32,32,128]{2,1,0:T(8,128)(2,1)S(1)} async-done(((bf16[32,32,128]{2,1,0:T(8,128)(2,1)}), bf16[32,32,128]{2,1,0:T(8,128)(2,1)S(1)}, u32[]{:S(2)}, u32[]{:S(2)}) %all-to-all-start) | async-done | bytes 262176 | tf_op jit(solution)/shard_map/all_to_all | solution.py:241
  125.7 13.6 %all_gather.25.g_ref = bf16[4,960,128]{2,1,0:T(8,128)(2,1)S(1)} all-gather(bf16[1,960,128]{2,1,0:T(8,128)(2,1)S(1)} %all_gather_reshape.3), channel_id=1, replica_groups=mesh['zh'=4,'zl'=4,'c'=2,'x'=4,'y'=4] {'y'}, dimensions={0}, use_global_device_ids=true | all-gather | bytes 1228800 | tf_op jit(solution)/shard_map/all_gather | solution.py:248
  139.3 2.6 %shard_map.149 = bf16[4,768,128]{2,1,0:T(8,128)(2,1)S(1)} custom-call(s32[1]{0:T(128)} %bitcast.24.ix_ref, bf16[4,960,128]{2,1,0:T(8,128)(2,1)S(1)} %all_gather.25.g_ref, bf16[3840,128]{1,0:T(8,128)(2,1)S(1)} %pad_maximum_fusion.1.w0_ref, bf16[3840,128]{1,0:T(8,128)(2,1)S(1)} %collective-permute-done.1.w1_ref, ...), custom_call_target="tpu_custom_call" | custom-call | tf_op jit(solution)/shard_map/pallas_call | solution.py:251
  141.9 13.1 %all_to_all.20.p_ref = bf16[4,768,128]{2,1,0:T(8,128)(2,1)S(1)} all-to-all(bf16[4,768,128]{2,1,0:T(8,128)(2,1)S(1)} %shard_map.149), channel_id=1, replica_groups=mesh['zh'=4,'zl'=4,'c'=2,'x'=4,'y'=4] {'x'}, dimensions={0} | all-to-all | bytes 1572864 | tf_op jit(solution)/shard_map/all_to_all | solution.py:254
  155.2 9.6 %all-gather.2 = bf16[1536,128]{1,0:T(8,128)(2,1)S(1)} all-gather(bf16[384,128]{1,0:T(8,128)(2,1)S(1)} %shard_map.150), channel_id=4, replica_groups=mesh['zh'=4,'zl'=4,'c'=2,'x'=4,'y'=4] {'x'}, dimensions={0}, use_global_device_ids=true | all-gather | bytes 491520 | tf_op jit(solution)/shard_map/all_gather | solution.py:256
  164.8 2.0 shard_map.151
  166.8 11.9 %all_to_all.21 = bf16[4,960,128]{2,1,0:T(8,128)(2,1)S(1)} all-to-all(bf16[4,960,128]{2,1,0:T(8,128)(2,1)S(1)} %shard_map.151), channel_id=1, replica_groups=mesh['zh'=4,'zl'=4,'c'=2,'x'=4,'y'=4] {'y'}, dimensions={0} | all-to-all | bytes 1966080 | tf_op jit(solution)/shard_map/all_to_all | solution.py:260
  179.3 34.5 %all_to_all.22 = bf16[32,32,128]{2,1,0:T(8,128)(2,1)S(1)} all-to-all(bf16[32,32,128]{2,1,0:T(8,128)(2,1)S(1)} %pad.21.clone), channel_id=1, replica_groups=mesh['zh'=4,'zl'=4,'c'=2,'x'=4,'y'=4] {'zh','zl','c'}, dimensions={0} | all-to-all | bytes 524288 | tf_op jit(solution)/shard_map/all_to_all | solution.py:264
  (165 shorter events, 19.8 us)
Async XLA Ops:
  0.6 22.1 %copy-start = (f32[128,5]{0,1:T(8,128)S(1)}, f32[128,5]{0,1:T(8,128)}, u32[]{:S(2)}) copy-start(f32[128,5]{0,1:T(8,128)} %param.27) | copy-start | bytes 7684
  3.1 31.7 %collective-permute-start = (bf16[3,576]{1,0:T(4,128)(2,1)}, bf16[3,576]{1,0:T(4,128)(2,1)S(1)}, u32[]{:S(2)}, u32[]{:S(2)}) collective-permute-start(bf16[3,576]{1,0:T(4,128)(2,1)} %pad_maximum_fusion.8), channel_id=1, source_target_pairs={{0,16},{16,32},{32,48},{48,64},{64,80},{80,96},{96,112},{112,128},... | collective-permute-start | bytes 10376 | tf_op jit(solution)/shard_map/ppermute | solution.py:150
  14.0 8.1 %copy-start.31 = (s32[32]{0:T(128)S(1)}, s32[32]{0:T(128)}, u32[]{:S(2)}) copy-start(s32[32]{0:T(128)} %param.32) | copy-start | bytes 388
  14.0 9.6 %copy-start.20 = (f32[4,256]{1,0:T(4,128)S(1)}, f32[4,256]{1,0:T(4,128)}, u32[]{:S(2)}) copy-start(f32[4,256]{1,0:T(4,128)} %param.26) | copy-start | bytes 12292
  14.0 10.2 %copy-start.14 = (f32[4,320]{1,0:T(4,128)S(1)}, f32[4,320]{1,0:T(4,128)}, u32[]{:S(2)}) copy-start(f32[4,320]{1,0:T(4,128)} %param.25) | copy-start | bytes 15364
  14.0 10.3 %copy-start.26 = (s32[128,2]{0,1:T(2,128)S(1)}, s32[128,2]{0,1:T(2,128)}, u32[]{:S(2)}) copy-start(s32[128,2]{0,1:T(2,128)} %param.30) | copy-start | bytes 3076
  14.0 11.7 %copy-start.15 = (f32[128,2]{0,1:T(2,128)S(1)}, f32[128,2]{0,1:T(2,128)}, u32[]{:S(2)}) copy-start(f32[128,2]{0,1:T(2,128)} %param.31) | copy-start | bytes 3076
  14.0 125.3 %collective-permute-start.2 = (bf16[3840,128]{1,0:T(8,128)(2,1)}, bf16[3840,128]{1,0:T(8,128)(2,1)S(1)}, u32[]{:S(2)}, u32[]{:S(2)}) collective-permute-start(bf16[3840,128]{1,0:T(8,128)(2,1)} %pad_maximum_fusion.3), channel_id=1, source_target_pairs={{0,8},{4,12},{8,0},{12,4},{1,9},{5,13},{9,1},{13,5},{2,10},{6,14},... | collective-permute-start | bytes 2949128 | tf_op jit(solution)/shard_map/ppermute | solution.py:162
  19.8 119.5 %collective-permute-start.1 = (bf16[3840,128]{1,0:T(8,128)(2,1)}, bf16[3840,128]{1,0:T(8,128)(2,1)S(1)}, u32[]{:S(2)}, u32[]{:S(2)}) collective-permute-start(bf16[3840,128]{1,0:T(8,128)(2,1)} %pad_maximum_fusion.2), channel_id=1, source_target_pairs={{0,4},{4,8},{8,12},{12,0},{1,5},{5,9},{9,13},{13,1},{2,6},{6,10},{... | collective-permute-start | bytes 2949128 | tf_op jit(solution)/shard_map/ppermute | solution.py:162
  22.0 4.1 %copy-start.22 = (pred[8]{0:T(512)(128)(4,1)}, pred[8]{0:T(512)(128)(4,1)S(1)}, u32[]{:S(2)}) copy-start(pred[8]{0:T(512)(128)(4,1)S(1)} %iota_compare_fusion.11) | copy-start | bytes 28
  22.1 4.0 %copy-start.24 = (pred[8]{0:T(512)(128)(4,1)}, pred[8]{0:T(512)(128)(4,1)S(1)}, u32[]{:S(2)}) copy-start(pred[8]{0:T(512)(128)(4,1)S(1)} %iota_compare_fusion.13) | copy-start | bytes 28
  29.0 5.1 %copy-start.30 = (bf16[1,5]{1,0:T(2,128)(2,1)S(1)}, bf16[1,5]{1,0:T(2,128)(2,1)}, u32[]{:S(2)}) copy-start(bf16[1,5]{1,0:T(2,128)(2,1)} %get-tuple-element.107) | copy-start | bytes 34
  29.0 6.9 %copy-start.16 = (f32[1,256]{1,0:T(1,128)S(1)}, f32[1,256]{1,0:T(1,128)}, u32[]{:S(2)}) copy-start(f32[1,256]{1,0:T(1,128)} %get-tuple-element.95) | copy-start | bytes 3076
  29.0 7.0 %copy-start.17 = (f32[1,256]{1,0:T(1,128)S(1)}, f32[1,256]{1,0:T(1,128)}, u32[]{:S(2)}) copy-start(f32[1,256]{1,0:T(1,128)} %get-tuple-element.96) | copy-start | bytes 3076
  31.5 6.2 %copy-start.12 = (bf16[128,320]{0,1:T(8,128)(2,1)S(1)}, bf16[128,320]{0,1:T(8,128)(2,1)}, u32[]{:S(2)}) copy-start(bf16[128,320]{0,1:T(8,128)(2,1)} %param.22) | copy-start | bytes 245764
  37.6 18.8 %copy-start.18 = (pred[8,8]{1,0:T(8,128)(4,1)S(1)}, pred[8,8]{1,0:T(8,128)(4,1)}, u32[]{:S(2)}) copy-start(pred[8,8]{1,0:T(8,128)(4,1)} %get-tuple-element.112) | copy-start | bytes 196
  37.6 18.9 %copy-start.19 = (pred[8,8]{1,0:T(8,128)(4,1)S(1)}, pred[8,8]{1,0:T(8,128)(4,1)}, u32[]{:S(2)}) copy-start(pred[8,8]{1,0:T(8,128)(4,1)} %get-tuple-element.113) | copy-start | bytes 196
  37.6 18.9 %copy-start.23 = (pred[8]{0:T(512)(128)(4,1)S(1)}, pred[8]{0:T(512)(128)(4,1)}, u32[]{:S(2)}) copy-start(pred[8]{0:T(512)(128)(4,1)} %copy-done.22) | copy-start | bytes 28
  37.6 18.9 %copy-start.25 = (pred[8]{0:T(512)(128)(4,1)S(1)}, pred[8]{0:T(512)(128)(4,1)}, u32[]{:S(2)}) copy-start(pred[8]{0:T(512)(128)(4,1)} %copy-done.24) | copy-start | bytes 28
  38.8 48.0 %copy-start.29 = (pred[4,4]{1,0:T(4,128)(4,1)S(1)}, pred[4,4]{1,0:T(4,128)(4,1)}, u32[]{:S(2)}) copy-start(pred[4,4]{1,0:T(4,128)(4,1)} %fusion.65) | copy-start | bytes 52
  38.8 48.1 %copy-start.28 = (pred[4]{0:T(512)(128)(4,1)S(1)}, pred[4]{0:T(512)(128)(4,1)}, u32[]{:S(2)}) copy-start(pred[4]{0:T(512)(128)(4,1)} %copy-done.27) | copy-start | bytes 16
  57.4 31.3 %copy-start.32 = (f32[5]{0:T(128)S(1)}, f32[5]{0:T(128)}, u32[]{:S(2)}) copy-start(f32[5]{0:T(128)} %param.28) | copy-start | bytes 64
  58.9 29.7 %copy-start.6 = (f32[128,320]{0,1:T(8,128)S(1)}, f32[128,320]{0,1:T(8,128)}, u32[]{:S(2)}) copy-start(f32[128,320]{0,1:T(8,128)} %copy-done.5) | copy-start | bytes 491524
  88.6 4.8 %copy-start.13 = (bf16[128,1024]{0,1:T(8,128)(2,1)S(1)}, bf16[128,1024]{0,1:T(8,128)(2,1)}, u32[]{:S(2)}) copy-start(bf16[128,1024]{0,1:T(8,128)(2,1)} %copy.135) | copy-start | bytes 786436
  93.5 9.9 %copy-start.1 = (bf16[1280,128]{1,0:T(8,128)(2,1)S(1)}, bf16[1280,128]{1,0:T(8,128)(2,1)}, u32[]{:S(2)}) copy-start(bf16[1280,128]{1,0:T(8,128)(2,1)} %get-tuple-element.121) | copy-start | bytes 983044
  93.5 9.9 %copy-start.4 = (bf16[1280,128]{1,0:T(8,128)(2,1)S(1)}, bf16[1280,128]{1,0:T(8,128)(2,1)}, u32[]{:S(2)}) copy-start(bf16[1280,128]{1,0:T(8,128)(2,1)} %get-tuple-element.76) | copy-start | bytes 983044
  95.8 29.5 %all-to-all-start = ((bf16[32,32,128]{2,1,0:T(8,128)(2,1)}), bf16[32,32,128]{2,1,0:T(8,128)(2,1)S(1)}, u32[]{:S(2)}, u32[]{:S(2)}) async-start(bf16[32,32,128]{2,1,0:T(8,128)(2,1)} %bitcast.142), calls=%async_computation | async-start | bytes 524288 | tf_op jit(solution)/shard_map/all_to_all | solution.py:241
  104.4 34.9 %collective-permute-start.3 = (bf16[3840,128]{1,0:T(8,128)(2,1)}, bf16[3840,128]{1,0:T(8,128)(2,1)}, u32[]{:S(2)}, u32[]{:S(2)}) collective-permute-start(bf16[3840,128]{1,0:T(8,128)(2,1)} %pad_maximum_fusion.4), channel_id=1, source_target_pairs={{0,12},{4,0},{8,4},{12,8},{1,13},{5,1},{9,5},{13,9},{2,14},{6,2},{... | collective-permute-start | bytes 2949128 | tf_op jit(solution)/shard_map/ppermute | solution.py:162
  179.0 34.9 %copy-start.7 = (f32[128,1024]{1,0:T(8,128)S(1)}, f32[128,1024]{1,0:T(8,128)}, u32[]{:S(2)}) copy-start(f32[128,1024]{1,0:T(8,128)} %get-tuple-element.64) | copy-start | bytes 1572868
  179.0 34.9 %copy-start.8 = (f32[128,1024]{1,0:T(8,128)S(1)}, f32[128,1024]{1,0:T(8,128)}, u32[]{:S(2)}) copy-start(f32[128,1024]{1,0:T(8,128)} %get-tuple-element.67) | copy-start | bytes 1572868
  179.0 34.9 %copy-start.9 = (f32[128,1024]{1,0:T(8,128)S(1)}, f32[128,1024]{1,0:T(8,128)}, u32[]{:S(2)}) copy-start(f32[128,1024]{1,0:T(8,128)} %get-tuple-element.115) | copy-start | bytes 1572868
  179.0 34.8 %copy-start.10 = (f32[128,1024]{1,0:T(8,128)S(1)}, f32[128,1024]{1,0:T(8,128)}, u32[]{:S(2)}) copy-start(f32[128,1024]{1,0:T(8,128)} %get-tuple-element.117) | copy-start | bytes 1572868
  (6 other events, 9.1 us)

commit v2 on v1

v2 whole, which is shorter than its diff:
```python
import jax
import jax.numpy as jnp
from jax import lax
from jax.experimental import pallas as pl
from jax.experimental.pallas import tpu as pltpu
from jax.sharding import Mesh
from jax.sharding import PartitionSpec as P

HEAD_DIM = 64
STATE = 128
CONV = 4
CTX = ("zh", "zl", "c")
EXP = ("x", "y")
NEAR = ("zl", "c")
LANES = 128
HALF = 6
GROUPS = 5
PIECE = 32

BF = jnp.bfloat16
F32 = jnp.float32


def dot(a, b):
    return jnp.dot(a, b, preferred_element_type=F32)


def kernel_call(kernel, outs, *operands, scalars=0, scratch=()):
    specs = [pl.BlockSpec(memory_space=pltpu.SMEM)] * scalars
    specs += [pl.BlockSpec(memory_space=pltpu.VMEM)] * (len(operands) - scalars)
    shapes = [jax.ShapeDtypeStruct(shape, kind) for shape, kind in outs]
    result = pl.pallas_call(
        kernel,
        out_shape=shapes,
        in_specs=specs,
        out_specs=[pl.BlockSpec(memory_space=pltpu.VMEM)] * len(outs),
        scratch_shapes=list(scratch),
        compiler_params=pltpu.CompilerParams(vmem_limit_bytes=48 << 20),
    )(*operands)
    return result[0] if len(outs) == 1 else result


def exact(a, b, dims=((1,), (0,))):
    return lax.dot_general(a, b, (dims, ((), ())), precision=lax.Precision.HIGHEST, preferred_element_type=F32)


def iota(shape, axis):
    return lax.broadcasted_iota(jnp.int32, shape, axis)


def silu(value):
    return value * jax.nn.sigmoid(value)


def turned(value):
    return value.astype(F32).T


def column(row):
    size = row.shape[1]
    hit = iota((size, size), 0) == iota((size, size), 1)
    return jnp.sum(jnp.where(hit, row.astype(F32), 0.0), axis=1, keepdims=True)


def edge_kernel(x_ref, bc_ref, out_ref):
    width, rows = x_ref.shape
    out_ref[:, :width] = turned(x_ref[...])[rows - 16 :].astype(BF)
    out_ref[:, width:384] = jnp.zeros((16, 384 - width), BF)
    out_ref[:, 384:] = bc_ref[rows - 16 :]


def route_kernel(routes_ref, row_ref, select_ref, pick_ref, half_ref):
    tokens = routes_ref.shape[1]
    experts = row_ref.shape[1]
    slots = experts * PIECE
    hot = [
        (column(routes_ref[k : k + 1]) == iota((tokens, experts), 1).astype(F32)).astype(F32)
        for k in range(2)
    ]
    earlier = (iota((tokens, tokens), 0) > iota((tokens, tokens), 1)).astype(BF)
    before = dot(earlier, (hot[0] + hot[1]).astype(BF))
    for k in range(2):
        rank = jnp.sum(hot[k] * before, axis=1, keepdims=True).astype(jnp.int32)
        owner = jnp.sum(hot[k] * row_ref[...].astype(F32), axis=1, keepdims=True).astype(jnp.int32)
        half = (rank >= HALF).astype(jnp.int32)
        base = owner * PIECE + rank - HALF * half
        half_ref[:, k : k + 1] = half.astype(F32)
        places = iota((tokens, slots), 1)
        for plane, where in enumerate((base + HALF * half, base + HALF * (half + 2), base + 4 * HALF)):
            start = (plane * 2 + k) * tokens
            pick_ref[start : start + tokens] = (places == where).astype(F32).astype(BF)
    hot = [(routes_ref[k : k + 1] == iota((experts, tokens), 0)).astype(F32) for k in range(2)]
    later = (iota((tokens, tokens), 0) < iota((tokens, tokens), 1)).astype(BF)
    before = dot((hot[0] + hot[1]).astype(BF), later)
    places = iota((slots, tokens), 0)
    planes = [jnp.zeros((slots, tokens), F32)] * 4
    owned = column(row_ref[...])
    for k in range(2):
        rank = jnp.sum(hot[k] * before, axis=0, keepdims=True).astype(jnp.int32)
        owner = jnp.sum(hot[k] * owned, axis=0, keepdims=True).astype(jnp.int32)
        half = (rank >= HALF).astype(jnp.int32)
        base = owner * PIECE + rank - HALF * half
        last = base + 4 * HALF
        wheres = (
            base + HALF * half,
            base + HALF * (half + 2),
            jnp.where(half == 0, last, -1),
            jnp.where(half == 1, last, -1),
        )
        planes = [p + (places == w).astype(F32) for p, w in zip(planes, wheres)]
    for plane in range(4):
        select_ref[:, plane * tokens : (plane + 1) * tokens] = planes[plane].astype(BF)


def spread(columns, heads):
    rows = columns.shape[0]
    return jnp.concatenate(
        [jnp.broadcast_to(columns[:, h : h + 1], (rows, HEAD_DIM)) for h in range(heads)], axis=1
    )


def write_logs(ref, start, logs):
    high = logs.astype(BF).astype(F32)
    places = iota((16, STATE), 0)
    tail = jnp.where(places == 0, high, jnp.where(places == 1, logs - high, 0.0))
    ref[start : start + 16] = tail.astype(BF)


def read_logs(tail):
    tail = tail.astype(F32)
    return tail[0:1] + tail[1:2]


def state_kernel(x_ref, bc_ref, rim_ref, cx_ref, cbc_ref, decay_ref, xs_ref, bcs_ref, run_ref, turn_ref, msg_ref, scratch):
    width, tokens = x_ref.shape
    heads = width // HEAD_DIM

    def conv(rim, value, taps):
        long = jnp.concatenate([rim.astype(F32), value], axis=0)
        total = taps[CONV - 1 : CONV] * long[16:]
        for back in range(1, CONV):
            total += taps[CONV - 1 - back : CONV - back] * pltpu.roll(long, back, 0)[16:]
        return silu(total)

    parts = []
    for start in range(0, width, LANES):
        stop = min(start + LANES, width)
        parts.append(conv(rim_ref[:, start:stop], turned(x_ref[start:stop]), cx_ref[:, start:stop]))
    xs = jnp.concatenate(parts, axis=1)
    bcs = conv(rim_ref[:, 384:], bc_ref[...].astype(F32), cbc_ref[...])
    lower = (iota((tokens, tokens), 0) >= iota((tokens, tokens), 1)).astype(F32)
    scratch[...] = jnp.zeros(scratch.shape, F32)
    scratch[:heads] = decay_ref[...]
    run = exact(lower, scratch[...], ((1,), (1,)))
    last = run[tokens - 1 : tokens]
    tails = jnp.exp(last - run)
    state = exact(xs * spread(tails, heads), bcs[:, :STATE], ((0,), (0,)))
    xs_ref[...] = xs
    bcs_ref[...] = bcs
    run_ref[...] = run
    turn_ref[...] = exact(scratch[...], lower, ((1,), (1,)))
    msg_ref[:width] = state.astype(BF)
    write_logs(msg_ref, width, last)


def inner_kernel(xs_ref, bcs_ref, run_ref, turn_ref, skip_ref, z_ref, y_ref, z_out_ref):
    tokens, width = xs_ref.shape
    lower = iota((tokens, tokens), 0) >= iota((tokens, tokens), 1)
    scores = exact(bcs_ref[:, STATE:], bcs_ref[:, :STATE], ((1,), (1,)))
    outs = []
    for h in range(width // HEAD_DIM):
        gaps = run_ref[:, h : h + 1] - turn_ref[h : h + 1]
        weight = jnp.where(lower, jnp.exp(jnp.where(lower, gaps, 0.0)), 0.0) * scores
        x = xs_ref[:, h * HEAD_DIM : (h + 1) * HEAD_DIM]
        outs.append(exact(weight, x) + skip_ref[h] * x)
    y_ref[...] = jnp.concatenate(outs, axis=1)
    z_out_ref[...] = silu(turned(z_ref[...]))


def near_kernel(place_ref, near_ref, carried_ref, log_ref, msg_ref, scratch):
    count, rows, _ = near_ref.shape
    rows -= 16
    heads = rows // HEAD_DIM
    total = [jnp.zeros((HEAD_DIM, STATE), F32)] * heads
    kept = total
    log = jnp.zeros((1, STATE), F32)
    kept_log = log
    for j in range(count):
        own = place_ref[0] == j
        kept = [jnp.where(own, t, k) for t, k in zip(total, kept)]
        kept_log = jnp.where(own, log, kept_log)
        step = read_logs(near_ref[j, rows:])
        factor = jnp.exp(step)
        log = log + step
        total = [
            factor[:, h : h + 1] * total[h] + near_ref[j, h * HEAD_DIM : (h + 1) * HEAD_DIM].astype(F32)
            for h in range(heads)
        ]
    for h in range(heads):
        carried_ref[h * HEAD_DIM : (h + 1) * HEAD_DIM] = kept[h]
        scratch[h * HEAD_DIM : (h + 1) * HEAD_DIM] = total[h].astype(BF)
    log_ref[...] = jnp.broadcast_to(kept_log, log_ref.shape)
    part = rows // 2
    msg_ref[:part] = scratch[pl.ds(pl.multiple_of(place_ref[1] * part, 32), part)]
    write_logs(msg_ref, part, log)


def far_kernel(place_ref, far_ref, out_ref):
    part = out_ref.shape[0]
    units = part // 32
    lanes = iota((1, STATE), 1)
    total = [jnp.zeros((32, STATE), F32)] * units
    for g in range(far_ref.shape[0] - 1):
        factor = jnp.exp(read_logs(far_ref[g, part:]))
        earlier = g < place_ref[2]
        for u in range(units):
            head = (place_ref[1] * units + u) // 2
            one = jnp.sum(jnp.where(lanes == head, factor, 0.0), axis=1, keepdims=True)
            state = far_ref[g, u * 32 : (u + 1) * 32].astype(F32)
            total[u] = jnp.where(earlier, one * total[u] + state, total[u])
    for u in range(units):
        out_ref[u * 32 : (u + 1) * 32] = total[u].astype(BF)


def finish_kernel(
    place_ref, own_ref, other_ref, near_ref, log_ref, bcs_ref, run_ref, y_ref, z_ref, gain_ref, select_ref,
    normed_ref, out_ref, scratch,
):
    part = own_ref.shape[0]
    tokens, width = y_ref.shape
    heads = width // HEAD_DIM
    core = place_ref[1]
    scratch[pl.ds(pl.multiple_of(core * part, 32), part)] = own_ref[...]
    scratch[pl.ds(pl.multiple_of((1 - core) * part, 32), part)] = other_ref[...]
    factor = jnp.exp(log_ref[0:1])
    carried = jnp.concatenate(
        [
            near_ref[h * HEAD_DIM : (h + 1) * HEAD_DIM]
            + factor[:, h : h + 1] * scratch[h * HEAD_DIM : (h + 1) * HEAD_DIM].astype(F32)
            for h in range(heads)
        ],
        axis=0,
    )
    outer = exact(bcs_ref[:, STATE:], carried, ((1,), (1,))) * spread(jnp.exp(run_ref[...]), heads)
    gated = (y_ref[...] + outer) * z_ref[...]
    square = gated * gated
    scales = jnp.concatenate(
        [
            jnp.broadcast_to(
                lax.rsqrt(
                    jnp.mean(square[:, h * HEAD_DIM : (h + 1) * HEAD_DIM], axis=1, keepdims=True) + 1e-05
                ),
                (tokens, HEAD_DIM),
            )
            for h in range(heads)
        ],
        axis=1,
    )
    normed = (gated * scales * gain_ref[...]).astype(BF)
    normed_ref[...] = turned(normed).astype(BF)
    blank = jnp.zeros((tokens, 64), BF)
    planes = jnp.concatenate(
        [
            normed[:, :128],
            normed[:, 128:256],
            jnp.concatenate([normed[:, 256:], blank], axis=1),
            jnp.concatenate([blank, normed[:, 256:]], axis=1),
        ],
        axis=0,
    )
    out_ref[...] = dot(select_ref[...], planes).astype(BF)


def piece_kernel(block_ref, gate_ref, up_ref, down_ref, out_ref):
    span = gate_ref.shape[0]
    out_ref[:span] = gate_ref[...]
    out_ref[span : 2 * span] = up_ref[...]
    for b in range(span // LANES):
        start = 2 * span + b * LANES
        out_ref[start : start + LANES] = down_ref[:, b * LANES : (b + 1) * LANES]


def weight_piece(block, gate, up, down):
    span = gate.shape[0] // 4
    return pl.pallas_call(
        piece_kernel,
        out_shape=jax.ShapeDtypeStruct((3 * span, LANES), BF),
        grid_spec=pltpu.PrefetchScalarGridSpec(
            num_scalar_prefetch=1,
            grid=(1,),
            in_specs=[
                pl.BlockSpec((span, LANES), lambda i, b: (b[0], 0)),
                pl.BlockSpec((span, LANES), lambda i, b: (b[0], 0)),
                pl.BlockSpec((LANES, span), lambda i, b: (0, b[0])),
            ],
            out_specs=pl.BlockSpec((3 * span, LANES), lambda i, b: (0, 0)),
        ),
        compiler_params=pltpu.CompilerParams(vmem_limit_bytes=32 << 20),
    )(block, gate, up, down)


def mix_kernel(pick_ref, rows_ref, gates_ref, half_ref, out_ref):
    tokens = gates_ref.shape[1]
    picked = dot(pick_ref[...], rows_ref[...])
    totals = [0.0, 0.0, 0.0]
    for k in range(2):
        gate = column(gates_ref[k : k + 1])
        for plane in range(3):
            start = (plane * 2 + k) * tokens
            one = picked[start : start + tokens]
            if plane == 2:
                one = jnp.where(half_ref[:, k : k + 1] > 0.5, one[:, 64:], one[:, :64])
            totals[plane] = totals[plane] + gate * one
    for plane in range(3):
        size = min(LANES, out_ref.shape[0] - plane * LANES)
        out_ref[plane * LANES : plane * LANES + size] = totals[plane].T.astype(BF)


def gate_up_kernel(ix_ref, g_ref, w0_ref, w1_ref, w2_ref, w3_ref, out_ref):
    rows = 2 * 192
    wide = [jnp.concatenate([g_ref[y, :rows], g_ref[y, rows : 2 * rows]], axis=1) for y in range(4)]
    slim = []
    for y in range(4):
        packed = g_ref[y, 2 * rows :]
        slim.append(jnp.concatenate([packed[:, :64], packed[:, 64:]], axis=0))
    pairs = [jnp.concatenate([slim[0], slim[1]], axis=1), jnp.concatenate([slim[2], slim[3]], axis=1)]
    for s, w_ref in enumerate((w0_ref, w1_ref, w2_ref, w3_ref)):
        target = lax.rem(ix_ref[0] - s + 4, 4)

        def weight(start, size):
            return jnp.concatenate(
                [w_ref[start : start + size], w_ref[1280 + start : 1280 + start + size]], axis=1
            )

        total = dot(wide[0], weight(0, 256))
        for y in range(1, 4):
            total += dot(wide[y], weight(y * 320, 256))
        for p in range(2):
            low, high = weight(p * 640 + 256, 64), weight(p * 640 + 576, 64)
            total += dot(pairs[p], jnp.concatenate([low, high], axis=0))
        out_ref[target, :rows] = total[:, :LANES].astype(BF)
        out_ref[target, rows:] = total[:, LANES:].astype(BF)


def hidden_kernel(p_ref, out_ref):
    rows = p_ref.shape[1] // 2
    total = p_ref[0].astype(F32)
    for i in range(1, 4):
        total += p_ref[i].astype(F32)
    gate, up = total[:rows], total[rows:]
    hidden = (silu(gate) * up).astype(BF)
    for i in range(4):
        out_ref[i] = hidden


def down_kernel(ix_ref, h_ref, w0_ref, w1_ref, w2_ref, w3_ref, out_ref):
    rows = h_ref.shape[1]
    half = rows // 2
    hid = jnp.concatenate([h_ref[lax.rem(ix_ref[0] - s + 4, 4)] for s in range(4)], axis=1)
    blocks = []
    for b in range(5):
        weight = []
        for w_ref in (w0_ref, w1_ref, w2_ref, w3_ref):
            start = 2560 + b * 256
            weight.append(
                jnp.concatenate([w_ref[start : start + 128], w_ref[start + 128 : start + 256]], axis=1)
            )
        blocks.append(dot(hid, jnp.concatenate(weight, axis=0)))
    full = jnp.concatenate(blocks, axis=1)
    for y in range(4):
        own = full[:, y * 320 : (y + 1) * 320]
        out_ref[y, :rows] = own[:, :128].astype(BF)
        out_ref[y, rows : 2 * rows] = own[:, 128:256].astype(BF)
        last = own[:, 256:]
        out_ref[y, 2 * rows :] = jnp.concatenate([last[:half], last[half:]], axis=1).astype(BF)


def body(
    seq_x,
    z_gate,
    bc_in,
    conv_x,
    conv_bc,
    log_decay,
    skip_d,
    norm_gain,
    routes,
    route_gates,
    placement,
    gate_w,
    up_w,
    down_w,
):
    tokens, width = seq_x.shape
    heads = width // HEAD_DIM
    experts = placement.shape[0]
    slots = experts * PIECE
    ix = lax.axis_index("x").astype(jnp.int32)
    place = jnp.stack([lax.axis_index(NEAR), lax.axis_index("c"), lax.axis_index("zh")]).astype(jnp.int32)

    edge = kernel_call(edge_kernel, [((16, 640), BF)], seq_x.T, bc_in)
    rim = lax.ppermute(edge, CTX, [(i, i + 1) for i in range(31)])
    select, pick, half = kernel_call(
        route_kernel,
        [((slots, 4 * tokens), BF), ((6 * tokens, slots), BF), ((tokens, 2), F32)],
        routes.T,
        placement.reshape(1, experts),
    )
    ixs = ix.reshape(1)
    pieces = {s: weight_piece(lax.rem(ixs + s, 4), gate_w[0], up_w[0], down_w[0]) for s in (1, 3, 2, 0)}
    swapped = {s: lax.ppermute(pieces[s], "x", [(i, (i + s) % 4) for i in range(4)]) for s in (1, 3, 2)}
    rim, select, pick, half, held = lax.optimization_barrier((rim, select, pick, half, pieces[1]))
    xs, bcs, run, turn, message = kernel_call(
        state_kernel,
        [
            ((tokens, width), F32),
            ((tokens, 2 * STATE), F32),
            ((tokens, STATE), F32),
            ((STATE, tokens), F32),
            ((width + 16, STATE), BF),
        ],
        seq_x.T,
        bc_in,
        rim,
        conv_x,
        conv_bc,
        log_decay.T,
        scratch=[pltpu.VMEM((STATE, tokens), F32)],
    )
    near = lax.all_gather(message, NEAR)
    near, swapped[1], swapped[3] = lax.optimization_barrier((near, swapped[1], swapped[3]))
    near_carried, near_log, group = kernel_call(
        near_kernel,
        [((width, STATE), F32), ((8, STATE), F32), ((width // 2 + 16, STATE), BF)],
        place,
        near,
        scalars=1,
        scratch=[pltpu.VMEM((width, STATE), BF)],
    )
    fars = lax.all_gather(group, "zh")
    turn, group = lax.optimization_barrier((turn, group))
    y_in, z_in = pl.pallas_call(
        inner_kernel,
        out_shape=[jax.ShapeDtypeStruct((tokens, width), F32)] * 2,
        in_specs=[pl.BlockSpec(memory_space=pltpu.VMEM)] * 4
        + [pl.BlockSpec(memory_space=pltpu.SMEM), pl.BlockSpec(memory_space=pltpu.VMEM)],
        out_specs=[pl.BlockSpec(memory_space=pltpu.VMEM)] * 2,
        compiler_params=pltpu.CompilerParams(vmem_limit_bytes=32 << 20),
    )(xs, bcs, run, turn, skip_d, z_gate.T)
    far = kernel_call(far_kernel, [((width // 2, STATE), BF)], place, fars, scalars=1)
    other = lax.ppermute(far, "c", [(0, 1), (1, 0)])
    normed, outgoing = kernel_call(
        finish_kernel,
        [((width, tokens), BF), ((slots, LANES), BF)],
        place,
        far,
        other,
        near_carried,
        near_log,
        bcs,
        run,
        y_in,
        z_in,
        norm_gain.reshape(1, width),
        select,
        scalars=1,
        scratch=[pltpu.VMEM((width, STATE), BF)],
    )
    arrived = lax.all_to_all(outgoing.reshape(experts, PIECE, LANES), CTX, 0, 0, tiled=True)
    rows = (
        arrived[:, : GROUPS * HALF]
        .reshape(experts, GROUPS, HALF, LANES)
        .transpose(1, 0, 2, 3)
        .reshape(GROUPS * experts * HALF, LANES)
    )
    wide = lax.all_gather(rows, "y")
    count = 2 * experts * HALF
    weights = [pieces[0], swapped[1], swapped[2], swapped[3]]
    parts = kernel_call(gate_up_kernel, [((4, 2 * count, LANES), BF)], ixs, wide, *weights, scalars=1)
    parts = lax.all_to_all(parts, "x", 0, 0, tiled=True)
    hidden = kernel_call(hidden_kernel, [((4, count, LANES), BF)], parts)
    hiddens = lax.all_to_all(hidden, "x", 0, 0, tiled=True)
    downs = kernel_call(down_kernel, [((4, count * 5 // 2, LANES), BF)], ixs, hiddens, *weights, scalars=1)
    downs = lax.all_to_all(downs, "y", 0, 0, tiled=True)
    result = jnp.sum(downs.astype(F32), axis=0).astype(BF)
    result = result.reshape(GROUPS, experts, HALF, LANES).transpose(1, 0, 2, 3)
    result = jnp.pad(result.reshape(experts, GROUPS * HALF, LANES), ((0, 0), (0, 2), (0, 0)))
    returned = lax.all_to_all(result, CTX, 0, 0, tiled=True).reshape(slots, LANES)
    mixed = kernel_call(mix_kernel, [((width, tokens), BF)], pick, returned, route_gates.T, half)
    return (normed.T, mixed.T)


def solution(mesh):
    split = Mesh(mesh.devices.reshape(4, 4, 2, 4, 4), ("zh", "zl", "c", "x", "y"))
    placed = (
        P(CTX, EXP),
        P(CTX, EXP),
        P(CTX, None),
        P(None, EXP),
        P(),
        P(CTX, EXP),
        P(EXP),
        P(EXP),
        P(CTX, None),
        P(CTX, None),
        P(),
        P(CTX, None, EXP),
        P(CTX, None, EXP),
        P(CTX, EXP, None),
    )
    return jax.shard_map(
        body,
        mesh=split,
        in_specs=placed,
        out_specs=(P(CTX, EXP), P(CTX, EXP)),
        check_vma=False,
    )
```

time: 216 us -> 193 us (0.89)
  other arithmetic: 15.1 us -> 0.32 us
  Pallas kernels: 4.7 us -> 16.7 us
  local copies, waits for them, and re-layouts: 18.9 us -> 10.2 us
  matrix products: 7.91 us -> 0 us
  blocking collectives: 128 us -> 122 us
    all_gather x3 -> x2, blocking collectives: 55.1 us -> 39.9 us  [the longest x1 22.9 us: body(): fars = lax.all_gather(group, 'zh')]
    pallas_call x3 -> x15, Pallas kernels: 4.7 us -> 16.7 us  [the longest x10 12.8 us: kernel_call(): pl.pallas_call(kernel, out_shape=shapes, in_specs=specs, out_specs=[pl.Bl...]
    all_to_all x1 -> x2, blocking collectives: 34.5 us -> 43.9 us  [the longest x1 35.1 us: body(): lax.all_to_all(result, CTX, 0, 0, tiled=True).reshape(slots, LANES)]
    dot_general x9 -> x0, matrix products: 7.91 us -> none  [the longest x1 2.36 us: body(): jnp.einsum('btj,btl->jl', select, planes, preferred_element_type=F32)]
    concatenate x8 -> x0, other arithmetic: 5.57 us -> none  [the longest x4 4.22 us: body(): jnp.concatenate([lax.dynamic_slice_in_dim(a, start, span, 0) for a in (ga...]
    reduce_sum x7 -> x0, other arithmetic: 4.4 us -> none  [the longest x1 2.22 us: table(): planes.append(jnp.sum(jnp.where(hit, value[:, :, None], 0.0), axis=1))]
    reduce_sum x4 -> x0, local copies, waits for them, and re-layouts: 4.35 us -> none  [table(): planes.append(jnp.sum(jnp.where(hit, value[:, :, None], 0.0), axis=1))]
    unnamed x76 -> x56, local copies, waits for them, and re-layouts: 5.79 us -> 9.82 us
  transfers between devices with their start and end apart: 5 -> 6, of which waited for: 1 -> 2; matrix products, arithmetic and copies ran while one was open for 16% -> 0% of each run, Pallas kernels for 0% -> 3%
where the time goes in v2:
time: 193 us; the launch traced here: 192 us
  blocking collectives  122 us (63%)
  starting transfers between devices  25.7 us (13%)
  Pallas kernels  16.7 us (9%)
  waiting for transfers between devices  16.3 us (8%)
  local copies, waits for them, and re-layouts  10.2 us (5%)
    all_to_all x1, blocking collectives, body(): lax.all_to_all(result, CTX, 0, 0, tiled=True).reshape(slots, LANES)  35.1 us
    all_gather x1, blocking collectives, body(): fars = lax.all_gather(group, 'zh')  22.9 us
    all_gather x1, blocking collectives, body(): near = lax.all_gather(message, NEAR)  17 us
    all_to_all x1, waiting for transfers between devices, body(): lax.all_to_all(outgoing.reshape(experts, PIECE, LANES), CTX, 0, 0, tiled=...  15.2 us
    all_gather x1, blocking collectives, body(): wide = lax.all_gather(rows, 'y')  13.4 us
    pallas_call x10, Pallas kernels, kernel_call(): pl.pallas_call(kernel, out_shape=shapes, in_specs=specs, out_specs=[pl.Bl...  12.8 us
    all_to_all x1, blocking collectives, body(): parts = lax.all_to_all(parts, 'x', 0, 0, tiled=True)  12.7 us
    all_to_all x1, blocking collectives, body(): downs = lax.all_to_all(downs, 'y', 0, 0, tiled=True)  12 us
  transfers between devices with their start and end apart: 6, of which 2 were waited for; matrix products, arithmetic and copies ran while one was open for 0% of the time, Pallas kernels for 3%

profile of v2, /device:TPU:1, one launch (start us, length us, event | category | flops | bytes accessed | tf_op | source)
XLA Modules:
  0.0 192.1 jit_solution(3544132910272534159)
XLA Ops:
  0.6 1.3 copy-done
  2.0 1.3 copy-done.2
  3.3 1.3 copy-done.4
  4.7 3.9 %collective-permute-start.1 = (bf16[3840,128]{1,0:T(8,128)(2,1)S(1)}, bf16[3840,128]{1,0:T(8,128)(2,1)S(1)}, u32[]{:S(2)}, u32[]{:S(2)}) collective-permute-start(bf16[3840,128]{1,0:T(8,128)(2,1)S(1)} %shard_map.151), channel_id=1, source_target_pairs={{0,4},{4,8},{8,12},{12,0},{1,5},{5,9},{9,13},{13,1},{2,6},{6,10},{... | collective-permute-start | bytes 2949128 | tf_op jit(solution)/shard_map/ppermute | solution.py:411
  8.8 1.1 shard_map.153
  9.8 3.3 %collective-permute-start.2 = (bf16[3840,128]{1,0:T(8,128)(2,1)}, bf16[3840,128]{1,0:T(8,128)(2,1)S(1)}, u32[]{:S(2)}, u32[]{:S(2)}) collective-permute-start(bf16[3840,128]{1,0:T(8,128)(2,1)} %shard_map.153), channel_id=1, source_target_pairs={{0,12},{4,0},{8,4},{12,8},{1,13},{5,1},{9,5},{13,9},{2,14},{6,2},{... | collective-permute-start | bytes 2949128 | tf_op jit(solution)/shard_map/ppermute | solution.py:411
  13.3 4.9 %collective-permute-start = (bf16[16,640]{1,0:T(8,128)(2,1)S(1)}, bf16[16,640]{1,0:T(8,128)(2,1)S(1)}, u32[]{:S(2)}, u32[]{:S(2)}) collective-permute-start(bf16[16,640]{1,0:T(8,128)(2,1)S(1)} %shard_map.149), channel_id=1, source_target_pairs={{0,16},{16,32},{32,48},{48,64},{64,80},{80,96},{96,112},{112,128},... | collective-permute-start | bytes 61448 | tf_op jit(solution)/shard_map/ppermute | solution.py:402
  18.2 1.6 shard_map.150
  19.8 1.2 copy-done.14
  21.0 1.1 collective-permute-done.rim_ref
  22.1 1.0 shard_map.152
  23.0 17.0 %all-gather = bf16[2688,128]{1,0:T(8,128)(2,1)S(1)} all-gather(bf16[336,128]{1,0:T(8,128)(2,1)S(1)} %get-tuple-element.29), channel_id=2, replica_groups=mesh['zh'=4,'zl'=4,'c'=2,'x'=4,'y'=4] {'zl','c'}, dimensions={0}, use_global_device_ids=true | all-gather | bytes 774144 | tf_op jit(solution)/shard_map/all_gather | solution.py:430
  40.1 1.0 copy-done.11
  41.9 22.9 %all-gather.1 = bf16[704,128]{1,0:T(8,128)(2,1)S(1)} all-gather(bf16[176,128]{1,0:T(8,128)(2,1)S(1)} %get-tuple-element.31), channel_id=3, replica_groups=mesh['zh'=4,'zl'=4,'c'=2,'x'=4,'y'=4] {'zh'}, dimensions={0}, use_global_device_ids=true | all-gather | bytes 225280 | tf_op jit(solution)/shard_map/all_gather | solution.py:440
  65.4 3.5 %collective-permute-start.3 = (bf16[160,128]{1,0:T(8,128)(2,1)S(1)}, bf16[160,128]{1,0:T(8,128)(2,1)S(1)}, u32[]{:S(2)}, u32[]{:S(2)}) collective-permute-start(bf16[160,128]{1,0:T(8,128)(2,1)S(1)} %shard_map.155.own_ref), channel_id=1, source_target_pairs={{0,16},{16,0},{1,17},{17,1},{2,18},{18,2},{3,19},{19,3},{4,20},{20... | collective-permute-start | bytes 122888 | tf_op jit(solution)/shard_map/ppermute | solution.py:451
  69.0 1.5 shard_map.156
  70.5 2.6 %shard_map.157 = (bf16[320,128]{1,0:T(8,128)(2,1)}, bf16[1024,128]{1,0:T(8,128)(2,1)}) custom-call(s32[3]{0:T(128)S(1)} %pad_add_fusion.place_ref, bf16[160,128]{1,0:T(8,128)(2,1)S(1)} %shard_map.155.own_ref, bf16[160,128]{1,0:T(8,128)(2,1)S(1)} %collective-permute-done.3.other_ref, f32[320,128]{1,0:T(8,128)S(1)} %get-tuple-element.32.near_ref, ...), custom_call_target="tpu_custom_call" | custom-call | tf_op jit(solution)/shard_map/pallas_call | solution.py:32
  73.1 6.9 %all-to-all-start = ((bf16[32,32,128]{2,1,0:T(8,128)(2,1)}), bf16[32,32,128]{2,1,0:T(8,128)(2,1)S(1)}, u32[]{:S(2)}, u32[]{:S(2)}) async-start(bf16[32,32,128]{2,1,0:T(8,128)(2,1)} %bitcast.15), calls=%async_computation | async-start | bytes 524288 | tf_op jit(solution)/shard_map/all_to_all | solution.py:469
  80.0 1.3 copy-done.5
  81.3 1.1 shard_map.159
  82.4 3.2 %collective-permute-start.4 = (bf16[3840,128]{1,0:T(8,128)(2,1)}, bf16[3840,128]{1,0:T(8,128)(2,1)}, u32[]{:S(2)}, u32[]{:S(2)}) collective-permute-start(bf16[3840,128]{1,0:T(8,128)(2,1)} %shard_map.159), channel_id=1, source_target_pairs={{0,8},{4,12},{8,0},{12,4},{1,9},{5,13},{9,1},{13,5},{2,10},{6,14},... | collective-permute-start | bytes 2949128 | tf_op jit(solution)/shard_map/ppermute | solution.py:411
  85.8 0.9 copy-done.7
  86.8 15.2 %all-to-all-done = bf16[32,32,128]{2,1,0:T(8,128)(2,1)S(1)} async-done(((bf16[32,32,128]{2,1,0:T(8,128)(2,1)}), bf16[32,32,128]{2,1,0:T(8,128)(2,1)S(1)}, u32[]{:S(2)}, u32[]{:S(2)}) %all-to-all-start) | async-done | bytes 262176 | tf_op jit(solution)/shard_map/all_to_all | solution.py:469
  102.3 13.4 %all_gather.19.g_ref = bf16[4,960,128]{2,1,0:T(8,128)(2,1)S(1)} all-gather(bf16[1,960,128]{2,1,0:T(8,128)(2,1)S(1)} %all_gather_reshape.3), channel_id=1, replica_groups=mesh['zh'=4,'zl'=4,'c'=2,'x'=4,'y'=4] {'y'}, dimensions={0}, use_global_device_ids=true | all-gather | bytes 1228800 | tf_op jit(solution)/shard_map/all_gather | solution.py:476
  115.7 1.2 copy-done.12
  116.9 2.6 %shard_map.160 = bf16[4,768,128]{2,1,0:T(8,128)(2,1)S(1)} custom-call(s32[1]{0:T(128)} %bitcast.6.ix_ref, bf16[4,960,128]{2,1,0:T(8,128)(2,1)S(1)} %all_gather.19.g_ref, bf16[3840,128]{1,0:T(8,128)(2,1)S(1)} %copy-done.8, bf16[3840,128]{1,0:T(8,128)(2,1)S(1)} %copy-done.10, bf16[3840,128]{1,0:T(8,128)(2,1)} %collective-permute-done.4.w2_ref, ...), custom_call_target="tpu_custom_call" | custom-call | tf_op jit(solution)/shard_map/pallas_call | solution.py:32
  119.5 12.7 %all_to_all.25.p_ref = bf16[4,768,128]{2,1,0:T(8,128)(2,1)S(1)} all-to-all(bf16[4,768,128]{2,1,0:T(8,128)(2,1)S(1)} %shard_map.160), channel_id=1, replica_groups=mesh['zh'=4,'zl'=4,'c'=2,'x'=4,'y'=4] {'x'}, dimensions={0} | all-to-all | bytes 1572864 | tf_op jit(solution)/shard_map/all_to_all | solution.py:480
  132.3 8.8 %all_to_all.26.h_ref = bf16[4,384,128]{2,1,0:T(8,128)(2,1)S(1)} all-to-all(bf16[4,384,128]{2,1,0:T(8,128)(2,1)S(1)} %shard_map.161), channel_id=1, replica_groups=mesh['zh'=4,'zl'=4,'c'=2,'x'=4,'y'=4] {'x'}, dimensions={0} | all-to-all | bytes 786432 | tf_op jit(solution)/shard_map/all_to_all | solution.py:482
  141.1 2.0 %shard_map.162 = bf16[4,960,128]{2,1,0:T(8,128)(2,1)S(1)} custom-call(s32[1]{0:T(128)} %bitcast.6.ix_ref, bf16[4,384,128]{2,1,0:T(8,128)(2,1)S(1)} %all_to_all.26.h_ref, bf16[3840,128]{1,0:T(8,128)(2,1)S(1)} %copy-done.8, bf16[3840,128]{1,0:T(8,128)(2,1)S(1)} %copy-done.10, bf16[3840,128]{1,0:T(8,128)(2,1)} %collective-permute-done.4.w2_ref, ...), custom_call_target="tpu_custom_call" | custom-call | tf_op jit(solution)/shard_map/pallas_call | solution.py:32
  143.1 12.0 %all_to_all.27 = bf16[4,960,128]{2,1,0:T(8,128)(2,1)S(1)} all-to-all(bf16[4,960,128]{2,1,0:T(8,128)(2,1)S(1)} %shard_map.162), channel_id=1, replica_groups=mesh['zh'=4,'zl'=4,'c'=2,'x'=4,'y'=4] {'y'}, dimensions={0} | all-to-all | bytes 1966080 | tf_op jit(solution)/shard_map/all_to_all | solution.py:484
  155.6 35.1 %all_to_all.28 = bf16[32,32,128]{2,1,0:T(8,128)(2,1)S(1)} all-to-all(bf16[32,32,128]{2,1,0:T(8,128)(2,1)S(1)} %pad.4.clone), channel_id=1, replica_groups=mesh['zh'=4,'zl'=4,'c'=2,'x'=4,'y'=4] {'zh','zl','c'}, dimensions={0} | all-to-all | bytes 524288 | tf_op jit(solution)/shard_map/all_to_all | solution.py:488
  190.7 1.4 shard_map.163
  (66 shorter events, 3.0 us)
Async XLA Ops:
  0.6 1.3 copy-start
  2.0 1.3 copy-start.2
  3.3 1.3 copy-start.4
  4.7 35.3 %collective-permute-start.1 = (bf16[3840,128]{1,0:T(8,128)(2,1)S(1)}, bf16[3840,128]{1,0:T(8,128)(2,1)S(1)}, u32[]{:S(2)}, u32[]{:S(2)}) collective-permute-start(bf16[3840,128]{1,0:T(8,128)(2,1)S(1)} %shard_map.151), channel_id=1, source_target_pairs={{0,4},{4,8},{8,12},{12,0},{1,5},{5,9},{9,13},{13,1},{2,6},{6,10},{... | collective-permute-start | bytes 2949128 | tf_op jit(solution)/shard_map/ppermute | solution.py:411
  8.7 4.5 %copy-start.16 = (bf16[128,320]{0,1:T(8,128)(2,1)S(1)}, bf16[128,320]{0,1:T(8,128)(2,1)}, u32[]{:S(2)}) copy-start(bf16[128,320]{0,1:T(8,128)(2,1)} %param.14) | copy-start | bytes 245764
  8.7 4.5 %copy-start.17 = (bf16[128,256]{1,0:T(8,128)(2,1)S(1)}, bf16[128,256]{1,0:T(8,128)(2,1)}, u32[]{:S(2)}) copy-start(bf16[128,256]{1,0:T(8,128)(2,1)} %bc_ref.3) | copy-start | bytes 196612
  8.7 9.5 %copy-start.24 = (s32[128,2]{0,1:T(2,128)S(1)}, s32[128,2]{0,1:T(2,128)}, u32[]{:S(2)}) copy-start(s32[128,2]{0,1:T(2,128)} %param.22) | copy-start | bytes 3076
  8.7 9.5 %copy-start.25 = (s32[32]{0:T(128)S(1)}, s32[32]{0:T(128)}, u32[]{:S(2)}) copy-start(s32[32]{0:T(128)} %param.24) | copy-start | bytes 388
  8.7 13.3 %copy-start.19 = (f32[4,320]{1,0:T(4,128)S(1)}, f32[4,320]{1,0:T(4,128)}, u32[]{:S(2)}) copy-start(f32[4,320]{1,0:T(4,128)} %cx_ref.1) | copy-start | bytes 15364
  8.7 13.3 %copy-start.20 = (f32[4,256]{1,0:T(4,128)S(1)}, f32[4,256]{1,0:T(4,128)}, u32[]{:S(2)}) copy-start(f32[4,256]{1,0:T(4,128)} %cbc_ref.1) | copy-start | bytes 12292
  8.7 13.3 %copy-start.21 = (f32[128,5]{0,1:T(8,128)S(1)}, f32[128,5]{0,1:T(8,128)}, u32[]{:S(2)}) copy-start(f32[128,5]{0,1:T(8,128)} %param.19) | copy-start | bytes 7684
  9.8 59.1 %copy-start.26 = (f32[320]{0:T(512)S(1)}, f32[320]{0:T(512)}, u32[]{:S(2)}) copy-start(f32[320]{0:T(512)} %param.21) | copy-start | bytes 3844
  9.8 59.1 %copy-start.18 = (bf16[128,320]{0,1:T(8,128)(2,1)S(1)}, bf16[128,320]{0,1:T(8,128)(2,1)}, u32[]{:S(2)}) copy-start(bf16[128,320]{0,1:T(8,128)(2,1)} %param.15) | copy-start | bytes 245764
  9.8 59.1 %copy-start.23 = (f32[5]{0:T(128)S(1)}, f32[5]{0:T(128)}, u32[]{:S(2)}) copy-start(f32[5]{0:T(128)} %skip_ref.1) | copy-start | bytes 64
  9.8 30.2 %collective-permute-start.2 = (bf16[3840,128]{1,0:T(8,128)(2,1)}, bf16[3840,128]{1,0:T(8,128)(2,1)S(1)}, u32[]{:S(2)}, u32[]{:S(2)}) collective-permute-start(bf16[3840,128]{1,0:T(8,128)(2,1)} %shard_map.153), channel_id=1, source_target_pairs={{0,12},{4,0},{8,4},{12,8},{1,13},{5,1},{9,5},{13,9},{2,14},{6,2},{... | collective-permute-start | bytes 2949128 | tf_op jit(solution)/shard_map/ppermute | solution.py:411
  13.3 8.8 %collective-permute-start = (bf16[16,640]{1,0:T(8,128)(2,1)S(1)}, bf16[16,640]{1,0:T(8,128)(2,1)S(1)}, u32[]{:S(2)}, u32[]{:S(2)}) collective-permute-start(bf16[16,640]{1,0:T(8,128)(2,1)S(1)} %shard_map.149), channel_id=1, source_target_pairs={{0,16},{16,32},{32,48},{48,64},{64,80},{80,96},{96,112},{112,128},... | collective-permute-start | bytes 61448 | tf_op jit(solution)/shard_map/ppermute | solution.py:402
  19.8 1.2 copy-start.14
  40.0 28.9 %copy-start.9 = (bf16[3840,128]{1,0:T(8,128)(2,1)}, bf16[3840,128]{1,0:T(8,128)(2,1)S(1)}, u32[]{:S(2)}) copy-start(bf16[3840,128]{1,0:T(8,128)(2,1)S(1)} %collective-permute-done.1.w1_ref) | copy-start | bytes 2949124
  40.0 1.0 copy-start.11
  65.4 5.1 %collective-permute-start.3 = (bf16[160,128]{1,0:T(8,128)(2,1)S(1)}, bf16[160,128]{1,0:T(8,128)(2,1)S(1)}, u32[]{:S(2)}, u32[]{:S(2)}) collective-permute-start(bf16[160,128]{1,0:T(8,128)(2,1)S(1)} %shard_map.155.own_ref), channel_id=1, source_target_pairs={{0,16},{16,0},{1,17},{17,1},{2,18},{18,2},{3,19},{19,3},{4,20},{20... | collective-permute-start | bytes 122888 | tf_op jit(solution)/shard_map/ppermute | solution.py:451
  69.0 11.0 %copy-start.3 = (bf16[1,5120,128]{2,1,0:T(8,128)(2,1)S(1)}, bf16[1,5120,128]{2,1,0:T(8,128)(2,1)}, u32[]{:S(2)}) copy-start(bf16[1,5120,128]{2,1,0:T(8,128)(2,1)} %param.26) | copy-start | bytes 3932164
  70.5 9.6 %copy-start.1 = (bf16[1,5120,128]{2,1,0:T(8,128)(2,1)S(1)}, bf16[1,5120,128]{2,1,0:T(8,128)(2,1)}, u32[]{:S(2)}) copy-start(bf16[1,5120,128]{2,1,0:T(8,128)(2,1)} %param.25) | copy-start | bytes 3932164
  73.1 28.9 %all-to-all-start = ((bf16[32,32,128]{2,1,0:T(8,128)(2,1)}), bf16[32,32,128]{2,1,0:T(8,128)(2,1)S(1)}, u32[]{:S(2)}, u32[]{:S(2)}) async-start(bf16[32,32,128]{2,1,0:T(8,128)(2,1)} %bitcast.15), calls=%async_computation | async-start | bytes 524288 | tf_op jit(solution)/shard_map/all_to_all | solution.py:469
  80.0 1.3 copy-start.5
  81.3 4.3 %copy-start.6 = (bf16[1,128,5120]{2,1,0:T(8,128)(2,1)S(1)}, bf16[1,128,5120]{2,1,0:T(8,128)(2,1)}, u32[]{:S(2)}) copy-start(bf16[1,128,5120]{2,1,0:T(8,128)(2,1)} %param.27) | copy-start | bytes 3932164
  82.4 33.3 %collective-permute-start.4 = (bf16[3840,128]{1,0:T(8,128)(2,1)}, bf16[3840,128]{1,0:T(8,128)(2,1)}, u32[]{:S(2)}, u32[]{:S(2)}) collective-permute-start(bf16[3840,128]{1,0:T(8,128)(2,1)} %shard_map.159), channel_id=1, source_target_pairs={{0,8},{4,12},{8,0},{12,4},{1,9},{5,13},{9,1},{13,5},{2,10},{6,14},... | collective-permute-start | bytes 2949128 | tf_op jit(solution)/shard_map/ppermute | solution.py:411
  102.1 13.6 %copy-start.8 = (bf16[3840,128]{1,0:T(8,128)(2,1)S(1)}, bf16[3840,128]{1,0:T(8,128)(2,1)}, u32[]{:S(2)}) copy-start(bf16[3840,128]{1,0:T(8,128)(2,1)} %copy-done.7) | copy-start | bytes 2949124
  102.1 13.6 %copy-start.10 = (bf16[3840,128]{1,0:T(8,128)(2,1)S(1)}, bf16[3840,128]{1,0:T(8,128)(2,1)}, u32[]{:S(2)}) copy-start(bf16[3840,128]{1,0:T(8,128)(2,1)} %copy-done.9) | copy-start | bytes 2949124
  115.7 1.2 copy-start.12
  132.2 8.9 %copy-start.13 = (bf16[3840,128]{1,0:T(8,128)(2,1)S(1)}, bf16[3840,128]{1,0:T(8,128)(2,1)}, u32[]{:S(2)}) copy-start(bf16[3840,128]{1,0:T(8,128)(2,1)} %copy-done.11) | copy-start | bytes 2949124
  155.3 35.4 %copy-start.15 = (bf16[768,1024]{1,0:T(8,128)(2,1)S(1)}, bf16[768,1024]{1,0:T(8,128)(2,1)}, u32[]{:S(2)}) copy-start(bf16[768,1024]{1,0:T(8,128)(2,1)} %copy-done.14) | copy-start | bytes 4718596
  155.3 35.4 %copy-start.22 = (f32[128,2]{0,1:T(2,128)S(1)}, f32[128,2]{0,1:T(2,128)}, u32[]{:S(2)}) copy-start(f32[128,2]{0,1:T(2,128)} %param.23) | copy-start | bytes 3076
  (1 other events, 0.9 us)

commit v3 on v2

--- a/solution.py
+++ b/solution.py
@@ -1,3 +1,5 @@
+import functools
+
 import jax
 import jax.numpy as jnp
 from jax import lax
@@ -35,7 +37,7 @@
         in_specs=specs,
         out_specs=[pl.BlockSpec(memory_space=pltpu.VMEM)] * len(outs),
         scratch_shapes=list(scratch),
-        compiler_params=pltpu.CompilerParams(vmem_limit_bytes=48 << 20),
+        compiler_params=pltpu.CompilerParams(vmem_limit_bytes=20 << 20),
     )(*operands)
     return result[0] if len(outs) == 1 else result
 
@@ -69,7 +71,7 @@
     out_ref[:, 384:] = bc_ref[rows - 16 :]
 
 
-def route_kernel(routes_ref, row_ref, select_ref, pick_ref, half_ref):
+def pick_kernel(routes_ref, row_ref, pick_ref, half_ref):
     tokens = routes_ref.shape[1]
     experts = row_ref.shape[1]
     slots = experts * PIECE
@@ -89,6 +91,12 @@
         for plane, where in enumerate((base + HALF * half, base + HALF * (half + 2), base + 4 * HALF)):
             start = (plane * 2 + k) * tokens
             pick_ref[start : start + tokens] = (places == where).astype(F32).astype(BF)
+
+
+def select_kernel(routes_ref, row_ref, select_ref):
+    tokens = routes_ref.shape[1]
+    experts = row_ref.shape[1]
+    slots = experts * PIECE
     hot = [(routes_ref[k : k + 1] == iota((experts, tokens), 0)).astype(F32) for k in range(2)]
     later = (iota((tokens, tokens), 0) < iota((tokens, tokens), 1)).astype(BF)
     before = dot((hot[0] + hot[1]).astype(BF), later)
@@ -271,32 +279,55 @@
     out_ref[...] = dot(select_ref[...], planes).astype(BF)
 
 
-def piece_kernel(block_ref, gate_ref, up_ref, down_ref, out_ref):
-    span = gate_ref.shape[0]
-    out_ref[:span] = gate_ref[...]
-    out_ref[span : 2 * span] = up_ref[...]
-    for b in range(span // LANES):
-        start = 2 * span + b * LANES
-        out_ref[start : start + LANES] = down_ref[:, b * LANES : (b + 1) * LANES]
-
-
-def weight_piece(block, gate, up, down):
+def piece_kernel(steps, ix_ref, gate_ref, up_ref, down_ref, *rest):
+    outs, (held, in_sems, out_sems) = rest[: len(steps)], rest[len(steps) :]
+    span = gate_ref.shape[0] // 4
+    arrivals = []
+    for i, step in enumerate(steps):
+        block = pl.multiple_of(lax.rem(ix_ref[0] + step, 4) * span, span)
+        pairs = [
+            (gate_ref.at[pl.ds(block, span)], held.at[i, pl.ds(0, span)]),
+            (up_ref.at[pl.ds(block, span)], held.at[i, pl.ds(span, span)]),
+        ]
+        for b in range(span // LANES):
+            pairs.append(
+                (
+                    down_ref.at[:, pl.ds(pl.multiple_of(block + b * LANES, LANES), LANES)],
+                    held.at[i, pl.ds(2 * span + b * LANES, LANES)],
+                )
+            )
+        arrivals.append(
+            [pltpu.make_async_copy(p, q, in_sems.at[i, n]) for n, (p, q) in enumerate(pairs)]
+        )
+    for copies in arrivals:
+        for copy in copies:
+            copy.start()
+    departures = []
+    for i, copies in enumerate(arrivals):
+        for copy in copies:
+            copy.wait()
+        departures.append(pltpu.make_async_copy(held.at[i], outs[i], out_sems.at[i]))
+        departures[i].start()
+    for copy in departures:
+        copy.wait()
+
+
+def weight_pieces(steps, ix, gate, up, down):
     span = gate.shape[0] // 4
+    count = len(steps)
+    whole = pl.BlockSpec(memory_space=pltpu.HBM)
     return pl.pallas_call(
-        piece_kernel,
-        out_shape=jax.ShapeDtypeStruct((3 * span, LANES), BF),
-        grid_spec=pltpu.PrefetchScalarGridSpec(
-            num_scalar_prefetch=1,
-            grid=(1,),
-            in_specs=[
-                pl.BlockSpec((span, LANES), lambda i, b: (b[0], 0)),
-                pl.BlockSpec((span, LANES), lambda i, b: (b[0], 0)),
-                pl.BlockSpec((LANES, span), lambda i, b: (0, b[0])),
-            ],
-            out_specs=pl.BlockSpec((3 * span, LANES), lambda i, b: (0, 0)),
-        ),
-        compiler_params=pltpu.CompilerParams(vmem_limit_bytes=32 << 20),
-    )(block, gate, up, down)
+        functools.partial(piece_kernel, steps),
+        out_shape=[jax.ShapeDtypeStruct((3 * span, LANES), BF)] * count,
+        in_specs=[pl.BlockSpec(memory_space=pltpu.SMEM), whole, whole, whole],
+        out_specs=[whole] * count,
+        scratch_shapes=[
+            pltpu.VMEM((count, 3 * span, LANES), BF),
+            pltpu.SemaphoreType.DMA((count, 2 + span // LANES)),
+            pltpu.SemaphoreType.DMA((count,)),
+        ],
+        compiler_params=pltpu.CompilerParams(vmem_limit_bytes=60 << 20),
+    )(ix, gate, up, down)
 
 
 def mix_kernel(pick_ref, rows_ref, gates_ref, half_ref, out_ref):
@@ -400,16 +431,10 @@
 
     edge = kernel_call(edge_kernel, [((16, 640), BF)], seq_x.T, bc_in)
     rim = lax.ppermute(edge, CTX, [(i, i + 1) for i in range(31)])
-    select, pick, half = kernel_call(
-        route_kernel,
-        [((slots, 4 * tokens), BF), ((6 * tokens, slots), BF), ((tokens, 2), F32)],
-        routes.T,
-        placement.reshape(1, experts),
-    )
     ixs = ix.reshape(1)
-    pieces = {s: weight_piece(lax.rem(ixs + s, 4), gate_w[0], up_w[0], down_w[0]) for s in (1, 3, 2, 0)}
-    swapped = {s: lax.ppermute(pieces[s], "x", [(i, (i + s) % 4) for i in range(4)]) for s in (1, 3, 2)}
-    rim, select, pick, half, held = lax.optimization_barrier((rim, select, pick, half, pieces[1]))
+    own = (gate_w[0], up_w[0], down_w[0])
+    pieces = dict(zip((1, 3, 2, 0), weight_pieces((1, 3, 2, 0), ixs, *own)))
+    swapped = {s: lax.ppermute(pieces[s], "x", [(i, (i + s) % 4) for i in range(4)]) for s in (1, 3)}
     xs, bcs, run, turn, message = kernel_call(
         state_kernel,
         [
@@ -438,14 +463,17 @@
         scratch=[pltpu.VMEM((width, STATE), BF)],
     )
     fars = lax.all_gather(group, "zh")
-    turn, group = lax.optimization_barrier((turn, group))
+    turn, group, *owned = lax.optimization_barrier((turn, group, routes, placement))
+    select = kernel_call(
+        select_kernel, [((slots, 4 * tokens), BF)], owned[0].T, owned[1].reshape(1, experts)
+    )
     y_in, z_in = pl.pallas_call(
         inner_kernel,
         out_shape=[jax.ShapeDtypeStruct((tokens, width), F32)] * 2,
         in_specs=[pl.BlockSpec(memory_space=pltpu.VMEM)] * 4
         + [pl.BlockSpec(memory_space=pltpu.SMEM), pl.BlockSpec(memory_space=pltpu.VMEM)],
         out_specs=[pl.BlockSpec(memory_space=pltpu.VMEM)] * 2,
-        compiler_params=pltpu.CompilerParams(vmem_limit_bytes=32 << 20),
+        compiler_params=pltpu.CompilerParams(vmem_limit_bytes=20 << 20),
     )(xs, bcs, run, turn, skip_d, z_gate.T)
     far = kernel_call(far_kernel, [((width // 2, STATE), BF)], place, fars, scalars=1)
     other = lax.ppermute(far, "c", [(0, 1), (1, 0)])
@@ -466,6 +494,14 @@
         scalars=1,
         scratch=[pltpu.VMEM((width, STATE), BF)],
     )
+    normed, *own = lax.optimization_barrier((normed, routes, placement))
+    swapped[2] = lax.ppermute(pieces[2], "x", [(i, (i + 2) % 4) for i in range(4)])
+    pick, half = kernel_call(
+        pick_kernel,
+        [((6 * tokens, slots), BF), ((tokens, 2), F32)],
+        own[0].T,
+        own[1].reshape(1, experts),
+    )
     arrived = lax.all_to_all(outgoing.reshape(experts, PIECE, LANES), CTX, 0, 0, tiled=True)
     rows = (
         arrived[:, : GROUPS * HALF]

time: 193 us -> 189 us (0.979)
  blocking collectives: 122 us -> 86 us
  waiting for transfers between devices: 16.3 us -> 43.4 us
  starting transfers between devices: 25.7 us -> 37.8 us
  local copies, waits for them, and re-layouts: 10.2 us -> 1.33 us
    all_to_all x1 -> x0, blocking collectives: 35.1 us -> none  [body(): lax.all_to_all(result, CTX, 0, 0, tiled=True).reshape(slots, LANES)]
    all_to_all x0 -> x1, waiting for transfers between devices: none -> 21.4 us  [body(): lax.all_to_all(result, CTX, 0, 0, tiled=True).reshape(slots, LANES)]
    all_to_all x0 -> x1, starting transfers between devices: none -> 10.6 us  [body(): lax.all_to_all(result, CTX, 0, 0, tiled=True).reshape(slots, LANES)]
    unnamed x56 -> x26, local copies, waits for them, and re-layouts: 9.82 us -> 0.26 us
    ppermute x0 -> x1, starting transfers between devices: none -> 3.76 us  [body(): lax.ppermute(pieces[2], 'x', [(i, (i + 2) % 4) for i in range(4)])]
    ppermute x3 -> x2, starting transfers between devices: 10.5 us -> 7.27 us  [body(): lax.ppermute(pieces[s], 'x', [(i, (i + s) % 4) for i in range(4)])]
    all_to_all x1, waiting for transfers between devices: 15.2 us -> 18.2 us  [body(): lax.all_to_all(outgoing.reshape(experts, PIECE, LANES), CTX, 0, 0, tiled=...]
    ppermute x1, waiting for transfers between devices: 1.05 us -> 3.81 us  [body(): rim = lax.ppermute(edge, CTX, [(i, i + 1) for i in range(31)])]
  transfers between devices with their start and end apart: 6 -> 7, of which waited for: 2 -> 3; matrix products, arithmetic and copies ran while one was open for 0% -> 0% of each run, Pallas kernels for 3% -> 2%
where the time goes in v3:
time: 189 us; the launch traced here: 188 us
  blocking collectives  86 us (46%)
  waiting for transfers between devices  43.4 us (23%)
  starting transfers between devices  37.8 us (20%)
  Pallas kernels  18.2 us (10%)
    all_gather x1, blocking collectives, body(): fars = lax.all_gather(group, 'zh')  23.6 us
    all_to_all x1, waiting for transfers between devices, body(): lax.all_to_all(result, CTX, 0, 0, tiled=True).reshape(slots, LANES)  21.4 us
    all_to_all x1, waiting for transfers between devices, body(): lax.all_to_all(outgoing.reshape(experts, PIECE, LANES), CTX, 0, 0, tiled=...  18.2 us
    all_gather x1, blocking collectives, body(): near = lax.all_gather(message, NEAR)  15.4 us
    all_gather x1, blocking collectives, body(): wide = lax.all_gather(rows, 'y')  13.7 us
    pallas_call x11, Pallas kernels, kernel_call(): pl.pallas_call(kernel, out_shape=shapes, in_specs=specs, out_specs=[pl.Bl...  13 us
    all_to_all x1, blocking collectives, body(): parts = lax.all_to_all(parts, 'x', 0, 0, tiled=True)  12.9 us
    all_to_all x1, blocking collectives, body(): downs = lax.all_to_all(downs, 'y', 0, 0, tiled=True)  11.8 us
  transfers between devices with their start and end apart: 7, of which 3 were waited for; matrix products, arithmetic and copies ran while one was open for 0% of the time, Pallas kernels for 2%

profile of v3, /device:TPU:1, one launch (start us, length us, event | category | flops | bytes accessed | tf_op | source)
XLA Modules:
  0.0 188.1 jit_solution(12013070615147850546)
XLA Ops:
  0.7 3.7 %shard_map.151 = (bf16[3840,128]{1,0:T(8,128)(2,1)}, bf16[3840,128]{1,0:T(8,128)(2,1)}, bf16[3840,128]{1,0:T(8,128)(2,1)}, bf16[3840,128]{1,0:T(8,128)(2,1)}) custom-call(s32[1]{0:T(128)} %bitcast.6.ix_ref, bf16[5120,128]{1,0:T(8,128)(2,1)} %bitcast.39, bf16[5120,128]{1,0:T(8,128)(2,1)} %bitcast.40, bf16[128,5120]{1,0:T(8,128)(2,1)} %bitcast.41), custom_call_target="tpu_custom_call" | custom-call | tf_op jit(solution)/shard_map/pallas_call | solution.py:319
  4.5 4.1 %collective-permute-start.1 = (bf16[3840,128]{1,0:T(8,128)(2,1)}, bf16[3840,128]{1,0:T(8,128)(2,1)S(1)}, u32[]{:S(2)}, u32[]{:S(2)}) collective-permute-start(bf16[3840,128]{1,0:T(8,128)(2,1)} %get-tuple-element.30), channel_id=1, source_target_pairs={{0,4},{4,8},{8,12},{12,0},{1,5},{5,9},{9,13},{13,1},{2,6},{6,10},{... | collective-permute-start | bytes 2949128 | tf_op jit(solution)/shard_map/ppermute | solution.py:437
  8.6 3.2 %collective-permute-start.2 = (bf16[3840,128]{1,0:T(8,128)(2,1)}, bf16[3840,128]{1,0:T(8,128)(2,1)S(1)}, u32[]{:S(2)}, u32[]{:S(2)}) collective-permute-start(bf16[3840,128]{1,0:T(8,128)(2,1)} %get-tuple-element.31), channel_id=1, source_target_pairs={{0,12},{4,0},{8,4},{12,8},{1,13},{5,1},{9,5},{13,9},{2,14},{6,2},{... | collective-permute-start | bytes 2949128 | tf_op jit(solution)/shard_map/ppermute | solution.py:437
  11.9 4.9 %collective-permute-start = (bf16[16,640]{1,0:T(8,128)(2,1)S(1)}, bf16[16,640]{1,0:T(8,128)(2,1)S(1)}, u32[]{:S(2)}, u32[]{:S(2)}) collective-permute-start(bf16[16,640]{1,0:T(8,128)(2,1)S(1)} %shard_map.149), channel_id=1, source_target_pairs={{0,16},{16,32},{32,48},{48,64},{64,80},{80,96},{96,112},{112,128},... | collective-permute-start | bytes 61448 | tf_op jit(solution)/shard_map/ppermute | solution.py:433
  16.8 3.8 %collective-permute-done.rim_ref = bf16[16,640]{1,0:T(8,128)(2,1)S(1)} collective-permute-done((bf16[16,640]{1,0:T(8,128)(2,1)S(1)}, bf16[16,640]{1,0:T(8,128)(2,1)S(1)}, u32[]{:S(2)}, u32[]{:S(2)}) %collective-permute-start) | collective-permute-done | bytes 20512 | tf_op jit(solution)/shard_map/ppermute | solution.py:433
  20.6 1.0 shard_map.150
  21.6 15.4 %all-gather = bf16[2688,128]{1,0:T(8,128)(2,1)S(1)} all-gather(bf16[336,128]{1,0:T(8,128)(2,1)S(1)} %get-tuple-element.29), channel_id=2, replica_groups=mesh['zh'=4,'zl'=4,'c'=2,'x'=4,'y'=4] {'zl','c'}, dimensions={0}, use_global_device_ids=true | all-gather | bytes 774144 | tf_op jit(solution)/shard_map/all_gather | solution.py:455
  37.0 0.8 shard_map.152
  37.9 23.6 %all-gather.1 = bf16[704,128]{1,0:T(8,128)(2,1)S(1)} all-gather(bf16[176,128]{1,0:T(8,128)(2,1)S(1)} %get-tuple-element.33), channel_id=3, replica_groups=mesh['zh'=4,'zl'=4,'c'=2,'x'=4,'y'=4] {'zh'}, dimensions={0}, use_global_device_ids=true | all-gather | bytes 225280 | tf_op jit(solution)/shard_map/all_gather | solution.py:465
  61.5 0.7 shard_map.153.own_ref
  62.1 4.4 %collective-permute-start.3 = (bf16[160,128]{1,0:T(8,128)(2,1)S(1)}, bf16[160,128]{1,0:T(8,128)(2,1)S(1)}, u32[]{:S(2)}, u32[]{:S(2)}) collective-permute-start(bf16[160,128]{1,0:T(8,128)(2,1)S(1)} %shard_map.153.own_ref), channel_id=1, source_target_pairs={{0,16},{16,0},{1,17},{17,1},{2,18},{18,2},{3,19},{19,3},{4,20},{20... | collective-permute-start | bytes 122888 | tf_op jit(solution)/shard_map/ppermute | solution.py:479
  66.6 1.1 shard_map.155.select_ref
  67.7 1.5 shard_map.154
  69.2 2.6 %shard_map.156 = (bf16[320,128]{1,0:T(8,128)(2,1)}, bf16[1024,128]{1,0:T(8,128)(2,1)}) custom-call(s32[3]{0:T(128)S(1)} %pad_add_fusion.place_ref, bf16[160,128]{1,0:T(8,128)(2,1)S(1)} %shard_map.153.own_ref, bf16[160,128]{1,0:T(8,128)(2,1)S(1)} %collective-permute-done.3.other_ref, f32[320,128]{1,0:T(8,128)S(1)} %get-tuple-element.34.near_ref, ...), custom_call_target="tpu_custom_call" | custom-call | tf_op jit(solution)/shard_map/pallas_call | solution.py:34
  71.8 6.9 %all-to-all-start = ((bf16[32,32,128]{2,1,0:T(8,128)(2,1)}), bf16[32,32,128]{2,1,0:T(8,128)(2,1)S(1)}, u32[]{:S(2)}, u32[]{:S(2)}) async-start(bf16[32,32,128]{2,1,0:T(8,128)(2,1)} %bitcast.17), calls=%async_computation | async-start | bytes 524288 | tf_op jit(solution)/shard_map/all_to_all | solution.py:505
  78.7 3.8 %collective-permute-start.4 = (bf16[3840,128]{1,0:T(8,128)(2,1)}, bf16[3840,128]{1,0:T(8,128)(2,1)}, u32[]{:S(2)}, u32[]{:S(2)}) collective-permute-start(bf16[3840,128]{1,0:T(8,128)(2,1)} %get-tuple-element.53), channel_id=1, source_target_pairs={{0,8},{4,12},{8,0},{12,4},{1,9},{5,13},{9,1},{13,5},{2,10},{6,14},... | collective-permute-start | bytes 2949128 | tf_op jit(solution)/shard_map/ppermute | solution.py:498
  82.5 18.2 %all-to-all-done = bf16[32,32,128]{2,1,0:T(8,128)(2,1)S(1)} async-done(((bf16[32,32,128]{2,1,0:T(8,128)(2,1)}), bf16[32,32,128]{2,1,0:T(8,128)(2,1)S(1)}, u32[]{:S(2)}, u32[]{:S(2)}) %all-to-all-start) | async-done | bytes 262176 | tf_op jit(solution)/shard_map/all_to_all | solution.py:505
  100.8 0.1 copy.21
  101.0 13.7 %all_gather.19.g_ref = bf16[4,960,128]{2,1,0:T(8,128)(2,1)S(1)} all-gather(bf16[1,960,128]{2,1,0:T(8,128)(2,1)S(1)} %all_gather_reshape.3), channel_id=1, replica_groups=mesh['zh'=4,'zl'=4,'c'=2,'x'=4,'y'=4] {'y'}, dimensions={0}, use_global_device_ids=true | all-gather | bytes 1228800 | tf_op jit(solution)/shard_map/all_gather | solution.py:512
  114.7 2.6 %shard_map.158 = bf16[4,768,128]{2,1,0:T(8,128)(2,1)S(1)} custom-call(s32[1]{0:T(128)} %bitcast.6.ix_ref, bf16[4,960,128]{2,1,0:T(8,128)(2,1)S(1)} %all_gather.19.g_ref, bf16[3840,128]{1,0:T(8,128)(2,1)S(1)} %copy-done, bf16[3840,128]{1,0:T(8,128)(2,1)S(1)} %collective-permute-done.1.w1_ref, bf16[3840,128]{1,0:T(8,128)(2,1)} %collective-permute-done.4.w2_ref, ...), custom_call_target="tpu_custom_call" | custom-call | tf_op jit(solution)/shard_map/pallas_call | solution.py:34
  117.3 12.9 %all_to_all.25.p_ref = bf16[4,768,128]{2,1,0:T(8,128)(2,1)S(1)} all-to-all(bf16[4,768,128]{2,1,0:T(8,128)(2,1)S(1)} %shard_map.158), channel_id=1, replica_groups=mesh['zh'=4,'zl'=4,'c'=2,'x'=4,'y'=4] {'x'}, dimensions={0} | all-to-all | bytes 1572864 | tf_op jit(solution)/shard_map/all_to_all | solution.py:516
  130.3 0.1 shard_map.159
  130.4 8.6 %all_to_all.26.h_ref = bf16[4,384,128]{2,1,0:T(8,128)(2,1)S(1)} all-to-all(bf16[4,384,128]{2,1,0:T(8,128)(2,1)S(1)} %shard_map.159), channel_id=1, replica_groups=mesh['zh'=4,'zl'=4,'c'=2,'x'=4,'y'=4] {'x'}, dimensions={0} | all-to-all | bytes 786432 | tf_op jit(solution)/shard_map/all_to_all | solution.py:518
  139.0 2.0 %shard_map.160 = bf16[4,960,128]{2,1,0:T(8,128)(2,1)S(1)} custom-call(s32[1]{0:T(128)} %bitcast.6.ix_ref, bf16[4,384,128]{2,1,0:T(8,128)(2,1)S(1)} %all_to_all.26.h_ref, bf16[3840,128]{1,0:T(8,128)(2,1)S(1)} %copy-done, bf16[3840,128]{1,0:T(8,128)(2,1)S(1)} %collective-permute-done.1.w1_ref, bf16[3840,128]{1,0:T(8,128)(2,1)} %collective-permute-done.4.w2_ref, ...), custom_call_target="tpu_custom_call" | custom-call | tf_op jit(solution)/shard_map/pallas_call | solution.py:34
  141.0 11.8 %all_to_all.27 = bf16[4,960,128]{2,1,0:T(8,128)(2,1)S(1)} all-to-all(bf16[4,960,128]{2,1,0:T(8,128)(2,1)S(1)} %shard_map.160), channel_id=1, replica_groups=mesh['zh'=4,'zl'=4,'c'=2,'x'=4,'y'=4] {'y'}, dimensions={0} | all-to-all | bytes 1966080 | tf_op jit(solution)/shard_map/all_to_all | solution.py:520
  152.8 0.2 reduce_sum.12
  153.2 0.1 copy.25
  153.3 0.8 pad.4.clone
  154.1 10.6 %all-to-all-start.4 = ((bf16[32,32,128]{2,1,0:T(8,128)(2,1)}), bf16[32,32,128]{2,1,0:T(8,128)(2,1)S(1)}, u32[]{:S(2)}, u32[]{:S(2)}) async-start(bf16[32,32,128]{2,1,0:T(8,128)(2,1)} %pad.4.clone), calls=%async_computation.4 | async-start | bytes 524288 | tf_op jit(solution)/shard_map/all_to_all | solution.py:524
  164.7 0.6 shard_map.157
  165.3 21.4 %all-to-all-done.4 = bf16[32,32,128]{2,1,0:T(8,128)(2,1)S(1)} async-done(((bf16[32,32,128]{2,1,0:T(8,128)(2,1)}), bf16[32,32,128]{2,1,0:T(8,128)(2,1)S(1)}, u32[]{:S(2)}, u32[]{:S(2)}) %all-to-all-start.4) | async-done | bytes 262176 | tf_op jit(solution)/shard_map/all_to_all | solution.py:524
  186.7 1.4 shard_map.161
  (35 shorter events, 0.6 us)
Async XLA Ops:
  0.6 11.1 %copy-start.1 = (bf16[128,320]{0,1:T(8,128)(2,1)S(1)}, bf16[128,320]{0,1:T(8,128)(2,1)}, u32[]{:S(2)}) copy-start(bf16[128,320]{0,1:T(8,128)(2,1)} %param.14) | copy-start | bytes 245764
  0.6 11.1 %copy-start.2 = (bf16[128,256]{1,0:T(8,128)(2,1)S(1)}, bf16[128,256]{1,0:T(8,128)(2,1)}, u32[]{:S(2)}) copy-start(bf16[128,256]{1,0:T(8,128)(2,1)} %bc_ref.3) | copy-start | bytes 196612
  0.7 20.0 %copy-start.4 = (f32[4,320]{1,0:T(4,128)S(1)}, f32[4,320]{1,0:T(4,128)}, u32[]{:S(2)}) copy-start(f32[4,320]{1,0:T(4,128)} %cx_ref.1) | copy-start | bytes 15364
  0.7 20.0 %copy-start.5 = (f32[4,256]{1,0:T(4,128)S(1)}, f32[4,256]{1,0:T(4,128)}, u32[]{:S(2)}) copy-start(f32[4,256]{1,0:T(4,128)} %cbc_ref.1) | copy-start | bytes 12292
  0.7 20.0 %copy-start.6 = (f32[128,5]{0,1:T(8,128)S(1)}, f32[128,5]{0,1:T(8,128)}, u32[]{:S(2)}) copy-start(f32[128,5]{0,1:T(8,128)} %param.19) | copy-start | bytes 7684
  4.4 62.1 %copy-start.11 = (f32[320]{0:T(512)S(1)}, f32[320]{0:T(512)}, u32[]{:S(2)}) copy-start(f32[320]{0:T(512)} %param.21) | copy-start | bytes 3844
  4.5 62.1 %copy-start.8 = (s32[128,2]{0,1:T(2,128)S(1)}, s32[128,2]{0,1:T(2,128)}, u32[]{:S(2)}) copy-start(s32[128,2]{0,1:T(2,128)} %param.22) | copy-start | bytes 3076
  4.5 62.1 %copy-start.10 = (s32[32]{0:T(128)S(1)}, s32[32]{0:T(128)}, u32[]{:S(2)}) copy-start(s32[32]{0:T(128)} %param.24) | copy-start | bytes 388
  4.5 32.5 %collective-permute-start.1 = (bf16[3840,128]{1,0:T(8,128)(2,1)}, bf16[3840,128]{1,0:T(8,128)(2,1)S(1)}, u32[]{:S(2)}, u32[]{:S(2)}) collective-permute-start(bf16[3840,128]{1,0:T(8,128)(2,1)} %get-tuple-element.30), channel_id=1, source_target_pairs={{0,4},{4,8},{8,12},{12,0},{1,5},{5,9},{9,13},{13,1},{2,6},{6,10},{... | collective-permute-start | bytes 2949128 | tf_op jit(solution)/shard_map/ppermute | solution.py:437
  8.6 28.5 %collective-permute-start.2 = (bf16[3840,128]{1,0:T(8,128)(2,1)}, bf16[3840,128]{1,0:T(8,128)(2,1)S(1)}, u32[]{:S(2)}, u32[]{:S(2)}) collective-permute-start(bf16[3840,128]{1,0:T(8,128)(2,1)} %get-tuple-element.31), channel_id=1, source_target_pairs={{0,12},{4,0},{8,4},{12,8},{1,13},{5,1},{9,5},{13,9},{2,14},{6,2},{... | collective-permute-start | bytes 2949128 | tf_op jit(solution)/shard_map/ppermute | solution.py:437
  11.9 8.8 %collective-permute-start = (bf16[16,640]{1,0:T(8,128)(2,1)S(1)}, bf16[16,640]{1,0:T(8,128)(2,1)S(1)}, u32[]{:S(2)}, u32[]{:S(2)}) collective-permute-start(bf16[16,640]{1,0:T(8,128)(2,1)S(1)} %shard_map.149), channel_id=1, source_target_pairs={{0,16},{16,32},{32,48},{48,64},{64,80},{80,96},{96,112},{112,128},... | collective-permute-start | bytes 61448 | tf_op jit(solution)/shard_map/ppermute | solution.py:433
  21.6 46.1 %copy-start.3 = (bf16[128,320]{0,1:T(8,128)(2,1)S(1)}, bf16[128,320]{0,1:T(8,128)(2,1)}, u32[]{:S(2)}) copy-start(bf16[128,320]{0,1:T(8,128)(2,1)} %param.15) | copy-start | bytes 245764
  21.6 46.1 %copy-start.9 = (f32[5]{0:T(128)S(1)}, f32[5]{0:T(128)}, u32[]{:S(2)}) copy-start(f32[5]{0:T(128)} %skip_ref.1) | copy-start | bytes 64
  62.1 7.1 %collective-permute-start.3 = (bf16[160,128]{1,0:T(8,128)(2,1)S(1)}, bf16[160,128]{1,0:T(8,128)(2,1)S(1)}, u32[]{:S(2)}, u32[]{:S(2)}) collective-permute-start(bf16[160,128]{1,0:T(8,128)(2,1)S(1)} %shard_map.153.own_ref), channel_id=1, source_target_pairs={{0,16},{16,0},{1,17},{17,1},{2,18},{18,2},{3,19},{19,3},{4,20},{20... | collective-permute-start | bytes 122888 | tf_op jit(solution)/shard_map/ppermute | solution.py:479
  71.8 28.9 %all-to-all-start = ((bf16[32,32,128]{2,1,0:T(8,128)(2,1)}), bf16[32,32,128]{2,1,0:T(8,128)(2,1)S(1)}, u32[]{:S(2)}, u32[]{:S(2)}) async-start(bf16[32,32,128]{2,1,0:T(8,128)(2,1)} %bitcast.17), calls=%async_computation | async-start | bytes 524288 | tf_op jit(solution)/shard_map/all_to_all | solution.py:505
  78.7 36.0 %collective-permute-start.4 = (bf16[3840,128]{1,0:T(8,128)(2,1)}, bf16[3840,128]{1,0:T(8,128)(2,1)}, u32[]{:S(2)}, u32[]{:S(2)}) collective-permute-start(bf16[3840,128]{1,0:T(8,128)(2,1)} %get-tuple-element.53), channel_id=1, source_target_pairs={{0,8},{4,12},{8,0},{12,4},{1,9},{5,13},{9,1},{13,5},{2,10},{6,14},... | collective-permute-start | bytes 2949128 | tf_op jit(solution)/shard_map/ppermute | solution.py:498
  100.8 13.9 %copy-start = (bf16[3840,128]{1,0:T(8,128)(2,1)S(1)}, bf16[3840,128]{1,0:T(8,128)(2,1)}, u32[]{:S(2)}) copy-start(bf16[3840,128]{1,0:T(8,128)(2,1)} %get-tuple-element.51.w0_ref) | copy-start | bytes 2949124
  153.1 33.7 %copy-start.7 = (f32[128,2]{0,1:T(2,128)S(1)}, f32[128,2]{0,1:T(2,128)}, u32[]{:S(2)}) copy-start(f32[128,2]{0,1:T(2,128)} %param.23) | copy-start | bytes 3076
  154.1 32.6 %all-to-all-start.4 = ((bf16[32,32,128]{2,1,0:T(8,128)(2,1)}), bf16[32,32,128]{2,1,0:T(8,128)(2,1)S(1)}, u32[]{:S(2)}, u32[]{:S(2)}) async-start(bf16[32,32,128]{2,1,0:T(8,128)(2,1)} %pad.4.clone), calls=%async_computation.4 | async-start | bytes 524288 | tf_op jit(solution)/shard_map/all_to_all | solution.py:524

commit v4 on v3

--- a/solution.py
+++ b/solution.py
@@ -347,7 +347,7 @@
         out_ref[plane * LANES : plane * LANES + size] = totals[plane].T.astype(BF)
 
 
-def gate_up_kernel(ix_ref, g_ref, w0_ref, w1_ref, w2_ref, w3_ref, out_ref):
+def gate_up_kernel(ix_ref, g_ref, gate_ref, up_ref, w1_ref, w2_ref, w3_ref, out_ref):
     rows = 2 * 192
     wide = [jnp.concatenate([g_ref[y, :rows], g_ref[y, rows : 2 * rows]], axis=1) for y in range(4)]
     slim = []
@@ -355,12 +355,17 @@
         packed = g_ref[y, 2 * rows :]
         slim.append(jnp.concatenate([packed[:, :64], packed[:, 64:]], axis=0))
     pairs = [jnp.concatenate([slim[0], slim[1]], axis=1), jnp.concatenate([slim[2], slim[3]], axis=1)]
-    for s, w_ref in enumerate((w0_ref, w1_ref, w2_ref, w3_ref)):
+    span = gate_ref.shape[0]
+    for s, w_ref in enumerate((None, w1_ref, w2_ref, w3_ref)):
         target = lax.rem(ix_ref[0] - s + 4, 4)
 
         def weight(start, size):
+            if w_ref is None:
+                return jnp.concatenate(
+                    [gate_ref[start : start + size], up_ref[start : start + size]], axis=1
+                )
             return jnp.concatenate(
-                [w_ref[start : start + size], w_ref[1280 + start : 1280 + start + size]], axis=1
+                [w_ref[start : start + size], w_ref[span + start : span + start + size]], axis=1
             )
 
         total = dot(wide[0], weight(0, 256))
@@ -384,15 +389,15 @@
         out_ref[i] = hidden
 
 
-def down_kernel(ix_ref, h_ref, w0_ref, w1_ref, w2_ref, w3_ref, out_ref):
+def down_kernel(ix_ref, h_ref, down_ref, w1_ref, w2_ref, w3_ref, out_ref):
     rows = h_ref.shape[1]
     half = rows // 2
     hid = jnp.concatenate([h_ref[lax.rem(ix_ref[0] - s + 4, 4)] for s in range(4)], axis=1)
     blocks = []
     for b in range(5):
-        weight = []
-        for w_ref in (w0_ref, w1_ref, w2_ref, w3_ref):
-            start = 2560 + b * 256
+        start = b * 256
+        weight = [down_ref[:, start : start + 256]]
+        for w_ref in (w1_ref, w2_ref, w3_ref):
             weight.append(
                 jnp.concatenate([w_ref[start : start + 128], w_ref[start + 128 : start + 256]], axis=1)
             )
@@ -404,6 +409,21 @@
         out_ref[y, rows : 2 * rows] = own[:, 128:256].astype(BF)
         last = own[:, 256:]
         out_ref[y, 2 * rows :] = jnp.concatenate([last[:half], last[half:]], axis=1).astype(BF)
+
+
+def expert_call(kernel, shape, ix, rows, own, own_specs, pieces, piece_spec):
+    whole = pl.BlockSpec(rows.shape, lambda i, b: (0, 0, 0))
+    return pl.pallas_call(
+        kernel,
+        out_shape=jax.ShapeDtypeStruct(shape, BF),
+        grid_spec=pltpu.PrefetchScalarGridSpec(
+            num_scalar_prefetch=1,
+            grid=(1,),
+            in_specs=[whole, *own_specs] + [piece_spec] * len(pieces),
+            out_specs=pl.BlockSpec(shape, lambda i, b: (0, 0, 0)),
+        ),
+        compiler_params=pltpu.CompilerParams(vmem_limit_bytes=24 << 20),
+    )(ix, rows, *own, *pieces)
 
 
 def body(
@@ -433,7 +453,7 @@
     rim = lax.ppermute(edge, CTX, [(i, i + 1) for i in range(31)])
     ixs = ix.reshape(1)
     own = (gate_w[0], up_w[0], down_w[0])
-    pieces = dict(zip((1, 3, 2, 0), weight_pieces((1, 3, 2, 0), ixs, *own)))
+    pieces = dict(zip((1, 3, 2), weight_pieces((1, 3, 2), ixs, *own)))
     swapped = {s: lax.ppermute(pieces[s], "x", [(i, (i + s) % 4) for i in range(4)]) for s in (1, 3)}
     xs, bcs, run, turn, message = kernel_call(
         state_kernel,
@@ -511,12 +531,33 @@
     )
     wide = lax.all_gather(rows, "y")
     count = 2 * experts * HALF
-    weights = [pieces[0], swapped[1], swapped[2], swapped[3]]
-    parts = kernel_call(gate_up_kernel, [((4, 2 * count, LANES), BF)], ixs, wide, *weights, scalars=1)
+    weights = [swapped[1], swapped[2], swapped[3]]
+    span = gate_w.shape[1] // 4
+    across = pl.BlockSpec((span, LANES), lambda i, b: (b[0], 0))
+    along = pl.BlockSpec((LANES, span), lambda i, b: (0, b[0]))
+    parts = expert_call(
+        gate_up_kernel,
+        (4, 2 * count, LANES),
+        ixs,
+        wide,
+        (gate_w[0], up_w[0]),
+        (across, across),
+        weights,
+        pl.BlockSpec((2 * span, LANES), lambda i, b: (0, 0)),
+    )
     parts = lax.all_to_all(parts, "x", 0, 0, tiled=True)
     hidden = kernel_call(hidden_kernel, [((4, count, LANES), BF)], parts)
     hiddens = lax.all_to_all(hidden, "x", 0, 0, tiled=True)
-    downs = kernel_call(down_kernel, [((4, count * 5 // 2, LANES), BF)], ixs, hiddens, *weights, scalars=1)
+    downs = expert_call(
+        down_kernel,
+        (4, count * 5 // 2, LANES),
+        ixs,
+        hiddens,
+        (down_w[0],),
+        (along,),
+        weights,
+        pl.BlockSpec((span, LANES), lambda i, b: (2, 0)),
+    )
     downs = lax.all_to_all(downs, "y", 0, 0, tiled=True)
     result = jnp.sum(downs.astype(F32), axis=0).astype(BF)
     result = result.reshape(GROUPS, experts, HALF, LANES).transpose(1, 0, 2, 3)

time: 189 us -> 191 us (1.011)
  local copies, waits for them, and re-layouts: 1.33 us -> 3.74 us
    pallas_call x11 -> x9, Pallas kernels: 13 us -> 8.42 us  [kernel_call(): pl.pallas_call(kernel, out_shape=shapes, in_specs=specs, out_specs=[pl.Bl...]
    pallas_call x0 -> x2, Pallas kernels: none -> 4.25 us  [expert_call(): pl.pallas_call(kernel, out_shape=jax.ShapeDtypeStruct(shape, BF), grid_sp...]
    unnamed x26 -> x42, local copies, waits for them, and re-layouts: 0.26 us -> 2.68 us
where the time goes in v4:
time: 191 us; the launch traced here: 190 us
  blocking collectives  86.3 us (45%)
  waiting for transfers between devices  43.4 us (23%)
  starting transfers between devices  37.8 us (20%)
  Pallas kernels  17.3 us (9%)
  local copies, waits for them, and re-layouts  3.74 us (2%)
    all_gather x1, blocking collectives, body(): fars = lax.all_gather(group, 'zh')  23.6 us
    all_to_all x1, waiting for transfers between devices, body(): lax.all_to_all(result, CTX, 0, 0, tiled=True).reshape(slots, LANES)  21.4 us
    all_to_all x1, waiting for transfers between devices, body(): lax.all_to_all(outgoing.reshape(experts, PIECE, LANES), CTX, 0, 0, tiled=...  18.2 us
    all_gather x1, blocking collectives, body(): near = lax.all_gather(message, NEAR)  15.4 us
    all_gather x1, blocking collectives, body(): wide = lax.all_gather(rows, 'y')  13.7 us
    all_to_all x1, blocking collectives, body(): parts = lax.all_to_all(parts, 'x', 0, 0, tiled=True)  13.1 us
    all_to_all x1, blocking collectives, body(): downs = lax.all_to_all(downs, 'y', 0, 0, tiled=True)  11.8 us
    all_to_all x1, starting transfers between devices, body(): lax.all_to_all(result, CTX, 0, 0, tiled=True).reshape(slots, LANES)  10.6 us
  transfers between devices with their start and end apart: 7, of which 3 were waited for; matrix products, arithmetic and copies ran while one was open for 0% of the time, Pallas kernels for 2%

profile of v4, /device:TPU:1, one launch (start us, length us, event | category | flops | bytes accessed | tf_op | source)
XLA Modules:
  0.0 189.9 jit_solution(5429626972133332014)
XLA Ops:
  0.7 3.1 %shard_map.151 = (bf16[3840,128]{1,0:T(8,128)(2,1)}, bf16[3840,128]{1,0:T(8,128)(2,1)}, bf16[3840,128]{1,0:T(8,128)(2,1)}) custom-call(s32[1]{0:T(128)} %bitcast.6.ix_ref, bf16[5120,128]{1,0:T(8,128)(2,1)} %bitcast.29, bf16[5120,128]{1,0:T(8,128)(2,1)} %bitcast.31, bf16[128,5120]{1,0:T(8,128)(2,1)} %bitcast.27), custom_call_target="tpu_custom_call" | custom-call | tf_op jit(solution)/shard_map/pallas_call | solution.py:319
  3.9 4.1 %collective-permute-start.1 = (bf16[3840,128]{1,0:T(8,128)(2,1)}, bf16[3840,128]{1,0:T(8,128)(2,1)S(1)}, u32[]{:S(2)}, u32[]{:S(2)}) collective-permute-start(bf16[3840,128]{1,0:T(8,128)(2,1)} %get-tuple-element.29), channel_id=1, source_target_pairs={{0,4},{4,8},{8,12},{12,0},{1,5},{5,9},{9,13},{13,1},{2,6},{6,10},{... | collective-permute-start | bytes 2949128 | tf_op jit(solution)/shard_map/ppermute | solution.py:457
  7.9 3.2 %collective-permute-start.2 = (bf16[3840,128]{1,0:T(8,128)(2,1)}, bf16[3840,128]{1,0:T(8,128)(2,1)S(1)}, u32[]{:S(2)}, u32[]{:S(2)}) collective-permute-start(bf16[3840,128]{1,0:T(8,128)(2,1)} %get-tuple-element.30), channel_id=1, source_target_pairs={{0,12},{4,0},{8,4},{12,8},{1,13},{5,1},{9,5},{13,9},{2,14},{6,2},{... | collective-permute-start | bytes 2949128 | tf_op jit(solution)/shard_map/ppermute | solution.py:457
  11.3 4.9 %collective-permute-start = (bf16[16,640]{1,0:T(8,128)(2,1)S(1)}, bf16[16,640]{1,0:T(8,128)(2,1)S(1)}, u32[]{:S(2)}, u32[]{:S(2)}) collective-permute-start(bf16[16,640]{1,0:T(8,128)(2,1)S(1)} %shard_map.149), channel_id=1, source_target_pairs={{0,16},{16,32},{32,48},{48,64},{64,80},{80,96},{96,112},{112,128},... | collective-permute-start | bytes 61448 | tf_op jit(solution)/shard_map/ppermute | solution.py:453
  16.2 3.8 %collective-permute-done.rim_ref = bf16[16,640]{1,0:T(8,128)(2,1)S(1)} collective-permute-done((bf16[16,640]{1,0:T(8,128)(2,1)S(1)}, bf16[16,640]{1,0:T(8,128)(2,1)S(1)}, u32[]{:S(2)}, u32[]{:S(2)}) %collective-permute-start) | collective-permute-done | bytes 20512 | tf_op jit(solution)/shard_map/ppermute | solution.py:453
  20.0 1.0 shard_map.150
  21.0 15.4 %all-gather = bf16[2688,128]{1,0:T(8,128)(2,1)S(1)} all-gather(bf16[336,128]{1,0:T(8,128)(2,1)S(1)} %get-tuple-element.28), channel_id=2, replica_groups=mesh['zh'=4,'zl'=4,'c'=2,'x'=4,'y'=4] {'zl','c'}, dimensions={0}, use_global_device_ids=true | all-gather | bytes 774144 | tf_op jit(solution)/shard_map/all_gather | solution.py:475
  36.4 0.8 shard_map.152
  37.3 23.6 %all-gather.1 = bf16[704,128]{1,0:T(8,128)(2,1)S(1)} all-gather(bf16[176,128]{1,0:T(8,128)(2,1)S(1)} %get-tuple-element.32), channel_id=3, replica_groups=mesh['zh'=4,'zl'=4,'c'=2,'x'=4,'y'=4] {'zh'}, dimensions={0}, use_global_device_ids=true | all-gather | bytes 225280 | tf_op jit(solution)/shard_map/all_gather | solution.py:485
  60.8 0.7 shard_map.153.own_ref
  61.5 4.4 %collective-permute-start.3 = (bf16[160,128]{1,0:T(8,128)(2,1)S(1)}, bf16[160,128]{1,0:T(8,128)(2,1)S(1)}, u32[]{:S(2)}, u32[]{:S(2)}) collective-permute-start(bf16[160,128]{1,0:T(8,128)(2,1)S(1)} %shard_map.153.own_ref), channel_id=1, source_target_pairs={{0,16},{16,0},{1,17},{17,1},{2,18},{18,2},{3,19},{19,3},{4,20},{20... | collective-permute-start | bytes 122888 | tf_op jit(solution)/shard_map/ppermute | solution.py:499
  65.9 1.1 shard_map.155.select_ref
  67.1 1.5 shard_map.154
  68.6 2.6 %shard_map.156 = (bf16[320,128]{1,0:T(8,128)(2,1)}, bf16[1024,128]{1,0:T(8,128)(2,1)}) custom-call(s32[3]{0:T(128)S(1)} %pad_add_fusion.place_ref, bf16[160,128]{1,0:T(8,128)(2,1)S(1)} %shard_map.153.own_ref, bf16[160,128]{1,0:T(8,128)(2,1)S(1)} %collective-permute-done.3.other_ref, f32[320,128]{1,0:T(8,128)S(1)} %get-tuple-element.33.near_ref, ...), custom_call_target="tpu_custom_call" | custom-call | tf_op jit(solution)/shard_map/pallas_call | solution.py:34
  71.2 6.9 %all-to-all-start = ((bf16[32,32,128]{2,1,0:T(8,128)(2,1)}), bf16[32,32,128]{2,1,0:T(8,128)(2,1)S(1)}, u32[]{:S(2)}, u32[]{:S(2)}) async-start(bf16[32,32,128]{2,1,0:T(8,128)(2,1)} %bitcast.17), calls=%async_computation | async-start | bytes 524288 | tf_op jit(solution)/shard_map/all_to_all | solution.py:525
  78.1 3.8 %collective-permute-start.4 = (bf16[3840,128]{1,0:T(8,128)(2,1)}, bf16[3840,128]{1,0:T(8,128)(2,1)}, u32[]{:S(2)}, u32[]{:S(2)}) collective-permute-start(bf16[3840,128]{1,0:T(8,128)(2,1)} %get-tuple-element.51), channel_id=1, source_target_pairs={{0,8},{4,12},{8,0},{12,4},{1,9},{5,13},{9,1},{13,5},{2,10},{6,14},... | collective-permute-start | bytes 2949128 | tf_op jit(solution)/shard_map/ppermute | solution.py:518
  81.9 18.2 %all-to-all-done = bf16[32,32,128]{2,1,0:T(8,128)(2,1)S(1)} async-done(((bf16[32,32,128]{2,1,0:T(8,128)(2,1)}), bf16[32,32,128]{2,1,0:T(8,128)(2,1)S(1)}, u32[]{:S(2)}, u32[]{:S(2)}) %all-to-all-start) | async-done | bytes 262176 | tf_op jit(solution)/shard_map/all_to_all | solution.py:525
  100.4 13.7 %all_gather.19.g_ref = bf16[4,960,128]{2,1,0:T(8,128)(2,1)S(1)} all-gather(bf16[1,960,128]{2,1,0:T(8,128)(2,1)S(1)} %all_gather_reshape.3), channel_id=1, replica_groups=mesh['zh'=4,'zl'=4,'c'=2,'x'=4,'y'=4] {'y'}, dimensions={0}, use_global_device_ids=true | all-gather | bytes 1228800 | tf_op jit(solution)/shard_map/all_gather | solution.py:532
  114.1 1.2 copy-done.4
  115.3 1.2 copy-done.7
  116.5 2.5 %shard_map.158 = bf16[4,768,128]{2,1,0:T(8,128)(2,1)S(1)} custom-call(s32[1]{0:T(128)} %bitcast.6.ix_ref, bf16[4,960,128]{2,1,0:T(8,128)(2,1)S(1)} %all_gather.19.g_ref, bf16[5120,128]{1,0:T(8,128)(2,1)S(1)} %bitcast.30, bf16[5120,128]{1,0:T(8,128)(2,1)S(1)} %bitcast.32, bf16[3840,128]{1,0:T(8,128)(2,1)S(1)} %copy-done.4, ...), custom_call_target="tpu_custom_call" | custom-call | tf_op jit(solution)/shard_map/pallas_call | solution.py:416
  119.0 13.1 %all_to_all.25.p_ref = bf16[4,768,128]{2,1,0:T(8,128)(2,1)S(1)} all-to-all(bf16[4,768,128]{2,1,0:T(8,128)(2,1)S(1)} %shard_map.158), channel_id=1, replica_groups=mesh['zh'=4,'zl'=4,'c'=2,'x'=4,'y'=4] {'x'}, dimensions={0} | all-to-all | bytes 1572864 | tf_op jit(solution)/shard_map/all_to_all | solution.py:548
  132.1 0.1 shard_map.159
  132.3 8.8 %all_to_all.26.h_ref = bf16[4,384,128]{2,1,0:T(8,128)(2,1)S(1)} all-to-all(bf16[4,384,128]{2,1,0:T(8,128)(2,1)S(1)} %shard_map.159), channel_id=1, replica_groups=mesh['zh'=4,'zl'=4,'c'=2,'x'=4,'y'=4] {'x'}, dimensions={0} | all-to-all | bytes 786432 | tf_op jit(solution)/shard_map/all_to_all | solution.py:550
  141.0 1.8 shard_map.160
  142.8 11.8 %all_to_all.27 = bf16[4,960,128]{2,1,0:T(8,128)(2,1)S(1)} all-to-all(bf16[4,960,128]{2,1,0:T(8,128)(2,1)S(1)} %shard_map.160), channel_id=1, replica_groups=mesh['zh'=4,'zl'=4,'c'=2,'x'=4,'y'=4] {'y'}, dimensions={0} | all-to-all | bytes 1966080 | tf_op jit(solution)/shard_map/all_to_all | solution.py:561
  154.6 0.2 reduce_sum.12
  155.1 0.7 pad.4.clone
  155.8 10.6 %all-to-all-start.4 = ((bf16[32,32,128]{2,1,0:T(8,128)(2,1)}), bf16[32,32,128]{2,1,0:T(8,128)(2,1)S(1)}, u32[]{:S(2)}, u32[]{:S(2)}) async-start(bf16[32,32,128]{2,1,0:T(8,128)(2,1)} %pad.4.clone), calls=%async_computation.4 | async-start | bytes 524288 | tf_op jit(solution)/shard_map/all_to_all | solution.py:565
  166.5 0.6 shard_map.157
  167.1 21.4 %all-to-all-done.4 = bf16[32,32,128]{2,1,0:T(8,128)(2,1)S(1)} async-done(((bf16[32,32,128]{2,1,0:T(8,128)(2,1)}), bf16[32,32,128]{2,1,0:T(8,128)(2,1)S(1)}, u32[]{:S(2)}, u32[]{:S(2)}) %all-to-all-start.4) | async-done | bytes 262176 | tf_op jit(solution)/shard_map/all_to_all | solution.py:565
  188.5 1.4 shard_map.161
  (51 shorter events, 0.8 us)
Async XLA Ops:
  0.6 10.5 %copy-start.9 = (bf16[128,320]{0,1:T(8,128)(2,1)S(1)}, bf16[128,320]{0,1:T(8,128)(2,1)}, u32[]{:S(2)}) copy-start(bf16[128,320]{0,1:T(8,128)(2,1)} %param.14) | copy-start | bytes 245764
  0.6 10.5 %copy-start.10 = (bf16[128,256]{1,0:T(8,128)(2,1)S(1)}, bf16[128,256]{1,0:T(8,128)(2,1)}, u32[]{:S(2)}) copy-start(bf16[128,256]{1,0:T(8,128)(2,1)} %bc_ref.3) | copy-start | bytes 196612
  0.7 19.4 %copy-start.12 = (f32[4,320]{1,0:T(4,128)S(1)}, f32[4,320]{1,0:T(4,128)}, u32[]{:S(2)}) copy-start(f32[4,320]{1,0:T(4,128)} %cx_ref.1) | copy-start | bytes 15364
  0.7 19.4 %copy-start.13 = (f32[4,256]{1,0:T(4,128)S(1)}, f32[4,256]{1,0:T(4,128)}, u32[]{:S(2)}) copy-start(f32[4,256]{1,0:T(4,128)} %cbc_ref.1) | copy-start | bytes 12292
  0.7 19.3 %copy-start.14 = (f32[128,5]{0,1:T(8,128)S(1)}, f32[128,5]{0,1:T(8,128)}, u32[]{:S(2)}) copy-start(f32[128,5]{0,1:T(8,128)} %param.19) | copy-start | bytes 7684
  3.8 62.1 %copy-start.19 = (f32[320]{0:T(512)S(1)}, f32[320]{0:T(512)}, u32[]{:S(2)}) copy-start(f32[320]{0:T(512)} %param.21) | copy-start | bytes 3844
  3.8 62.1 %copy-start.16 = (s32[128,2]{0,1:T(2,128)S(1)}, s32[128,2]{0,1:T(2,128)}, u32[]{:S(2)}) copy-start(s32[128,2]{0,1:T(2,128)} %param.22) | copy-start | bytes 3076
  3.8 62.1 %copy-start.18 = (s32[32]{0:T(128)S(1)}, s32[32]{0:T(128)}, u32[]{:S(2)}) copy-start(s32[32]{0:T(128)} %param.24) | copy-start | bytes 388
  3.9 32.5 %collective-permute-start.1 = (bf16[3840,128]{1,0:T(8,128)(2,1)}, bf16[3840,128]{1,0:T(8,128)(2,1)S(1)}, u32[]{:S(2)}, u32[]{:S(2)}) collective-permute-start(bf16[3840,128]{1,0:T(8,128)(2,1)} %get-tuple-element.29), channel_id=1, source_target_pairs={{0,4},{4,8},{8,12},{12,0},{1,5},{5,9},{9,13},{13,1},{2,6},{6,10},{... | collective-permute-start | bytes 2949128 | tf_op jit(solution)/shard_map/ppermute | solution.py:457
  7.9 28.5 %collective-permute-start.2 = (bf16[3840,128]{1,0:T(8,128)(2,1)}, bf16[3840,128]{1,0:T(8,128)(2,1)S(1)}, u32[]{:S(2)}, u32[]{:S(2)}) collective-permute-start(bf16[3840,128]{1,0:T(8,128)(2,1)} %get-tuple-element.30), channel_id=1, source_target_pairs={{0,12},{4,0},{8,4},{12,8},{1,13},{5,1},{9,5},{13,9},{2,14},{6,2},{... | collective-permute-start | bytes 2949128 | tf_op jit(solution)/shard_map/ppermute | solution.py:457
  11.3 8.8 %collective-permute-start = (bf16[16,640]{1,0:T(8,128)(2,1)S(1)}, bf16[16,640]{1,0:T(8,128)(2,1)S(1)}, u32[]{:S(2)}, u32[]{:S(2)}) collective-permute-start(bf16[16,640]{1,0:T(8,128)(2,1)S(1)} %shard_map.149), channel_id=1, source_target_pairs={{0,16},{16,32},{32,48},{48,64},{64,80},{80,96},{96,112},{112,128},... | collective-permute-start | bytes 61448 | tf_op jit(solution)/shard_map/ppermute | solution.py:453
  21.0 46.1 %copy-start.11 = (bf16[128,320]{0,1:T(8,128)(2,1)S(1)}, bf16[128,320]{0,1:T(8,128)(2,1)}, u32[]{:S(2)}) copy-start(bf16[128,320]{0,1:T(8,128)(2,1)} %param.15) | copy-start | bytes 245764
  21.0 46.1 %copy-start.17 = (f32[5]{0:T(128)S(1)}, f32[5]{0:T(128)}, u32[]{:S(2)}) copy-start(f32[5]{0:T(128)} %skip_ref.1) | copy-start | bytes 64
  36.4 32.2 %copy-start.3 = (bf16[3840,128]{1,0:T(8,128)(2,1)}, bf16[3840,128]{1,0:T(8,128)(2,1)S(1)}, u32[]{:S(2)}) copy-start(bf16[3840,128]{1,0:T(8,128)(2,1)S(1)} %collective-permute-done.1.w1_ref) | copy-start | bytes 2949124
  36.4 32.2 %copy-start.6 = (bf16[3840,128]{1,0:T(8,128)(2,1)}, bf16[3840,128]{1,0:T(8,128)(2,1)S(1)}, u32[]{:S(2)}) copy-start(bf16[3840,128]{1,0:T(8,128)(2,1)S(1)} %collective-permute-done.2.w3_ref) | copy-start | bytes 2949124
  61.5 7.1 %collective-permute-start.3 = (bf16[160,128]{1,0:T(8,128)(2,1)S(1)}, bf16[160,128]{1,0:T(8,128)(2,1)S(1)}, u32[]{:S(2)}, u32[]{:S(2)}) collective-permute-start(bf16[160,128]{1,0:T(8,128)(2,1)S(1)} %shard_map.153.own_ref), channel_id=1, source_target_pairs={{0,16},{16,0},{1,17},{17,1},{2,18},{18,2},{3,19},{19,3},{4,20},{20... | collective-permute-start | bytes 122888 | tf_op jit(solution)/shard_map/ppermute | solution.py:499
  71.2 28.9 %all-to-all-start = ((bf16[32,32,128]{2,1,0:T(8,128)(2,1)}), bf16[32,32,128]{2,1,0:T(8,128)(2,1)S(1)}, u32[]{:S(2)}, u32[]{:S(2)}) async-start(bf16[32,32,128]{2,1,0:T(8,128)(2,1)} %bitcast.17), calls=%async_computation | async-start | bytes 524288 | tf_op jit(solution)/shard_map/all_to_all | solution.py:525
  78.1 36.0 %collective-permute-start.4 = (bf16[3840,128]{1,0:T(8,128)(2,1)}, bf16[3840,128]{1,0:T(8,128)(2,1)}, u32[]{:S(2)}, u32[]{:S(2)}) collective-permute-start(bf16[3840,128]{1,0:T(8,128)(2,1)} %get-tuple-element.51), channel_id=1, source_target_pairs={{0,8},{4,12},{8,0},{12,4},{1,9},{5,13},{9,1},{13,5},{2,10},{6,14},... | collective-permute-start | bytes 2949128 | tf_op jit(solution)/shard_map/ppermute | solution.py:518
  100.1 14.0 %copy-start.2 = (bf16[1,5120,128]{2,1,0:T(8,128)(2,1)S(1)}, bf16[1,5120,128]{2,1,0:T(8,128)(2,1)}, u32[]{:S(2)}) copy-start(bf16[1,5120,128]{2,1,0:T(8,128)(2,1)} %param.26) | copy-start | bytes 3932164
  100.2 13.9 %copy-start.1 = (bf16[1,5120,128]{2,1,0:T(8,128)(2,1)S(1)}, bf16[1,5120,128]{2,1,0:T(8,128)(2,1)}, u32[]{:S(2)}) copy-start(bf16[1,5120,128]{2,1,0:T(8,128)(2,1)} %param.25) | copy-start | bytes 3932164
  114.1 1.2 copy-start.4
  115.3 1.2 copy-start.7
  119.0 22.0 %copy-start.5 = (bf16[3840,128]{1,0:T(8,128)(2,1)S(1)}, bf16[3840,128]{1,0:T(8,128)(2,1)}, u32[]{:S(2)}) copy-start(bf16[3840,128]{1,0:T(8,128)(2,1)} %copy-done.3) | copy-start | bytes 2949124
  119.0 22.0 %copy-start.8 = (bf16[3840,128]{1,0:T(8,128)(2,1)S(1)}, bf16[3840,128]{1,0:T(8,128)(2,1)}, u32[]{:S(2)}) copy-start(bf16[3840,128]{1,0:T(8,128)(2,1)} %copy-done.6) | copy-start | bytes 2949124
  132.1 8.9 %copy-start = (bf16[1,128,5120]{2,1,0:T(8,128)(2,1)S(1)}, bf16[1,128,5120]{2,1,0:T(8,128)(2,1)}, u32[]{:S(2)}) copy-start(bf16[1,128,5120]{2,1,0:T(8,128)(2,1)} %param.27) | copy-start | bytes 3932164
  154.8 33.6 %copy-start.15 = (f32[128,2]{0,1:T(2,128)S(1)}, f32[128,2]{0,1:T(2,128)}, u32[]{:S(2)}) copy-start(f32[128,2]{0,1:T(2,128)} %param.23) | copy-start | bytes 3076
  155.8 32.6 %all-to-all-start.4 = ((bf16[32,32,128]{2,1,0:T(8,128)(2,1)}), bf16[32,32,128]{2,1,0:T(8,128)(2,1)S(1)}, u32[]{:S(2)}, u32[]{:S(2)}) async-start(bf16[32,32,128]{2,1,0:T(8,128)(2,1)} %pad.4.clone), calls=%async_computation.4 | async-start | bytes 524288 | tf_op jit(solution)/shard_map/all_to_all | solution.py:565

commit v5 on v3

--- a/solution.py
+++ b/solution.py
@@ -347,7 +347,22 @@
         out_ref[plane * LANES : plane * LANES + size] = totals[plane].T.astype(BF)
 
 
-def gate_up_kernel(ix_ref, g_ref, w0_ref, w1_ref, w2_ref, w3_ref, out_ref):
+def gate_up_kernel(
+    ix_ref, rows_ref, gate_ref, up_ref, w1_ref, w2_ref, w3_ref, out_ref, g_ref, held, sems
+):
+    span = gate_ref.shape[0] // 4
+    block = pl.multiple_of(ix_ref[0] * span, span)
+    pairs = [
+        (rows_ref, g_ref),
+        (gate_ref.at[pl.ds(block, span)], held.at[0, pl.ds(0, span)]),
+        (up_ref.at[pl.ds(block, span)], held.at[0, pl.ds(span, span)]),
+    ]
+    for s, w_ref in enumerate((w1_ref, w2_ref, w3_ref)):
+        pairs.append((w_ref.at[pl.ds(0, 2 * span)], held.at[s + 1]))
+    copies = [pltpu.make_async_copy(p, q, sems.at[n]) for n, (p, q) in enumerate(pairs)]
+    for copy in copies:
+        copy.start()
+    copies[0].wait()
     rows = 2 * 192
     wide = [jnp.concatenate([g_ref[y, :rows], g_ref[y, rows : 2 * rows]], axis=1) for y in range(4)]
     slim = []
@@ -355,12 +370,14 @@
         packed = g_ref[y, 2 * rows :]
         slim.append(jnp.concatenate([packed[:, :64], packed[:, 64:]], axis=0))
     pairs = [jnp.concatenate([slim[0], slim[1]], axis=1), jnp.concatenate([slim[2], slim[3]], axis=1)]
-    for s, w_ref in enumerate((w0_ref, w1_ref, w2_ref, w3_ref)):
+    copies[1].wait()
+    for s in range(4):
         target = lax.rem(ix_ref[0] - s + 4, 4)
+        copies[s + 2].wait()
 
         def weight(start, size):
             return jnp.concatenate(
-                [w_ref[start : start + size], w_ref[1280 + start : 1280 + start + size]], axis=1
+                [held[s, start : start + size], held[s, span + start : span + start + size]], axis=1
             )
 
         total = dot(wide[0], weight(0, 256))
@@ -384,26 +401,57 @@
         out_ref[i] = hidden
 
 
-def down_kernel(ix_ref, h_ref, w0_ref, w1_ref, w2_ref, w3_ref, out_ref):
+def down_kernel(ix_ref, rows_ref, down_ref, w1_ref, w2_ref, w3_ref, out_ref, h_ref, own_ref, held, sems):
     rows = h_ref.shape[1]
     half = rows // 2
-    hid = jnp.concatenate([h_ref[lax.rem(ix_ref[0] - s + 4, 4)] for s in range(4)], axis=1)
-    blocks = []
-    for b in range(5):
-        weight = []
-        for w_ref in (w0_ref, w1_ref, w2_ref, w3_ref):
-            start = 2560 + b * 256
-            weight.append(
-                jnp.concatenate([w_ref[start : start + 128], w_ref[start + 128 : start + 256]], axis=1)
-            )
-        blocks.append(dot(hid, jnp.concatenate(weight, axis=0)))
-    full = jnp.concatenate(blocks, axis=1)
+    span = held.shape[1]
+    block = pl.multiple_of(ix_ref[0] * span, span)
+    pairs = [(rows_ref, h_ref), (down_ref.at[:, pl.ds(block, span)], own_ref)]
+    for s, w_ref in enumerate((w1_ref, w2_ref, w3_ref)):
+        pairs.append((w_ref.at[pl.ds(2 * span, span)], held.at[s]))
+    copies = [pltpu.make_async_copy(p, q, sems.at[n]) for n, (p, q) in enumerate(pairs)]
+    for copy in copies:
+        copy.start()
+    copies[0].wait()
+    hid = [h_ref[lax.rem(ix_ref[0] - s + 4, 4)] for s in range(4)]
+
+    def weight(s, start):
+        if s == 0:
+            return own_ref[:, start : start + 256]
+        return jnp.concatenate(
+            [held[s - 1, start : start + 128], held[s - 1, start + 128 : start + 256]], axis=1
+        )
+
+    full = 0.0
+    for pair in ((0, 1), (2, 3)):
+        for s in pair:
+            copies[s + 1].wait()
+        both = jnp.concatenate([hid[s] for s in pair], axis=1)
+        full += jnp.concatenate(
+            [
+                dot(both, jnp.concatenate([weight(s, b * 256) for s in pair], axis=0))
+                for b in range(span // 256)
+            ],
+            axis=1,
+        )
     for y in range(4):
         own = full[:, y * 320 : (y + 1) * 320]
         out_ref[y, :rows] = own[:, :128].astype(BF)
         out_ref[y, rows : 2 * rows] = own[:, 128:256].astype(BF)
         last = own[:, 256:]
         out_ref[y, 2 * rows :] = jnp.concatenate([last[:half], last[half:]], axis=1).astype(BF)
+
+
+def expert_call(kernel, shape, ix, operands, scratch):
+    return pl.pallas_call(
+        kernel,
+        out_shape=jax.ShapeDtypeStruct(shape, BF),
+        in_specs=[pl.BlockSpec(memory_space=pltpu.SMEM)]
+        + [pl.BlockSpec(memory_space=pltpu.HBM)] * len(operands),
+        out_specs=pl.BlockSpec(memory_space=pltpu.VMEM),
+        scratch_shapes=scratch,
+        compiler_params=pltpu.CompilerParams(vmem_limit_bytes=60 << 20),
+    )(ix, *operands)
 
 
 def body(
@@ -433,7 +481,7 @@
     rim = lax.ppermute(edge, CTX, [(i, i + 1) for i in range(31)])
     ixs = ix.reshape(1)
     own = (gate_w[0], up_w[0], down_w[0])
-    pieces = dict(zip((1, 3, 2, 0), weight_pieces((1, 3, 2, 0), ixs, *own)))
+    pieces = dict(zip((1, 3, 2), weight_pieces((1, 3, 2), ixs, *own)))
     swapped = {s: lax.ppermute(pieces[s], "x", [(i, (i + s) % 4) for i in range(4)]) for s in (1, 3)}
     xs, bcs, run, turn, message = kernel_call(
         state_kernel,
@@ -511,12 +559,447 @@
     )
     wide = lax.all_gather(rows, "y")
     count = 2 * experts * HALF
-    weights = [pieces[0], swapped[1], swapped[2], swapped[3]]
-    parts = kernel_call(gate_up_kernel, [((4, 2 * count, LANES), BF)], ixs, wide, *weights, scalars=1)
+    weights = [swapped[1], swapped[2], swapped[3]]
+    span = gate_w.shape[1] // 4
+    parts = []
+    for start in range(0, width, LANES):
+        stop = min(start + LANES, width)
+        parts.append(conv(rim_ref[:, start:stop], turned(x_ref[start:stop]), cx_ref[:, start:stop]))
+    xs = jnp.concatenate(parts, axis=1)
+    bcs = conv(rim_ref[:, 384:], bc_ref[...].astype(F32), cbc_ref[...])
+    lower = (iota((tokens, tokens), 0) >= iota((tokens, tokens), 1)).astype(F32)
+    scratch[...] = jnp.zeros(scratch.shape, F32)
+    scratch[:heads] = decay_ref[...]
+    run = exact(lower, scratch[...], ((1,), (1,)))
+    last = run[tokens - 1 : tokens]
+    tails = jnp.exp(last - run)
+    state = exact(xs * spread(tails, heads), bcs[:, :STATE], ((0,), (0,)))
+    xs_ref[...] = xs
+    bcs_ref[...] = bcs
+    run_ref[...] = run
+    turn_ref[...] = exact(scratch[...], lower, ((1,), (1,)))
+    msg_ref[:width] = state.astype(BF)
+    write_logs(msg_ref, width, last)
+
+
+def inner_kernel(xs_ref, bcs_ref, run_ref, turn_ref, skip_ref, z_ref, y_ref, z_out_ref):
+    tokens, width = xs_ref.shape
+    lower = iota((tokens, tokens), 0) >= iota((tokens, tokens), 1)
+    scores = exact(bcs_ref[:, STATE:], bcs_ref[:, :STATE], ((1,), (1,)))
+    outs = []
+    for h in range(width // HEAD_DIM):
+        gaps = run_ref[:, h : h + 1] - turn_ref[h : h + 1]
+        weight = jnp.where(lower, jnp.exp(jnp.where(lower, gaps, 0.0)), 0.0) * scores
+        x = xs_ref[:, h * HEAD_DIM : (h + 1) * HEAD_DIM]
+        outs.append(exact(weight, x) + skip_ref[h] * x)
+    y_ref[...] = jnp.concatenate(outs, axis=1)
+    z_out_ref[...] = silu(turned(z_ref[...]))
+
+
+def near_kernel(place_ref, near_ref, carried_ref, log_ref, msg_ref, scratch):
+    count, rows, _ = near_ref.shape
+    rows -= 16
+    heads = rows // HEAD_DIM
+    total = [jnp.zeros((HEAD_DIM, STATE), F32)] * heads
+    kept = total
+    log = jnp.zeros((1, STATE), F32)
+    kept_log = log
+    for j in range(count):
+        own = place_ref[0] == j
+        kept = [jnp.where(own, t, k) for t, k in zip(total, kept)]
+        kept_log = jnp.where(own, log, kept_log)
+        step = read_logs(near_ref[j, rows:])
+        factor = jnp.exp(step)
+        log = log + step
+        total = [
+            factor[:, h : h + 1] * total[h] + near_ref[j, h * HEAD_DIM : (h + 1) * HEAD_DIM].astype(F32)
+            for h in range(heads)
+        ]
+    for h in range(heads):
+        carried_ref[h * HEAD_DIM : (h + 1) * HEAD_DIM] = kept[h]
+        scratch[h * HEAD_DIM : (h + 1) * HEAD_DIM] = total[h].astype(BF)
+    log_ref[...] = jnp.broadcast_to(kept_log, log_ref.shape)
+    part = rows // 2
+    msg_ref[:part] = scratch[pl.ds(pl.multiple_of(place_ref[1] * part, 32), part)]
+    write_logs(msg_ref, part, log)
+
+
+def far_kernel(place_ref, far_ref, out_ref):
+    part = out_ref.shape[0]
+    units = part // 32
+    lanes = iota((1, STATE), 1)
+    total = [jnp.zeros((32, STATE), F32)] * units
+    for g in range(far_ref.shape[0] - 1):
+        factor = jnp.exp(read_logs(far_ref[g, part:]))
+        earlier = g < place_ref[2]
+        for u in range(units):
+            head = (place_ref[1] * units + u) // 2
+            one = jnp.sum(jnp.where(lanes == head, factor, 0.0), axis=1, keepdims=True)
+            state = far_ref[g, u * 32 : (u + 1) * 32].astype(F32)
+            total[u] = jnp.where(earlier, one * total[u] + state, total[u])
+    for u in range(units):
+        out_ref[u * 32 : (u + 1) * 32] = total[u].astype(BF)
+
+
+def finish_kernel(
+    place_ref, own_ref, other_ref, near_ref, log_ref, bcs_ref, run_ref, y_ref, z_ref, gain_ref, select_ref,
+    normed_ref, out_ref, scratch,
+):
+    part = own_ref.shape[0]
+    tokens, width = y_ref.shape
+    heads = width // HEAD_DIM
+    core = place_ref[1]
+    scratch[pl.ds(pl.multiple_of(core * part, 32), part)] = own_ref[...]
+    scratch[pl.ds(pl.multiple_of((1 - core) * part, 32), part)] = other_ref[...]
+    factor = jnp.exp(log_ref[0:1])
+    carried = jnp.concatenate(
+        [
+            near_ref[h * HEAD_DIM : (h + 1) * HEAD_DIM]
+            + factor[:, h : h + 1] * scratch[h * HEAD_DIM : (h + 1) * HEAD_DIM].astype(F32)
+            for h in range(heads)
+        ],
+        axis=0,
+    )
+    outer = exact(bcs_ref[:, STATE:], carried, ((1,), (1,))) * spread(jnp.exp(run_ref[...]), heads)
+    gated = (y_ref[...] + outer) * z_ref[...]
+    square = gated * gated
+    scales = jnp.concatenate(
+        [
+            jnp.broadcast_to(
+                lax.rsqrt(
+                    jnp.mean(square[:, h * HEAD_DIM : (h + 1) * HEAD_DIM], axis=1, keepdims=True) + 1e-05
+                ),
+                (tokens, HEAD_DIM),
+            )
+            for h in range(heads)
+        ],
+        axis=1,
+    )
+    normed = (gated * scales * gain_ref[...]).astype(BF)
+    normed_ref[...] = turned(normed).astype(BF)
+    blank = jnp.zeros((tokens, 64), BF)
+    planes = jnp.concatenate(
+        [
+            normed[:, :128],
+            normed[:, 128:256],
+            jnp.concatenate([normed[:, 256:], blank], axis=1),
+            jnp.concatenate([blank, normed[:, 256:]], axis=1),
+        ],
+        axis=0,
+    )
+    out_ref[...] = dot(select_ref[...], planes).astype(BF)
+
+
+def piece_kernel(steps, ix_ref, gate_ref, up_ref, down_ref, *rest):
+    outs, (held, in_sems, out_sems) = rest[: len(steps)], rest[len(steps) :]
+    span = gate_ref.shape[0] // 4
+    arrivals = []
+    for i, step in enumerate(steps):
+        block = pl.multiple_of(lax.rem(ix_ref[0] + step, 4) * span, span)
+        pairs = [
+            (gate_ref.at[pl.ds(block, span)], held.at[i, pl.ds(0, span)]),
+            (up_ref.at[pl.ds(block, span)], held.at[i, pl.ds(span, span)]),
+        ]
+        for b in range(span // LANES):
+            pairs.append(
+                (
+                    down_ref.at[:, pl.ds(pl.multiple_of(block + b * LANES, LANES), LANES)],
+                    held.at[i, pl.ds(2 * span + b * LANES, LANES)],
+                )
+            )
+        arrivals.append(
+            [pltpu.make_async_copy(p, q, in_sems.at[i, n]) for n, (p, q) in enumerate(pairs)]
+        )
+    for copies in arrivals:
+        for copy in copies:
+            copy.start()
+    departures = []
+    for i, copies in enumerate(arrivals):
+        for copy in copies:
+            copy.wait()
+        departures.append(pltpu.make_async_copy(held.at[i], outs[i], out_sems.at[i]))
+        departures[i].start()
+    for copy in departures:
+        copy.wait()
+
+
+def weight_pieces(steps, ix, gate, up, down):
+    span = gate.shape[0] // 4
+    count = len(steps)
+    whole = pl.BlockSpec(memory_space=pltpu.HBM)
+    return pl.pallas_call(
+        functools.partial(piece_kernel, steps),
+        out_shape=[jax.ShapeDtypeStruct((3 * span, LANES), BF)] * count,
+        in_specs=[pl.BlockSpec(memory_space=pltpu.SMEM), whole, whole, whole],
+        out_specs=[whole] * count,
+        scratch_shapes=[
+            pltpu.VMEM((count, 3 * span, LANES), BF),
+            pltpu.SemaphoreType.DMA((count, 2 + span // LANES)),
+            pltpu.SemaphoreType.DMA((count,)),
+        ],
+        compiler_params=pltpu.CompilerParams(vmem_limit_bytes=60 << 20),
+    )(ix, gate, up, down)
+
+
+def mix_kernel(pick_ref, rows_ref, gates_ref, half_ref, out_ref):
+    tokens = gates_ref.shape[1]
+    picked = dot(pick_ref[...], rows_ref[...])
+    totals = [0.0, 0.0, 0.0]
+    for k in range(2):
+        gate = column(gates_ref[k : k + 1])
+        for plane in range(3):
+            start = (plane * 2 + k) * tokens
+            one = picked[start : start + tokens]
+            if plane == 2:
+                one = jnp.where(half_ref[:, k : k + 1] > 0.5, one[:, 64:], one[:, :64])
+            totals[plane] = totals[plane] + gate * one
+    for plane in range(3):
+        size = min(LANES, out_ref.shape[0] - plane * LANES)
+        out_ref[plane * LANES : plane * LANES + size] = totals[plane].T.astype(BF)
+
+
+def gate_up_kernel(
+    ix_ref, rows_ref, gate_ref, up_ref, w1_ref, w2_ref, w3_ref, out_ref, g_ref, held, sems
+):
+    span = gate_ref.shape[0] // 4
+    block = pl.multiple_of(ix_ref[0] * span, span)
+    pairs = [
+        (rows_ref, g_ref),
+        (gate_ref.at[pl.ds(block, span)], held.at[0, pl.ds(0, span)]),
+        (up_ref.at[pl.ds(block, span)], held.at[0, pl.ds(span, span)]),
+    ]
+    for s, w_ref in enumerate((w1_ref, w2_ref, w3_ref)):
+        pairs.append((w_ref.at[pl.ds(0, 2 * span)], held.at[s + 1]))
+    copies = [pltpu.make_async_copy(p, q, sems.at[n]) for n, (p, q) in enumerate(pairs)]
+    for copy in copies:
+        copy.start()
+    copies[0].wait()
+    rows = 2 * 192
+    wide = [jnp.concatenate([g_ref[y, :rows], g_ref[y, rows : 2 * rows]], axis=1) for y in range(4)]
+    slim = []
+    for y in range(4):
+        packed = g_ref[y, 2 * rows :]
+        slim.append(jnp.concatenate([packed[:, :64], packed[:, 64:]], axis=0))
+    pairs = [jnp.concatenate([slim[0], slim[1]], axis=1), jnp.concatenate([slim[2], slim[3]], axis=1)]
+    copies[1].wait()
+    for s in range(4):
+        target = lax.rem(ix_ref[0] - s + 4, 4)
+        copies[s + 2].wait()
+
+        def weight(start, size):
+            return jnp.concatenate(
+                [held[s, start : start + size], held[s, span + start : span + start + size]], axis=1
+            )
+
+        total = dot(wide[0], weight(0, 256))
+        for y in range(1, 4):
+            total += dot(wide[y], weight(y * 320, 256))
+        for p in range(2):
+            low, high = weight(p * 640 + 256, 64), weight(p * 640 + 576, 64)
+            total += dot(pairs[p], jnp.concatenate([low, high], axis=0))
+        out_ref[target, :rows] = total[:, :LANES].astype(BF)
+        out_ref[target, rows:] = total[:, LANES:].astype(BF)
+
+
+def hidden_kernel(p_ref, out_ref):
+    rows = p_ref.shape[1] // 2
+    total = p_ref[0].astype(F32)
+    for i in range(1, 4):
+        total += p_ref[i].astype(F32)
+    gate, up = total[:rows], total[rows:]
+    hidden = (silu(gate) * up).astype(BF)
+    for i in range(4):
+        out_ref[i] = hidden
+
+
+def down_kernel(ix_ref, rows_ref, down_ref, w1_ref, w2_ref, w3_ref, out_ref, h_ref, own_ref, held, sems):
+    rows = h_ref.shape[1]
+    half = rows // 2
+    span = held.shape[1]
+    block = pl.multiple_of(ix_ref[0] * span, span)
+    pairs = [(rows_ref, h_ref), (down_ref.at[:, pl.ds(block, span)], own_ref)]
+    for s, w_ref in enumerate((w1_ref, w2_ref, w3_ref)):
+        pairs.append((w_ref.at[pl.ds(2 * span, span)], held.at[s]))
+    copies = [pltpu.make_async_copy(p, q, sems.at[n]) for n, (p, q) in enumerate(pairs)]
+    for copy in copies:
+        copy.start()
+    copies[0].wait()
+    hid = [h_ref[lax.rem(ix_ref[0] - s + 4, 4)] for s in range(4)]
+
+    def weight(s, start):
+        if s == 0:
+            return own_ref[:, start : start + 256]
+        return jnp.concatenate(
+            [held[s - 1, start : start + 128], held[s - 1, start + 128 : start + 256]], axis=1
+        )
+
+    full = 0.0
+    for pair in ((0, 1), (2, 3)):
+        for s in pair:
+            copies[s + 1].wait()
+        both = jnp.concatenate([hid[s] for s in pair], axis=1)
+        full += jnp.concatenate(
+            [
+                dot(both, jnp.concatenate([weight(s, b * 256) for s in pair], axis=0))
+                for b in range(span // 256)
+            ],
+            axis=1,
+        )
+    for y in range(4):
+        own = full[:, y * 320 : (y + 1) * 320]
+        out_ref[y, :rows] = own[:, :128].astype(BF)
+        out_ref[y, rows : 2 * rows] = own[:, 128:256].astype(BF)
+        last = own[:, 256:]
+        out_ref[y, 2 * rows :] = jnp.concatenate([last[:half], last[half:]], axis=1).astype(BF)
+
+
+def expert_call(kernel, shape, ix, operands, scratch):
+    return pl.pallas_call(
+        kernel,
+        out_shape=jax.ShapeDtypeStruct(shape, BF),
+        in_specs=[pl.BlockSpec(memory_space=pltpu.SMEM)]
+        + [pl.BlockSpec(memory_space=pltpu.HBM)] * len(operands),
+        out_specs=pl.BlockSpec(memory_space=pltpu.VMEM),
+        scratch_shapes=scratch,
+        compiler_params=pltpu.CompilerParams(vmem_limit_bytes=60 << 20),
+    )(ix, *operands)
+
+
+def body(
+    seq_x,
+    z_gate,
+    bc_in,
+    conv_x,
+    conv_bc,
+    log_decay,
+    skip_d,
+    norm_gain,
+    routes,
+    route_gates,
+    placement,
+    gate_w,
+    up_w,
+    down_w,
+):
+    tokens, width = seq_x.shape
+    heads = width // HEAD_DIM
+    experts = placement.shape[0]
+    slots = experts * PIECE
+    ix = lax.axis_index("x").astype(jnp.int32)
+    place = jnp.stack([lax.axis_index(NEAR), lax.axis_index("c"), lax.axis_index("zh")]).astype(jnp.int32)
+
+    edge = kernel_call(edge_kernel, [((16, 640), BF)], seq_x.T, bc_in)
+    rim = lax.ppermute(edge, CTX, [(i, i + 1) for i in range(31)])
+    ixs = ix.reshape(1)
+    own = (gate_w[0], up_w[0], down_w[0])
+    pieces = dict(zip((1, 3, 2), weight_pieces((1, 3, 2), ixs, *own)))
+    swapped = {s: lax.ppermute(pieces[s], "x", [(i, (i + s) % 4) for i in range(4)]) for s in (1, 3)}
+    xs, bcs, run, turn, message = kernel_call(
+        state_kernel,
+        [
+            ((tokens, width), F32),
+            ((tokens, 2 * STATE), F32),
+            ((tokens, STATE), F32),
+            ((STATE, tokens), F32),
+            ((width + 16, STATE), BF),
+        ],
+        seq_x.T,
+        bc_in,
+        rim,
+        conv_x,
+        conv_bc,
+        log_decay.T,
+        scratch=[pltpu.VMEM((STATE, tokens), F32)],
+    )
+    near = lax.all_gather(message, NEAR)
+    near, swapped[1], swapped[3] = lax.optimization_barrier((near, swapped[1], swapped[3]))
+    near_carried, near_log, group = kernel_call(
+        near_kernel,
+        [((width, STATE), F32), ((8, STATE), F32), ((width // 2 + 16, STATE), BF)],
+        place,
+        near,
+        scalars=1,
+        scratch=[pltpu.VMEM((width, STATE), BF)],
+    )
+    fars = lax.all_gather(group, "zh")
+    turn, group, *owned = lax.optimization_barrier((turn, group, routes, placement))
+    select = kernel_call(
+        select_kernel, [((slots, 4 * tokens), BF)], owned[0].T, owned[1].reshape(1, experts)
+    )
+    y_in, z_in = pl.pallas_call(
+        inner_kernel,
+        out_shape=[jax.ShapeDtypeStruct((tokens, width), F32)] * 2,
+        in_specs=[pl.BlockSpec(memory_space=pltpu.VMEM)] * 4
+        + [pl.BlockSpec(memory_space=pltpu.SMEM), pl.BlockSpec(memory_space=pltpu.VMEM)],
+        out_specs=[pl.BlockSpec(memory_space=pltpu.VMEM)] * 2,
+        compiler_params=pltpu.CompilerParams(vmem_limit_bytes=20 << 20),
+    )(xs, bcs, run, turn, skip_d, z_gate.T)
+    far = kernel_call(far_kernel, [((width // 2, STATE), BF)], place, fars, scalars=1)
+    other = lax.ppermute(far, "c", [(0, 1), (1, 0)])
+    normed, outgoing = kernel_call(
+        finish_kernel,
+        [((width, tokens), BF), ((slots, LANES), BF)],
+        place,
+        far,
+        other,
+        near_carried,
+        near_log,
+        bcs,
+        run,
+        y_in,
+        z_in,
+        norm_gain.reshape(1, width),
+        select,
+        scalars=1,
+        scratch=[pltpu.VMEM((width, STATE), BF)],
+    )
+    normed, *own = lax.optimization_barrier((normed, routes, placement))
+    swapped[2] = lax.ppermute(pieces[2], "x", [(i, (i + 2) % 4) for i in range(4)])
+    pick, half = kernel_call(
+        pick_kernel,
+        [((6 * tokens, slots), BF), ((tokens, 2), F32)],
+        own[0].T,
+        own[1].reshape(1, experts),
+    )
+    arrived = lax.all_to_all(outgoing.reshape(experts, PIECE, LANES), CTX, 0, 0, tiled=True)
+    rows = (
+        arrived[:, : GROUPS * HALF]
+        .reshape(experts, GROUPS, HALF, LANES)
+        .transpose(1, 0, 2, 3)
+        .reshape(GROUPS * experts * HALF, LANES)
+    )
+    wide = lax.all_gather(rows, "y")
+    count = 2 * experts * HALF
+    weights = [swapped[1], swapped[2], swapped[3]]
+    span = gate_w.shape[1] // 4
+    across = pl.BlockSpec((span, LANES), lambda i, b: (b[0], 0))
+    along = pl.BlockSpec((LANES, span), lambda i, b: (0, b[0]))
+    parts = expert_call(
+        gate_up_kernel,
+        (4, 2 * count, LANES),
+        ixs,
+        (wide, gate_w[0], up_w[0], *weights),
+        [
+            pltpu.VMEM(wide.shape, BF),
+            pltpu.VMEM((4, 2 * span, LANES), BF),
+            pltpu.SemaphoreType.DMA((6,)),
+        ],
+    )
     parts = lax.all_to_all(parts, "x", 0, 0, tiled=True)
     hidden = kernel_call(hidden_kernel, [((4, count, LANES), BF)], parts)
     hiddens = lax.all_to_all(hidden, "x", 0, 0, tiled=True)
-    downs = kernel_call(down_kernel, [((4, count * 5 // 2, LANES), BF)], ixs, hiddens, *weights, scalars=1)
+    downs = expert_call(
+        down_kernel,
+        (4, count * 5 // 2, LANES),
+        ixs,
+        (hiddens, down_w[0], *weights),
+        [
+            pltpu.VMEM(hiddens.shape, BF),
+            pltpu.VMEM((LANES, span), BF),
+            pltpu.VMEM((3, span, LANES), BF),
+            pltpu.SemaphoreType.DMA((5,)),
+        ],
+    )
     downs = lax.all_to_all(downs, "y", 0, 0, tiled=True)
     result = jnp.sum(downs.astype(F32), axis=0).astype(BF)
     result = result.reshape(GROUPS, experts, HALF, LANES).transpose(1, 0, 2, 3)

time: 189 us -> 195 us (1.032)
  Pallas kernels: 18.2 us -> 21.5 us
  blocking collectives: 86 us -> 88.7 us
    pallas_call x0 -> x2, Pallas kernels: none -> 8.51 us  [expert_call(): pl.pallas_call(kernel, out_shape=jax.ShapeDtypeStruct(shape, BF), in_spec...]
    pallas_call x11 -> x9, Pallas kernels: 13 us -> 8.44 us  [kernel_call(): pl.pallas_call(kernel, out_shape=shapes, in_specs=specs, out_specs=[pl.Bl...]
where the time goes in v5:
time: 195 us
  blocking collectives  88.7 us (45%)
  waiting for transfers between devices  43.4 us (22%)
  starting transfers between devices  37.5 us (19%)
  Pallas kernels  21.5 us (11%)
  local copies, waits for them, and re-layouts  2.28 us (1%)
    all_gather x1, blocking collectives, body(): fars = lax.all_gather(group, 'zh')  23.6 us
    all_to_all x1, waiting for transfers between devices, body(): lax.all_to_all(result, CTX, 0, 0, tiled=True).reshape(slots, LANES)  21.4 us
    all_to_all x1, waiting for transfers between devices, body(): lax.all_to_all(outgoing.reshape(experts, PIECE, LANES), CTX, 0, 0, tiled=...  18.2 us
    all_gather x1, blocking collectives, body(): near = lax.all_gather(message, NEAR)  15.4 us
    all_gather x1, blocking collectives, body(): wide = lax.all_gather(rows, 'y')  13.7 us
    all_to_all x1, blocking collectives, body(): parts = lax.all_to_all(parts, 'x', 0, 0, tiled=True)  13.5 us
    all_to_all x1, blocking collectives, body(): downs = lax.all_to_all(downs, 'y', 0, 0, tiled=True)  13.2 us
    all_to_all x1, starting transfers between devices, body(): lax.all_to_all(result, CTX, 0, 0, tiled=True).reshape(slots, LANES)  10.3 us
  transfers between devices with their start and end apart: 7, of which 3 were waited for; matrix products, arithmetic and copies ran while one was open for 0% of the time, Pallas kernels for 2%

profile of v5, /device:TPU:1, one launch (start us, length us, event | category | flops | bytes accessed | tf_op | source)
XLA Modules:
  0.0 194.7 jit_solution(773074838546037364)
XLA Ops:
  0.7 3.1 %shard_map.151 = (bf16[3840,128]{1,0:T(8,128)(2,1)}, bf16[3840,128]{1,0:T(8,128)(2,1)}, bf16[3840,128]{1,0:T(8,128)(2,1)}) custom-call(s32[1]{0:T(128)} %bitcast.6.ix_ref, bf16[5120,128]{1,0:T(8,128)(2,1)} %bitcast.41, bf16[5120,128]{1,0:T(8,128)(2,1)} %bitcast.43, bf16[128,5120]{1,0:T(8,128)(2,1)} %bitcast.39), custom_call_target="tpu_custom_call" | custom-call | tf_op jit(solution)/shard_map/pallas_call | solution.py:730
  3.8 4.1 %collective-permute-start.1 = (bf16[3840,128]{1,0:T(8,128)(2,1)}, bf16[3840,128]{1,0:T(8,128)(2,1)S(1)}, u32[]{:S(2)}, u32[]{:S(2)}) collective-permute-start(bf16[3840,128]{1,0:T(8,128)(2,1)} %get-tuple-element.29), channel_id=1, source_target_pairs={{0,4},{4,8},{8,12},{12,0},{1,5},{5,9},{9,13},{13,1},{2,6},{6,10},{... | collective-permute-start | bytes 2949128 | tf_op jit(solution)/shard_map/ppermute | solution.py:896
  7.9 3.2 %collective-permute-start.2 = (bf16[3840,128]{1,0:T(8,128)(2,1)}, bf16[3840,128]{1,0:T(8,128)(2,1)S(1)}, u32[]{:S(2)}, u32[]{:S(2)}) collective-permute-start(bf16[3840,128]{1,0:T(8,128)(2,1)} %get-tuple-element.30), channel_id=1, source_target_pairs={{0,12},{4,0},{8,4},{12,8},{1,13},{5,1},{9,5},{13,9},{2,14},{6,2},{... | collective-permute-start | bytes 2949128 | tf_op jit(solution)/shard_map/ppermute | solution.py:896
  11.2 4.9 %collective-permute-start = (bf16[16,640]{1,0:T(8,128)(2,1)S(1)}, bf16[16,640]{1,0:T(8,128)(2,1)S(1)}, u32[]{:S(2)}, u32[]{:S(2)}) collective-permute-start(bf16[16,640]{1,0:T(8,128)(2,1)S(1)} %shard_map.149), channel_id=1, source_target_pairs={{0,16},{16,32},{32,48},{48,64},{64,80},{80,96},{96,112},{112,128},... | collective-permute-start | bytes 61448 | tf_op jit(solution)/shard_map/ppermute | solution.py:892
  16.2 3.8 %collective-permute-done.rim_ref = bf16[16,640]{1,0:T(8,128)(2,1)S(1)} collective-permute-done((bf16[16,640]{1,0:T(8,128)(2,1)S(1)}, bf16[16,640]{1,0:T(8,128)(2,1)S(1)}, u32[]{:S(2)}, u32[]{:S(2)}) %collective-permute-start) | collective-permute-done | bytes 20512 | tf_op jit(solution)/shard_map/ppermute | solution.py:892
  20.0 1.0 shard_map.150
  21.0 15.4 %all-gather = bf16[2688,128]{1,0:T(8,128)(2,1)S(1)} all-gather(bf16[336,128]{1,0:T(8,128)(2,1)S(1)} %get-tuple-element.28), channel_id=2, replica_groups=mesh['zh'=4,'zl'=4,'c'=2,'x'=4,'y'=4] {'zl','c'}, dimensions={0}, use_global_device_ids=true | all-gather | bytes 774144 | tf_op jit(solution)/shard_map/all_gather | solution.py:914
  36.4 0.8 shard_map.152
  37.2 23.6 %all-gather.1 = bf16[704,128]{1,0:T(8,128)(2,1)S(1)} all-gather(bf16[176,128]{1,0:T(8,128)(2,1)S(1)} %get-tuple-element.32), channel_id=3, replica_groups=mesh['zh'=4,'zl'=4,'c'=2,'x'=4,'y'=4] {'zh'}, dimensions={0}, use_global_device_ids=true | all-gather | bytes 225280 | tf_op jit(solution)/shard_map/all_gather | solution.py:924
  60.8 0.7 shard_map.153.own_ref
  61.5 4.4 %collective-permute-start.3 = (bf16[160,128]{1,0:T(8,128)(2,1)S(1)}, bf16[160,128]{1,0:T(8,128)(2,1)S(1)}, u32[]{:S(2)}, u32[]{:S(2)}) collective-permute-start(bf16[160,128]{1,0:T(8,128)(2,1)S(1)} %shard_map.153.own_ref), channel_id=1, source_target_pairs={{0,16},{16,0},{1,17},{17,1},{2,18},{18,2},{3,19},{19,3},{4,20},{20... | collective-permute-start | bytes 122888 | tf_op jit(solution)/shard_map/ppermute | solution.py:938
  65.9 1.1 shard_map.155.select_ref
  67.1 1.5 shard_map.154
  68.6 2.6 %shard_map.156 = (bf16[320,128]{1,0:T(8,128)(2,1)}, bf16[1024,128]{1,0:T(8,128)(2,1)}) custom-call(s32[3]{0:T(128)S(1)} %pad_add_fusion.place_ref, bf16[160,128]{1,0:T(8,128)(2,1)S(1)} %shard_map.153.own_ref, bf16[160,128]{1,0:T(8,128)(2,1)S(1)} %collective-permute-done.3.other_ref, f32[320,128]{1,0:T(8,128)S(1)} %get-tuple-element.33.near_ref, ...), custom_call_target="tpu_custom_call" | custom-call | tf_op jit(solution)/shard_map/pallas_call | solution.py:34
  71.2 6.9 %all-to-all-start = ((bf16[32,32,128]{2,1,0:T(8,128)(2,1)}), bf16[32,32,128]{2,1,0:T(8,128)(2,1)S(1)}, u32[]{:S(2)}, u32[]{:S(2)}) async-start(bf16[32,32,128]{2,1,0:T(8,128)(2,1)} %bitcast.17), calls=%async_computation | async-start | bytes 524288 | tf_op jit(solution)/shard_map/all_to_all | solution.py:964
  78.1 3.8 %collective-permute-start.4 = (bf16[3840,128]{1,0:T(8,128)(2,1)S(1)}, bf16[3840,128]{1,0:T(8,128)(2,1)S(1)}, u32[]{:S(2)}, u32[]{:S(2)}) collective-permute-start(bf16[3840,128]{1,0:T(8,128)(2,1)S(1)} %copy-done.14), channel_id=1, source_target_pairs={{0,8},{4,12},{8,0},{12,4},{1,9},{5,13},{9,1},{13,5},{2,10},{6,14},... | collective-permute-start | bytes 2949128 | tf_op jit(solution)/shard_map/ppermute | solution.py:957
  81.9 18.2 %all-to-all-done = bf16[32,32,128]{2,1,0:T(8,128)(2,1)S(1)} async-done(((bf16[32,32,128]{2,1,0:T(8,128)(2,1)}), bf16[32,32,128]{2,1,0:T(8,128)(2,1)S(1)}, u32[]{:S(2)}, u32[]{:S(2)}) %all-to-all-start) | async-done | bytes 262176 | tf_op jit(solution)/shard_map/all_to_all | solution.py:964
  100.2 0.1 copy.21
  100.4 13.7 %all_gather.19.rows_ref = bf16[4,960,128]{2,1,0:T(8,128)(2,1)} all-gather(bf16[1,960,128]{2,1,0:T(8,128)(2,1)S(1)} %all_gather_reshape.3), channel_id=1, replica_groups=mesh['zh'=4,'zl'=4,'c'=2,'x'=4,'y'=4] {'y'}, dimensions={0}, use_global_device_ids=true | all-gather | bytes 1228800 | tf_op jit(solution)/shard_map/all_gather | solution.py:971
  114.1 1.0 copy-done.12
  115.1 5.4 %shard_map.158 = bf16[4,768,128]{2,1,0:T(8,128)(2,1)} custom-call(s32[1]{0:T(128)} %bitcast.6.ix_ref, bf16[4,960,128]{2,1,0:T(8,128)(2,1)} %all_gather.19.rows_ref, bf16[5120,128]{1,0:T(8,128)(2,1)} %bitcast.42, bf16[5120,128]{1,0:T(8,128)(2,1)} %bitcast.44, bf16[3840,128]{1,0:T(8,128)(2,1)} %copy-done.10, bf16[3840,128]{1,0:T(8,128)(2,1)} %copy-done.12, ...), custom_call_target="tpu_custom_call" | custom-call | tf_op jit(solution)/shard_map/pallas_call | solution.py:857
  120.5 13.5 %all_to_all.25.p_ref = bf16[4,768,128]{2,1,0:T(8,128)(2,1)S(1)} all-to-all(bf16[4,768,128]{2,1,0:T(8,128)(2,1)} %shard_map.158), channel_id=1, replica_groups=mesh['zh'=4,'zl'=4,'c'=2,'x'=4,'y'=4] {'x'}, dimensions={0} | all-to-all | bytes 1572864 | tf_op jit(solution)/shard_map/all_to_all | solution.py:988
  133.9 0.1 shard_map.159
  134.1 9.3 %all_to_all.26.rows_ref = bf16[4,384,128]{2,1,0:T(8,128)(2,1)} all-to-all(bf16[4,384,128]{2,1,0:T(8,128)(2,1)S(1)} %shard_map.159), channel_id=1, replica_groups=mesh['zh'=4,'zl'=4,'c'=2,'x'=4,'y'=4] {'x'}, dimensions={0} | all-to-all | bytes 786432 | tf_op jit(solution)/shard_map/all_to_all | solution.py:990
  143.4 3.1 %shard_map.160 = bf16[4,960,128]{2,1,0:T(8,128)(2,1)} custom-call(s32[1]{0:T(128)} %bitcast.6.ix_ref, bf16[4,384,128]{2,1,0:T(8,128)(2,1)} %all_to_all.26.rows_ref, bf16[128,5120]{1,0:T(8,128)(2,1)} %bitcast.40, bf16[3840,128]{1,0:T(8,128)(2,1)} %copy-done.10, bf16[3840,128]{1,0:T(8,128)(2,1)} %copy-done.12, bf16[3840,128]{1,0:T(8,128)(2,1)} %copy-done.11), custom_call_target="tpu_custom_call" | custom-call | tf_op jit(solution)/shard_map/pallas_call | solution.py:857
  146.5 13.2 %all_to_all.27 = bf16[4,960,128]{2,1,0:T(8,128)(2,1)S(1)} all-to-all(bf16[4,960,128]{2,1,0:T(8,128)(2,1)} %shard_map.160), channel_id=1, replica_groups=mesh['zh'=4,'zl'=4,'c'=2,'x'=4,'y'=4] {'y'}, dimensions={0} | all-to-all | bytes 1966080 | tf_op jit(solution)/shard_map/all_to_all | solution.py:1003
  159.7 0.2 reduce_sum.12
  160.2 0.7 pad.4.clone
  161.0 10.3 %all-to-all-start.4 = ((bf16[32,32,128]{2,1,0:T(8,128)(2,1)}), bf16[32,32,128]{2,1,0:T(8,128)(2,1)S(1)}, u32[]{:S(2)}, u32[]{:S(2)}) async-start(bf16[32,32,128]{2,1,0:T(8,128)(2,1)} %pad.4.clone), calls=%async_computation.4 | async-start | bytes 524288 | tf_op jit(solution)/shard_map/all_to_all | solution.py:1007
  171.3 0.6 shard_map.157
  171.9 21.4 %all-to-all-done.4 = bf16[32,32,128]{2,1,0:T(8,128)(2,1)S(1)} async-done(((bf16[32,32,128]{2,1,0:T(8,128)(2,1)}), bf16[32,32,128]{2,1,0:T(8,128)(2,1)S(1)}, u32[]{:S(2)}, u32[]{:S(2)}) %all-to-all-start.4) | async-done | bytes 262176 | tf_op jit(solution)/shard_map/all_to_all | solution.py:1007
  193.3 1.4 shard_map.161
  (41 shorter events, 0.7 us)
Async XLA Ops:
  0.6 10.5 %copy-start = (bf16[128,320]{0,1:T(8,128)(2,1)S(1)}, bf16[128,320]{0,1:T(8,128)(2,1)}, u32[]{:S(2)}) copy-start(bf16[128,320]{0,1:T(8,128)(2,1)} %param.14) | copy-start | bytes 245764
  0.6 10.5 %copy-start.1 = (bf16[128,256]{1,0:T(8,128)(2,1)S(1)}, bf16[128,256]{1,0:T(8,128)(2,1)}, u32[]{:S(2)}) copy-start(bf16[128,256]{1,0:T(8,128)(2,1)} %bc_ref.3) | copy-start | bytes 196612
  0.7 19.3 %copy-start.3 = (f32[4,320]{1,0:T(4,128)S(1)}, f32[4,320]{1,0:T(4,128)}, u32[]{:S(2)}) copy-start(f32[4,320]{1,0:T(4,128)} %cx_ref.1) | copy-start | bytes 15364
  0.7 19.3 %copy-start.4 = (f32[4,256]{1,0:T(4,128)S(1)}, f32[4,256]{1,0:T(4,128)}, u32[]{:S(2)}) copy-start(f32[4,256]{1,0:T(4,128)} %cbc_ref.1) | copy-start | bytes 12292
  0.7 19.3 %copy-start.5 = (f32[128,5]{0,1:T(8,128)S(1)}, f32[128,5]{0,1:T(8,128)}, u32[]{:S(2)}) copy-start(f32[128,5]{0,1:T(8,128)} %param.19) | copy-start | bytes 7684
  3.8 62.1 %copy-start.13 = (f32[320]{0:T(512)S(1)}, f32[320]{0:T(512)}, u32[]{:S(2)}) copy-start(f32[320]{0:T(512)} %param.21) | copy-start | bytes 3844
  3.8 62.1 %copy-start.7 = (s32[128,2]{0,1:T(2,128)S(1)}, s32[128,2]{0,1:T(2,128)}, u32[]{:S(2)}) copy-start(s32[128,2]{0,1:T(2,128)} %param.22) | copy-start | bytes 3076
  3.8 62.1 %copy-start.9 = (s32[32]{0:T(128)S(1)}, s32[32]{0:T(128)}, u32[]{:S(2)}) copy-start(s32[32]{0:T(128)} %param.24) | copy-start | bytes 388
  3.8 32.5 %collective-permute-start.1 = (bf16[3840,128]{1,0:T(8,128)(2,1)}, bf16[3840,128]{1,0:T(8,128)(2,1)S(1)}, u32[]{:S(2)}, u32[]{:S(2)}) collective-permute-start(bf16[3840,128]{1,0:T(8,128)(2,1)} %get-tuple-element.29), channel_id=1, source_target_pairs={{0,4},{4,8},{8,12},{12,0},{1,5},{5,9},{9,13},{13,1},{2,6},{6,10},{... | collective-permute-start | bytes 2949128 | tf_op jit(solution)/shard_map/ppermute | solution.py:896
  7.9 28.5 %collective-permute-start.2 = (bf16[3840,128]{1,0:T(8,128)(2,1)}, bf16[3840,128]{1,0:T(8,128)(2,1)S(1)}, u32[]{:S(2)}, u32[]{:S(2)}) collective-permute-start(bf16[3840,128]{1,0:T(8,128)(2,1)} %get-tuple-element.30), channel_id=1, source_target_pairs={{0,12},{4,0},{8,4},{12,8},{1,13},{5,1},{9,5},{13,9},{2,14},{6,2},{... | collective-permute-start | bytes 2949128 | tf_op jit(solution)/shard_map/ppermute | solution.py:896
  11.2 8.8 %collective-permute-start = (bf16[16,640]{1,0:T(8,128)(2,1)S(1)}, bf16[16,640]{1,0:T(8,128)(2,1)S(1)}, u32[]{:S(2)}, u32[]{:S(2)}) collective-permute-start(bf16[16,640]{1,0:T(8,128)(2,1)S(1)} %shard_map.149), channel_id=1, source_target_pairs={{0,16},{16,32},{32,48},{48,64},{64,80},{80,96},{96,112},{112,128},... | collective-permute-start | bytes 61448 | tf_op jit(solution)/shard_map/ppermute | solution.py:892
  21.0 46.1 %copy-start.2 = (bf16[128,320]{0,1:T(8,128)(2,1)S(1)}, bf16[128,320]{0,1:T(8,128)(2,1)}, u32[]{:S(2)}) copy-start(bf16[128,320]{0,1:T(8,128)(2,1)} %param.15) | copy-start | bytes 245764
  21.0 46.1 %copy-start.8 = (f32[5]{0:T(128)S(1)}, f32[5]{0:T(128)}, u32[]{:S(2)}) copy-start(f32[5]{0:T(128)} %skip_ref.1) | copy-start | bytes 64
  36.4 32.2 %copy-start.10 = (bf16[3840,128]{1,0:T(8,128)(2,1)}, bf16[3840,128]{1,0:T(8,128)(2,1)S(1)}, u32[]{:S(2)}) copy-start(bf16[3840,128]{1,0:T(8,128)(2,1)S(1)} %collective-permute-done.1.w1_ref) | copy-start | bytes 2949124
  36.4 32.2 %copy-start.11 = (bf16[3840,128]{1,0:T(8,128)(2,1)}, bf16[3840,128]{1,0:T(8,128)(2,1)S(1)}, u32[]{:S(2)}) copy-start(bf16[3840,128]{1,0:T(8,128)(2,1)S(1)} %collective-permute-done.2.w3_ref) | copy-start | bytes 2949124
  61.5 7.1 %collective-permute-start.3 = (bf16[160,128]{1,0:T(8,128)(2,1)S(1)}, bf16[160,128]{1,0:T(8,128)(2,1)S(1)}, u32[]{:S(2)}, u32[]{:S(2)}) collective-permute-start(bf16[160,128]{1,0:T(8,128)(2,1)S(1)} %shard_map.153.own_ref), channel_id=1, source_target_pairs={{0,16},{16,0},{1,17},{17,1},{2,18},{18,2},{3,19},{19,3},{4,20},{20... | collective-permute-start | bytes 122888 | tf_op jit(solution)/shard_map/ppermute | solution.py:938
  68.6 9.5 %copy-start.14 = (bf16[3840,128]{1,0:T(8,128)(2,1)S(1)}, bf16[3840,128]{1,0:T(8,128)(2,1)}, u32[]{:S(2)}) copy-start(bf16[3840,128]{1,0:T(8,128)(2,1)} %get-tuple-element.51) | copy-start | bytes 2949124
  71.2 28.9 %all-to-all-start = ((bf16[32,32,128]{2,1,0:T(8,128)(2,1)}), bf16[32,32,128]{2,1,0:T(8,128)(2,1)S(1)}, u32[]{:S(2)}, u32[]{:S(2)}) async-start(bf16[32,32,128]{2,1,0:T(8,128)(2,1)} %bitcast.17), calls=%async_computation | async-start | bytes 524288 | tf_op jit(solution)/shard_map/all_to_all | solution.py:964
  78.1 36.0 %collective-permute-start.4 = (bf16[3840,128]{1,0:T(8,128)(2,1)S(1)}, bf16[3840,128]{1,0:T(8,128)(2,1)S(1)}, u32[]{:S(2)}, u32[]{:S(2)}) collective-permute-start(bf16[3840,128]{1,0:T(8,128)(2,1)S(1)} %copy-done.14), channel_id=1, source_target_pairs={{0,8},{4,12},{8,0},{12,4},{1,9},{5,13},{9,1},{13,5},{2,10},{6,14},... | collective-permute-start | bytes 2949128 | tf_op jit(solution)/shard_map/ppermute | solution.py:957
  114.1 1.0 copy-start.12
  160.0 33.3 %copy-start.6 = (f32[128,2]{0,1:T(2,128)S(1)}, f32[128,2]{0,1:T(2,128)}, u32[]{:S(2)}) copy-start(f32[128,2]{0,1:T(2,128)} %param.23) | copy-start | bytes 3076
  161.0 32.3 %all-to-all-start.4 = ((bf16[32,32,128]{2,1,0:T(8,128)(2,1)}), bf16[32,32,128]{2,1,0:T(8,128)(2,1)S(1)}, u32[]{:S(2)}, u32[]{:S(2)}) async-start(bf16[32,32,128]{2,1,0:T(8,128)(2,1)} %pad.4.clone), calls=%async_computation.4 | async-start | bytes 524288 | tf_op jit(solution)/shard_map/all_to_all | solution.py:1007

commit v6 on v3

--- a/solution.py
+++ b/solution.py
@@ -392,7 +392,7 @@
     for b in range(5):
         weight = []
         for w_ref in (w0_ref, w1_ref, w2_ref, w3_ref):
-            start = 2560 + b * 256
+            start = b * 256
             weight.append(
                 jnp.concatenate([w_ref[start : start + 128], w_ref[start + 128 : start + 256]], axis=1)
             )
@@ -404,6 +404,20 @@
         out_ref[y, rows : 2 * rows] = own[:, 128:256].astype(BF)
         last = own[:, 256:]
         out_ref[y, 2 * rows :] = jnp.concatenate([last[:half], last[half:]], axis=1).astype(BF)
+
+
+def expert_call(kernel, shape, ix, rows, pieces, piece_spec):
+    return pl.pallas_call(
+        kernel,
+        out_shape=jax.ShapeDtypeStruct(shape, BF),
+        grid_spec=pltpu.PrefetchScalarGridSpec(
+            num_scalar_prefetch=1,
+            grid=(1,),
+            in_specs=[pl.BlockSpec(rows.shape, lambda i, b: (0, 0, 0))] + [piece_spec] * len(pieces),
+            out_specs=pl.BlockSpec(shape, lambda i, b: (0, 0, 0)),
+        ),
+        compiler_params=pltpu.CompilerParams(vmem_limit_bytes=20 << 20),
+    )(ix, rows, *pieces)
 
 
 def body(
@@ -430,8 +444,8 @@
     place = jnp.stack([lax.axis_index(NEAR), lax.axis_index("c"), lax.axis_index("zh")]).astype(jnp.int32)
 
     edge = kernel_call(edge_kernel, [((16, 640), BF)], seq_x.T, bc_in)
+    ixs, edge = lax.optimization_barrier((ix.reshape(1), edge))
     rim = lax.ppermute(edge, CTX, [(i, i + 1) for i in range(31)])
-    ixs = ix.reshape(1)
     own = (gate_w[0], up_w[0], down_w[0])
     pieces = dict(zip((1, 3, 2, 0), weight_pieces((1, 3, 2, 0), ixs, *own)))
     swapped = {s: lax.ppermute(pieces[s], "x", [(i, (i + s) % 4) for i in range(4)]) for s in (1, 3)}
@@ -512,11 +526,25 @@
     wide = lax.all_gather(rows, "y")
     count = 2 * experts * HALF
     weights = [pieces[0], swapped[1], swapped[2], swapped[3]]
-    parts = kernel_call(gate_up_kernel, [((4, 2 * count, LANES), BF)], ixs, wide, *weights, scalars=1)
+    parts = expert_call(
+        gate_up_kernel,
+        (4, 2 * count, LANES),
+        ixs,
+        wide,
+        weights,
+        pl.BlockSpec((2 * gate_w.shape[1] // 4, LANES), lambda i, b: (0, 0)),
+    )
     parts = lax.all_to_all(parts, "x", 0, 0, tiled=True)
     hidden = kernel_call(hidden_kernel, [((4, count, LANES), BF)], parts)
     hiddens = lax.all_to_all(hidden, "x", 0, 0, tiled=True)
-    downs = kernel_call(down_kernel, [((4, count * 5 // 2, LANES), BF)], ixs, hiddens, *weights, scalars=1)
+    downs = expert_call(
+        down_kernel,
+        (4, count * 5 // 2, LANES),
+        ixs,
+        hiddens,
+        weights,
+        pl.BlockSpec((gate_w.shape[1] // 4, LANES), lambda i, b: (2, 0)),
+    )
     downs = lax.all_to_all(downs, "y", 0, 0, tiled=True)
     result = jnp.sum(downs.astype(F32), axis=0).astype(BF)
     result = result.reshape(GROUPS, experts, HALF, LANES).transpose(1, 0, 2, 3)

time: 189 us -> 190 us (level)
    pallas_call x11 -> x9, Pallas kernels: 13 us -> 8.42 us  [kernel_call(): pl.pallas_call(kernel, out_shape=shapes, in_specs=specs, out_specs=[pl.Bl...]
    pallas_call x0 -> x2, Pallas kernels: none -> 4.24 us  [expert_call(): pl.pallas_call(kernel, out_shape=jax.ShapeDtypeStruct(shape, BF), grid_sp...]
where the time goes in v6:
time: 190 us; the launch traced here: 189 us
  blocking collectives  85.7 us (45%)
  waiting for transfers between devices  43.6 us (23%)
  starting transfers between devices  37.9 us (20%)
  Pallas kernels  17.9 us (9%)
  local copies, waits for them, and re-layouts  3.05 us (2%)
    all_gather x1, blocking collectives, body(): fars = lax.all_gather(group, 'zh')  23.4 us
    all_to_all x1, waiting for transfers between devices, body(): lax.all_to_all(result, CTX, 0, 0, tiled=True).reshape(slots, LANES)  21.4 us
    all_to_all x1, waiting for transfers between devices, body(): lax.all_to_all(outgoing.reshape(experts, PIECE, LANES), CTX, 0, 0, tiled=...  18.4 us
    all_gather x1, blocking collectives, body(): near = lax.all_gather(message, NEAR)  15.4 us
    all_gather x1, blocking collectives, body(): wide = lax.all_gather(rows, 'y')  13.7 us
    all_to_all x1, blocking collectives, body(): parts = lax.all_to_all(parts, 'x', 0, 0, tiled=True)  12.8 us
    all_to_all x1, blocking collectives, body(): downs = lax.all_to_all(downs, 'y', 0, 0, tiled=True)  11.8 us
    all_to_all x1, starting transfers between devices, body(): lax.all_to_all(result, CTX, 0, 0, tiled=True).reshape(slots, LANES)  10.6 us
  transfers between devices with their start and end apart: 7, of which 3 were waited for; matrix products, arithmetic and copies ran while one was open for 0% of the time, Pallas kernels for 2%

profile of v6, /device:TPU:1, one launch (start us, length us, event | category | flops | bytes accessed | tf_op | source)
XLA Modules:
  0.0 189.4 jit_solution(6044108678923312398)
XLA Ops:
  0.6 0.9 copy-done.1
  1.5 0.8 copy-done.3
  2.5 3.8 %shard_map.151 = (bf16[3840,128]{1,0:T(8,128)(2,1)}, bf16[3840,128]{1,0:T(8,128)(2,1)}, bf16[3840,128]{1,0:T(8,128)(2,1)}, bf16[3840,128]{1,0:T(8,128)(2,1)}) custom-call(s32[1]{0:T(128)} %bitcast.4.ix_ref, bf16[5120,128]{1,0:T(8,128)(2,1)} %bitcast.39, bf16[5120,128]{1,0:T(8,128)(2,1)} %bitcast.40, bf16[128,5120]{1,0:T(8,128)(2,1)} %bitcast.41), custom_call_target="tpu_custom_call" | custom-call | tf_op jit(solution)/shard_map/pallas_call | solution.py:319
  6.3 4.1 %collective-permute-start.1 = (bf16[3840,128]{1,0:T(8,128)(2,1)}, bf16[3840,128]{1,0:T(8,128)(2,1)S(1)}, u32[]{:S(2)}, u32[]{:S(2)}) collective-permute-start(bf16[3840,128]{1,0:T(8,128)(2,1)} %get-tuple-element.34), channel_id=1, source_target_pairs={{0,4},{4,8},{8,12},{12,0},{1,5},{5,9},{9,13},{13,1},{2,6},{6,10},{... | collective-permute-start | bytes 2949128 | tf_op jit(solution)/shard_map/ppermute | solution.py:451
  10.4 3.2 %collective-permute-start.2 = (bf16[3840,128]{1,0:T(8,128)(2,1)}, bf16[3840,128]{1,0:T(8,128)(2,1)S(1)}, u32[]{:S(2)}, u32[]{:S(2)}) collective-permute-start(bf16[3840,128]{1,0:T(8,128)(2,1)} %get-tuple-element.35), channel_id=1, source_target_pairs={{0,12},{4,0},{8,4},{12,8},{1,13},{5,1},{9,5},{13,9},{2,14},{6,2},{... | collective-permute-start | bytes 2949128 | tf_op jit(solution)/shard_map/ppermute | solution.py:451
  13.6 4.9 %collective-permute-start = (bf16[16,640]{1,0:T(8,128)(2,1)S(1)}, bf16[16,640]{1,0:T(8,128)(2,1)S(1)}, u32[]{:S(2)}, u32[]{:S(2)}) collective-permute-start(bf16[16,640]{1,0:T(8,128)(2,1)S(1)} %shard_map.149), channel_id=1, source_target_pairs={{0,16},{16,32},{32,48},{48,64},{64,80},{80,96},{96,112},{112,128},... | collective-permute-start | bytes 61448 | tf_op jit(solution)/shard_map/ppermute | solution.py:448
  18.6 3.8 %collective-permute-done.rim_ref = bf16[16,640]{1,0:T(8,128)(2,1)S(1)} collective-permute-done((bf16[16,640]{1,0:T(8,128)(2,1)S(1)}, bf16[16,640]{1,0:T(8,128)(2,1)S(1)}, u32[]{:S(2)}, u32[]{:S(2)}) %collective-permute-start) | collective-permute-done | bytes 20512 | tf_op jit(solution)/shard_map/ppermute | solution.py:448
  22.4 1.0 shard_map.150
  23.4 15.4 %all-gather = bf16[2688,128]{1,0:T(8,128)(2,1)S(1)} all-gather(bf16[336,128]{1,0:T(8,128)(2,1)S(1)} %get-tuple-element.32), channel_id=2, replica_groups=mesh['zh'=4,'zl'=4,'c'=2,'x'=4,'y'=4] {'zl','c'}, dimensions={0}, use_global_device_ids=true | all-gather | bytes 774144 | tf_op jit(solution)/shard_map/all_gather | solution.py:469
  38.8 0.8 shard_map.152
  39.6 23.4 %all-gather.1 = bf16[704,128]{1,0:T(8,128)(2,1)S(1)} all-gather(bf16[176,128]{1,0:T(8,128)(2,1)S(1)} %get-tuple-element.37), channel_id=3, replica_groups=mesh['zh'=4,'zl'=4,'c'=2,'x'=4,'y'=4] {'zh'}, dimensions={0}, use_global_device_ids=true | all-gather | bytes 225280 | tf_op jit(solution)/shard_map/all_gather | solution.py:479
  63.0 0.7 shard_map.153.own_ref
  63.7 4.6 %collective-permute-start.3 = (bf16[160,128]{1,0:T(8,128)(2,1)S(1)}, bf16[160,128]{1,0:T(8,128)(2,1)S(1)}, u32[]{:S(2)}, u32[]{:S(2)}) collective-permute-start(bf16[160,128]{1,0:T(8,128)(2,1)S(1)} %shard_map.153.own_ref), channel_id=1, source_target_pairs={{0,16},{16,0},{1,17},{17,1},{2,18},{18,2},{3,19},{19,3},{4,20},{20... | collective-permute-start | bytes 122888 | tf_op jit(solution)/shard_map/ppermute | solution.py:493
  68.3 1.1 shard_map.155.select_ref
  69.5 1.5 shard_map.154
  71.0 2.6 %shard_map.156 = (bf16[320,128]{1,0:T(8,128)(2,1)}, bf16[1024,128]{1,0:T(8,128)(2,1)}) custom-call(s32[3]{0:T(128)S(1)} %pad_add_fusion.place_ref, bf16[160,128]{1,0:T(8,128)(2,1)S(1)} %shard_map.153.own_ref, bf16[160,128]{1,0:T(8,128)(2,1)S(1)} %collective-permute-done.3.other_ref, f32[320,128]{1,0:T(8,128)S(1)} %get-tuple-element.38.near_ref, ...), custom_call_target="tpu_custom_call" | custom-call | tf_op jit(solution)/shard_map/pallas_call | solution.py:34
  73.5 6.9 %all-to-all-start = ((bf16[32,32,128]{2,1,0:T(8,128)(2,1)}), bf16[32,32,128]{2,1,0:T(8,128)(2,1)S(1)}, u32[]{:S(2)}, u32[]{:S(2)}) async-start(bf16[32,32,128]{2,1,0:T(8,128)(2,1)} %bitcast.17), calls=%async_computation | async-start | bytes 524288 | tf_op jit(solution)/shard_map/all_to_all | solution.py:519
  80.5 3.6 %collective-permute-start.4 = (bf16[3840,128]{1,0:T(8,128)(2,1)}, bf16[3840,128]{1,0:T(8,128)(2,1)}, u32[]{:S(2)}, u32[]{:S(2)}) collective-permute-start(bf16[3840,128]{1,0:T(8,128)(2,1)} %get-tuple-element.57), channel_id=1, source_target_pairs={{0,8},{4,12},{8,0},{12,4},{1,9},{5,13},{9,1},{13,5},{2,10},{6,14},... | collective-permute-start | bytes 2949128 | tf_op jit(solution)/shard_map/ppermute | solution.py:512
  84.1 18.4 %all-to-all-done = bf16[32,32,128]{2,1,0:T(8,128)(2,1)S(1)} async-done(((bf16[32,32,128]{2,1,0:T(8,128)(2,1)}), bf16[32,32,128]{2,1,0:T(8,128)(2,1)S(1)}, u32[]{:S(2)}, u32[]{:S(2)}) %all-to-all-start) | async-done | bytes 262176 | tf_op jit(solution)/shard_map/all_to_all | solution.py:519
  102.8 13.7 %all_gather.19.g_ref = bf16[4,960,128]{2,1,0:T(8,128)(2,1)S(1)} all-gather(bf16[1,960,128]{2,1,0:T(8,128)(2,1)S(1)} %all_gather_reshape.3), channel_id=1, replica_groups=mesh['zh'=4,'zl'=4,'c'=2,'x'=4,'y'=4] {'y'}, dimensions={0}, use_global_device_ids=true | all-gather | bytes 1228800 | tf_op jit(solution)/shard_map/all_gather | solution.py:526
  116.5 2.5 %shard_map.158 = bf16[4,768,128]{2,1,0:T(8,128)(2,1)S(1)} custom-call(s32[1]{0:T(128)} %bitcast.4.ix_ref, bf16[4,960,128]{2,1,0:T(8,128)(2,1)S(1)} %all_gather.19.g_ref, bf16[3840,128]{1,0:T(8,128)(2,1)S(1)} %copy-done, bf16[3840,128]{1,0:T(8,128)(2,1)S(1)} %collective-permute-done.1.w1_ref, bf16[3840,128]{1,0:T(8,128)(2,1)} %collective-permute-done.4.w2_ref, ...), custom_call_target="tpu_custom_call" | custom-call | tf_op jit(solution)/shard_map/pallas_call | solution.py:410
  119.0 12.8 %all_to_all.25.p_ref = bf16[4,768,128]{2,1,0:T(8,128)(2,1)S(1)} all-to-all(bf16[4,768,128]{2,1,0:T(8,128)(2,1)S(1)} %shard_map.158), channel_id=1, replica_groups=mesh['zh'=4,'zl'=4,'c'=2,'x'=4,'y'=4] {'x'}, dimensions={0} | all-to-all | bytes 1572864 | tf_op jit(solution)/shard_map/all_to_all | solution.py:537
  131.8 0.1 shard_map.159
  131.9 8.6 %all_to_all.26.h_ref = bf16[4,384,128]{2,1,0:T(8,128)(2,1)S(1)} all-to-all(bf16[4,384,128]{2,1,0:T(8,128)(2,1)S(1)} %shard_map.159), channel_id=1, replica_groups=mesh['zh'=4,'zl'=4,'c'=2,'x'=4,'y'=4] {'x'}, dimensions={0} | all-to-all | bytes 786432 | tf_op jit(solution)/shard_map/all_to_all | solution.py:539
  140.6 1.8 shard_map.160
  142.3 11.8 %all_to_all.27 = bf16[4,960,128]{2,1,0:T(8,128)(2,1)S(1)} all-to-all(bf16[4,960,128]{2,1,0:T(8,128)(2,1)S(1)} %shard_map.160), channel_id=1, replica_groups=mesh['zh'=4,'zl'=4,'c'=2,'x'=4,'y'=4] {'y'}, dimensions={0} | all-to-all | bytes 1966080 | tf_op jit(solution)/shard_map/all_to_all | solution.py:548
  154.1 0.2 reduce_sum.12
  154.6 0.7 pad.4.clone
  155.4 10.6 %all-to-all-start.4 = ((bf16[32,32,128]{2,1,0:T(8,128)(2,1)}), bf16[32,32,128]{2,1,0:T(8,128)(2,1)S(1)}, u32[]{:S(2)}, u32[]{:S(2)}) async-start(bf16[32,32,128]{2,1,0:T(8,128)(2,1)} %pad.4.clone), calls=%async_computation.4 | async-start | bytes 524288 | tf_op jit(solution)/shard_map/all_to_all | solution.py:552
  166.0 0.6 shard_map.157
  166.6 21.4 %all-to-all-done.4 = bf16[32,32,128]{2,1,0:T(8,128)(2,1)S(1)} async-done(((bf16[32,32,128]{2,1,0:T(8,128)(2,1)}), bf16[32,32,128]{2,1,0:T(8,128)(2,1)S(1)}, u32[]{:S(2)}, u32[]{:S(2)}) %all-to-all-start.4) | async-done | bytes 262176 | tf_op jit(solution)/shard_map/all_to_all | solution.py:552
  188.0 1.4 shard_map.161
  (39 shorter events, 0.8 us)
Async XLA Ops:
  0.6 0.9 copy-start.1
  1.5 0.8 copy-start.3
  2.5 19.9 %copy-start.2 = (bf16[128,320]{0,1:T(8,128)(2,1)S(1)}, bf16[128,320]{0,1:T(8,128)(2,1)}, u32[]{:S(2)}) copy-start(bf16[128,320]{0,1:T(8,128)(2,1)} %param.14) | copy-start | bytes 245764
  2.5 19.9 %copy-start.4 = (bf16[128,256]{1,0:T(8,128)(2,1)S(1)}, bf16[128,256]{1,0:T(8,128)(2,1)}, u32[]{:S(2)}) copy-start(bf16[128,256]{1,0:T(8,128)(2,1)} %bc_ref.3) | copy-start | bytes 196612
  2.5 19.9 %copy-start.6 = (f32[4,320]{1,0:T(4,128)S(1)}, f32[4,320]{1,0:T(4,128)}, u32[]{:S(2)}) copy-start(f32[4,320]{1,0:T(4,128)} %cx_ref.1) | copy-start | bytes 15364
  2.5 19.9 %copy-start.7 = (f32[4,256]{1,0:T(4,128)S(1)}, f32[4,256]{1,0:T(4,128)}, u32[]{:S(2)}) copy-start(f32[4,256]{1,0:T(4,128)} %cbc_ref.1) | copy-start | bytes 12292
  2.5 19.9 %copy-start.8 = (f32[128,5]{0,1:T(8,128)S(1)}, f32[128,5]{0,1:T(8,128)}, u32[]{:S(2)}) copy-start(f32[128,5]{0,1:T(8,128)} %param.19) | copy-start | bytes 7684
  6.3 62.0 %copy-start.13 = (f32[320]{0:T(512)S(1)}, f32[320]{0:T(512)}, u32[]{:S(2)}) copy-start(f32[320]{0:T(512)} %param.21) | copy-start | bytes 3844
  6.3 62.0 %copy-start.10 = (s32[128,2]{0,1:T(2,128)S(1)}, s32[128,2]{0,1:T(2,128)}, u32[]{:S(2)}) copy-start(s32[128,2]{0,1:T(2,128)} %param.22) | copy-start | bytes 3076
  6.3 62.0 %copy-start.12 = (s32[32]{0:T(128)S(1)}, s32[32]{0:T(128)}, u32[]{:S(2)}) copy-start(s32[32]{0:T(128)} %param.24) | copy-start | bytes 388
  6.3 32.4 %collective-permute-start.1 = (bf16[3840,128]{1,0:T(8,128)(2,1)}, bf16[3840,128]{1,0:T(8,128)(2,1)S(1)}, u32[]{:S(2)}, u32[]{:S(2)}) collective-permute-start(bf16[3840,128]{1,0:T(8,128)(2,1)} %get-tuple-element.34), channel_id=1, source_target_pairs={{0,4},{4,8},{8,12},{12,0},{1,5},{5,9},{9,13},{13,1},{2,6},{6,10},{... | collective-permute-start | bytes 2949128 | tf_op jit(solution)/shard_map/ppermute | solution.py:451
  10.4 28.4 %collective-permute-start.2 = (bf16[3840,128]{1,0:T(8,128)(2,1)}, bf16[3840,128]{1,0:T(8,128)(2,1)S(1)}, u32[]{:S(2)}, u32[]{:S(2)}) collective-permute-start(bf16[3840,128]{1,0:T(8,128)(2,1)} %get-tuple-element.35), channel_id=1, source_target_pairs={{0,12},{4,0},{8,4},{12,8},{1,13},{5,1},{9,5},{13,9},{2,14},{6,2},{... | collective-permute-start | bytes 2949128 | tf_op jit(solution)/shard_map/ppermute | solution.py:451
  13.6 8.8 %collective-permute-start = (bf16[16,640]{1,0:T(8,128)(2,1)S(1)}, bf16[16,640]{1,0:T(8,128)(2,1)S(1)}, u32[]{:S(2)}, u32[]{:S(2)}) collective-permute-start(bf16[16,640]{1,0:T(8,128)(2,1)S(1)} %shard_map.149), channel_id=1, source_target_pairs={{0,16},{16,32},{32,48},{48,64},{64,80},{80,96},{96,112},{112,128},... | collective-permute-start | bytes 61448 | tf_op jit(solution)/shard_map/ppermute | solution.py:448
  23.4 46.1 %copy-start.5 = (bf16[128,320]{0,1:T(8,128)(2,1)S(1)}, bf16[128,320]{0,1:T(8,128)(2,1)}, u32[]{:S(2)}) copy-start(bf16[128,320]{0,1:T(8,128)(2,1)} %param.15) | copy-start | bytes 245764
  23.4 46.1 %copy-start.11 = (f32[5]{0:T(128)S(1)}, f32[5]{0:T(128)}, u32[]{:S(2)}) copy-start(f32[5]{0:T(128)} %skip_ref.1) | copy-start | bytes 64
  63.7 7.3 %collective-permute-start.3 = (bf16[160,128]{1,0:T(8,128)(2,1)S(1)}, bf16[160,128]{1,0:T(8,128)(2,1)S(1)}, u32[]{:S(2)}, u32[]{:S(2)}) collective-permute-start(bf16[160,128]{1,0:T(8,128)(2,1)S(1)} %shard_map.153.own_ref), channel_id=1, source_target_pairs={{0,16},{16,0},{1,17},{17,1},{2,18},{18,2},{3,19},{19,3},{4,20},{20... | collective-permute-start | bytes 122888 | tf_op jit(solution)/shard_map/ppermute | solution.py:493
  73.5 28.9 %all-to-all-start = ((bf16[32,32,128]{2,1,0:T(8,128)(2,1)}), bf16[32,32,128]{2,1,0:T(8,128)(2,1)S(1)}, u32[]{:S(2)}, u32[]{:S(2)}) async-start(bf16[32,32,128]{2,1,0:T(8,128)(2,1)} %bitcast.17), calls=%async_computation | async-start | bytes 524288 | tf_op jit(solution)/shard_map/all_to_all | solution.py:519
  80.5 36.0 %collective-permute-start.4 = (bf16[3840,128]{1,0:T(8,128)(2,1)}, bf16[3840,128]{1,0:T(8,128)(2,1)}, u32[]{:S(2)}, u32[]{:S(2)}) collective-permute-start(bf16[3840,128]{1,0:T(8,128)(2,1)} %get-tuple-element.57), channel_id=1, source_target_pairs={{0,8},{4,12},{8,0},{12,4},{1,9},{5,13},{9,1},{13,5},{2,10},{6,14},... | collective-permute-start | bytes 2949128 | tf_op jit(solution)/shard_map/ppermute | solution.py:512
  102.6 13.9 %copy-start = (bf16[3840,128]{1,0:T(8,128)(2,1)S(1)}, bf16[3840,128]{1,0:T(8,128)(2,1)}, u32[]{:S(2)}) copy-start(bf16[3840,128]{1,0:T(8,128)(2,1)} %get-tuple-element.55.w0_ref) | copy-start | bytes 2949124
  154.4 33.6 %copy-start.9 = (f32[128,2]{0,1:T(2,128)S(1)}, f32[128,2]{0,1:T(2,128)}, u32[]{:S(2)}) copy-start(f32[128,2]{0,1:T(2,128)} %param.23) | copy-start | bytes 3076
  155.4 32.6 %all-to-all-start.4 = ((bf16[32,32,128]{2,1,0:T(8,128)(2,1)}), bf16[32,32,128]{2,1,0:T(8,128)(2,1)S(1)}, u32[]{:S(2)}, u32[]{:S(2)}) async-start(bf16[32,32,128]{2,1,0:T(8,128)(2,1)} %pad.4.clone), calls=%async_computation.4 | async-start | bytes 524288 | tf_op jit(solution)/shard_map/all_to_all | solution.py:552
